TPU v7x, 256 devices: a whole 4x4x8 slice. The times are simulated.
256 devices in a mesh: replica: 8 (over y, x_hi), fsdp: 32 (over x_lo, z, core).
Axes of the slice: x: 4 (x_hi: 2, x_lo: 2; x = x_hi * 2 + x_lo), y: 4, z: 8, core: 2. Of those that a mesh axis runs over, the one named last changes fastest.
Arguments:
- hidden: bfloat16 [8, 16384, 4096], P('replica', 'fsdp'), may hold values from -6 to 6
- kv_weight: bfloat16 [8, 4096, 1024], P('replica', 'fsdp'), may hold values from -0.09375 to 0.09375
- kv_cotangent: bfloat16 [8, 16384, 1024], P('replica', 'fsdp'), may hold values from -6 to 6
- outer_global: float32 [4096, 512], P('fsdp'), may hold values from -6 to 6
- outer_local: float32 [8, 4096, 512], P('replica', 'fsdp'), may hold values from -6 to 6
- outer_momentum: float32 [4096, 512], P('fsdp'), may hold values from -6 to 6
Outputs:
- kv_out: bfloat16 [8, 16384, 1024], P('replica', 'fsdp')
- grad_hidden: bfloat16 [8, 16384, 4096], P('replica', 'fsdp')
- grad_weight: float32 [8, 4096, 1024], P('replica', 'fsdp')
- new_global: float32 [4096, 512], P('fsdp')
- new_momentum: float32 [4096, 512], P('fsdp')
All inputs are finite; a program needn't handle non-finite values.
Results may differ from a plain program's by a relative error of at most 0.001.
Values may be sent and summed in bfloat16 or wider, within the bound.
No kernel may reach another device: no remote copies, remote signals or barrier semaphores. Data moves between devices by JAX's collectives and lax.ppermute only.
A program may use at most 128 MiB of HBM per device.

v0:
```python
import jax
import jax.numpy as jnp
from jax import lax
from jax.sharding import PartitionSpec as P


def outer_update(global_rows, momentum_rows, outer_grad):
    new_momentum = 0.9 * momentum_rows + outer_grad
    new_global = global_rows - 0.7 * (outer_grad + 0.9 * new_momentum)
    return (new_global, new_momentum)


def local(hidden, kv_weight, kv_cotangent, outer_global, outer_local, outer_momentum):
    rows = hidden[0]
    cotan = kv_cotangent[0]
    shard = kv_weight[0]
    fsdp_count = lax.axis_size("fsdp")
    scale = (rows.shape[0] * fsdp_count) ** (-0.5)
    full_weight = lax.all_gather(shard, "fsdp", axis=0, tiled=True)
    keys = jnp.dot(rows, full_weight, preferred_element_type=jnp.float32)
    back = lax.dot_general(
        cotan, full_weight, (((1,), (1,)), ((), ())), preferred_element_type=jnp.float32
    )
    grads = lax.psum_scatter(
        lax.dot_general(rows, cotan, (((0,), (0,)), ((), ())), preferred_element_type=jnp.float32)
        * scale,
        "fsdp",
        scatter_dimension=0,
        tiled=True,
    )
    replica_count = lax.axis_size("replica")
    delta = outer_global - outer_local[0]
    total = lax.psum(delta, "replica")
    new_global, new_momentum = outer_update(outer_global, outer_momentum, total / replica_count)
    return (
        keys.astype(jnp.bfloat16)[None],
        back.astype(jnp.bfloat16)[None],
        grads[None],
        new_global,
        new_momentum,
    )


def solution(mesh):
    return jax.shard_map(
        local,
        mesh=mesh,
        in_specs=(
            P("replica", "fsdp", None),
            P("replica", "fsdp", None),
            P("replica", "fsdp", None),
            P("fsdp", None),
            P("replica", "fsdp", None),
            P("fsdp", None),
        ),
        out_specs=(
            P("replica", "fsdp", None),
            P("replica", "fsdp", None),
            P("replica", "fsdp", None),
            P("fsdp", None),
            P("fsdp", None),
        ),
        check_vma=False,
    )
```

profile of v0, /device:TPU:1, one launch (start us, length us, event | category | flops | bytes accessed | tf_op | source)
XLA Modules:
  0.0 239.9 jit_solution(2676486126178067005)
XLA Ops:
  8.0 0.0 copy-start
  8.0 0.0 all-reduce.2.cloned.1.call-start
  8.1 1.8 bitcast_subtract_fusion
  9.9 0.0 all-reduce.2.cloned.1.call-update
  9.9 0.0 all-gather.3.cloned.1.call-start
  10.0 0.5 all-gather.3.cloned.1.call-update
  10.5 0.0 reduce-scatter.2.cloned.1.call-start
  10.6 0.0 copy-done
  10.6 10.4 %broadcast_multiply_fusion = f32[4096,1024]{1,0:T(8,128)} fusion(bf16[1,512,4096]{2,1,0:T(8,128)(2,1)} %param.6, bf16[1,512,1024]{2,1,0:T(8,128)(2,1)S(1)} %copy-done), kind=kOutput, calls=%fused_computation.4 | convolution fusion | flops 4299161600 | bytes 22020096 | tf_op jit(solution)/shard_map/dot_general | solution.py:25
  20.9 0.0 copy-start.1
  20.9 0.0 copy-start.2
  20.9 0.0 reduce-scatter.2.cloned.1.call-update
  21.0 81.2 %all-reduce.2.cloned.1.call-done = f32[128,512]{1,0:T(8,128)} async-done(((f32[128,512]{1,0:T(8,128)}), f32[128,512]{1,0:T(8,128)}) %all-reduce.2.cloned.1.call-update) | async-done | bytes 262160 | tf_op jit(solution)/shard_map/psum | solution.py:33
  102.2 0.0 copy-done.1
  102.2 0.0 copy-done.2
  102.2 1.8 multiply_subtract_fusion
  104.0 0.0 all-gather.3.cloned.1.call-done
  104.0 0.0 copy-start.3
  104.0 0.0 copy-start.4
  104.0 9.6 %fusion.7 = bf16[1,512,4096]{2,1,0:T(8,128)(2,1)} fusion(bf16[1,4096,1024]{2,1,0:T(8,128)(2,1)} %all-gather.3.cloned.1.call-done, bf16[1,512,1024]{2,1,0:T(8,128)(2,1)S(1)} %copy-done), kind=kOutput, calls=%fused_computation.6 | convolution fusion | flops 4297064448 | bytes 13631488 | tf_op jit(solution)/shard_map/dot_general | solution.py:21
  113.6 0.0 copy-done.3
  113.6 0.0 copy-done.4
  113.6 5.5 %fusion.17 = bf16[1,512,1024]{2,1,0:T(8,128)(2,1)} fusion(bf16[1,4096,1024]{2,1,0:T(8,128)(2,1)S(1)} %copy-done.3, bf16[1,512,4096]{2,1,0:T(8,128)(2,1)S(1)} %copy-done.4), kind=kOutput, calls=%fused_computation.10 | convolution fusion | flops 4295491584 | bytes 13631488 | tf_op jit(solution)/shard_map/dot_general | solution.py:20
  119.1 113.3 %reduce-scatter.2.cloned.1.call-done = f32[128,1024]{1,0:T(8,128)} async-done(((f32[4096,1024]{1,0:T(8,128)}), f32[128,1024]{1,0:T(8,128)}) %reduce-scatter.2.cloned.1.call-update) | async-done | bytes 524304 | tf_op jit(solution)/shard_map/reduce_scatter | solution.py:24
Async XLA Ops:
  8.0 2.6 %copy-start = (bf16[1,512,1024]{2,1,0:T(8,128)(2,1)S(1)}, bf16[1,512,1024]{2,1,0:T(8,128)(2,1)}, u32[]{:S(2)}) copy-start(bf16[1,512,1024]{2,1,0:T(8,128)(2,1)} %param.8) | copy-start | bytes 3145732
  8.0 94.1 %all-reduce.2.cloned.1.call-start = ((), (), s32[]{:S(2)}) async-start(), calls=%async_computation.2 | async-start | bytes 524288 | tf_op jit(solution)/shard_map/psum | solution.py:33
  9.9 94.1 %all-gather.3.cloned.1.call-start = ((), (), s32[]{:S(2)}) async-start(), calls=%async_computation.3 | async-start | bytes 8650752 | tf_op jit(solution)/shard_map/all_gather | solution.py:19
  10.5 221.9 %reduce-scatter.2.cloned.1.call-start = ((), (), s32[]{:S(2)}) async-start(), calls=%async_computation.1 | async-start | bytes 17301504 | tf_op jit(solution)/shard_map/reduce_scatter | solution.py:24
  20.9 81.2 %copy-start.1 = (f32[128,512]{1,0:T(8,128)S(1)}, f32[128,512]{1,0:T(8,128)}, u32[]{:S(2)}) copy-start(f32[128,512]{1,0:T(8,128)} %param.9) | copy-start | bytes 786436
  20.9 81.2 %copy-start.2 = (f32[128,512]{1,0:T(8,128)S(1)}, f32[128,512]{1,0:T(8,128)}, u32[]{:S(2)}) copy-start(f32[128,512]{1,0:T(8,128)} %param.11) | copy-start | bytes 786436
  104.0 9.6 %copy-start.3 = (bf16[1,4096,1024]{2,1,0:T(8,128)(2,1)S(1)}, bf16[1,4096,1024]{2,1,0:T(8,128)(2,1)}, u32[]{:S(2)}) copy-start(bf16[1,4096,1024]{2,1,0:T(8,128)(2,1)} %all-gather.3.cloned.1.call-done) | copy-start | bytes 25165828
  104.0 9.6 %copy-start.4 = (bf16[1,512,4096]{2,1,0:T(8,128)(2,1)S(1)}, bf16[1,512,4096]{2,1,0:T(8,128)(2,1)}, u32[]{:S(2)}) copy-start(bf16[1,512,4096]{2,1,0:T(8,128)(2,1)} %param.6) | copy-start | bytes 12582916
Sparse Core Ops, SparseCore 0:
  12.0 90.0 all-reduce.1
Sparse Core Ops, SparseCore 1:
  12.3 77.2 all-gather.2
  92.5 139.9 reduce-scatter.1
where the time goes:
time: 243 us; the launch traced here: 240 us
  waiting for transfers between devices  195 us (80%)
  matrix products  25.5 us (10%)
  between operations  15.5 us (6%)
  other arithmetic  3.67 us (2%)
    reduce_scatter x1, waiting for transfers between devices, local(): lax.psum_scatter(lax.dot_general(rows, cotan, (((0,), (0,)), ((), ())), p...  113 us
    psum x1, waiting for transfers between devices, local(): total = lax.psum(delta, 'replica')  81.2 us
    dot_general x1, matrix products, local(): lax.dot_general(rows, cotan, (((0,), (0,)), ((), ())), preferred_element_...  10.4 us
    dot_general x1, matrix products, local(): lax.dot_general(cotan, full_weight, (((1,), (1,)), ((), ())), preferred_e...  9.62 us
    dot_general x1, matrix products, local(): keys = jnp.dot(rows, full_weight, preferred_element_type=jnp.float32)  5.5 us
  transfers between devices with their start and end apart: 3, of which 2 were waited for; matrix products, arithmetic and copies ran while one was open for 11% of the time, Pallas kernels for 0%

commit v1 on v0

v1 whole, which is shorter than its diff:
```python
import functools

import jax
import jax.numpy as jnp
from jax import lax
from jax.experimental import pallas as pl
from jax.experimental.pallas import tpu as pltpu
from jax.sharding import PartitionSpec as P

BF16, F16, F32 = jnp.bfloat16, jnp.float16, jnp.float32
ZS, CORES, XS = 8, 2, 2
UP = 8.0
ORDER = (4, -3, 0, 3, -2, 2, -1, 1)


def fsdp_perm(fn):
    pairs = []
    for x in range(XS):
        for z in range(ZS):
            for c in range(CORES):
                nx, nz, nc = fn(x, z, c)
                pairs.append((x * 16 + z * 2 + c, nx * 16 + (nz % ZS) * 2 + nc))
    return pairs


Z_UP = fsdp_perm(lambda x, z, c: (x, z + 1 - 2 * c, c))
Z_DOWN = fsdp_perm(lambda x, z, c: (x, z - 1 + 2 * c, c))
X_SWAP = fsdp_perm(lambda x, z, c: (1 - x, z, c))
CORE_SWAP = fsdp_perm(lambda x, z, c: (x, z, 1 - c))


class Order:
    def __init__(self, place):
        self.place = place

    def wait(self, *values):
        *values, self.place = lax.optimization_barrier((*values, self.place))
        return values

    def gate(self, value):
        return lax.optimization_barrier((value, self.place))[0]


def block_at(place, dx, dz, dc):
    core = (place[2] + dc) % CORES
    return ((place[0] + dx) % XS) * 16 + ((place[1] + (1 - 2 * core) * dz + ZS) % ZS) * 2 + core


def columns(tokens, spot):
    return pl.BlockSpec(
        (tokens, 128), lambda i, place: (0, block_at(place, *spot)), pipeline_mode=pl.Buffered(1)
    )


def packed(tokens, k):
    return pl.BlockSpec((tokens, 128), lambda i, place: (0, k), pipeline_mode=pl.Buffered(1))


def whole(shape):
    return pl.BlockSpec(shape, lambda i, place: (0, 0), pipeline_mode=pl.Buffered(1))


def params(mib):
    return pltpu.CompilerParams(vmem_limit_bytes=mib << 20)


COST = pl.CostEstimate(flops=1 << 20, bytes_accessed=1 << 16, transcendentals=0)


def pack_kernel(place, *refs):
    count = len(ORDER)
    for half, out in enumerate(refs[2 * count :]):
        for k in range(count):
            out[:, k * 128 : (k + 1) * 128] = refs[half * count + k][...]


def pack(hidden, place):
    tokens = hidden.shape[0]
    count = len(ORDER)
    spots = [(dx, dz, 0) for dx in (0, 1) for dz in ORDER]
    shape = (tokens, count * 128)
    return pl.pallas_call(
        pack_kernel,
        out_shape=[jax.ShapeDtypeStruct(shape, hidden.dtype)] * 2,
        grid_spec=pltpu.PrefetchScalarGridSpec(
            num_scalar_prefetch=1,
            grid=(1,),
            in_specs=[columns(tokens, s) for s in spots],
            out_specs=[whole(shape)] * 2,
        ),
        compiler_params=params(8),
        cost_estimate=COST,
        name="pack",
    )(place, *([hidden] * len(spots)))


def grad_kernel(sizes, scale, place, *refs):
    count = len(ORDER)
    own = refs[0][...]
    other = jnp.concatenate([r[...] for r in refs[1 : count + 1]], axis=1)
    own_cot, other_cot = refs[count + 1 : count + 3]
    outs = refs[count + 3 :]
    dims = (((0,), (0,)), ((), ()))
    width = own_cot.shape[1]
    step = 512
    for n in range(0, width, step):
        cols = slice(n, n + step)
        total = lax.dot_general(own, own_cot[:, cols], dims, preferred_element_type=F32)
        total += lax.dot_general(other, other_cot[:, cols], dims, preferred_element_type=F32)
        total = total * scale
        at = 0
        for out, size in zip(outs, sizes):
            out[:, cols] = total[at : at + size].astype(out.dtype)
            at += size


def grad(place, dx, hidden, cot, sizes, scale):
    tokens, width = cot[0].shape
    count = len(ORDER)
    spots = [(dx, dz, 0) for dz in ORDER]
    return pl.pallas_call(
        functools.partial(grad_kernel, sizes, scale),
        out_shape=[jax.ShapeDtypeStruct((s, width), F32) for s in sizes],
        grid_spec=pltpu.PrefetchScalarGridSpec(
            num_scalar_prefetch=1,
            grid=(1,),
            in_specs=[whole((tokens, count * 128))]
            + [columns(tokens, s) for s in spots]
            + [whole((tokens, width))] * 2,
            out_specs=[whole((s, width)) for s in sizes],
        ),
        compiler_params=params(24),
        cost_estimate=COST,
        name="grad",
    )(place, hidden[0][dx], *([hidden[1]] * count), *cot)


def use_kernel(spots, arrays, first, place, *refs):
    count = len(spots)
    rows = [jnp.concatenate([r[...] for r in refs[k * count : (k + 1) * count]], axis=1) for k in range(2)]
    refs = refs[2 * count :]
    weight = jnp.concatenate([r[...] for r in refs[:arrays]], axis=0)
    refs = refs[arrays:]
    cot, refs = refs[:2], refs[2:]
    if not first:
        acc, refs = refs[:2], refs[3:]
    out_keys, out_back, out_other, block, sems = refs[:2], refs[2], refs[3], refs[4], refs[5]
    dims = (((1,), (1,)), ((), ()))
    block[...] = lax.dot_general(cot[0][...], weight, dims, preferred_element_type=F32).astype(BF16)
    copies = []
    for k, spot in enumerate(spots):
        at = pl.multiple_of(block_at(place, *spot) * 128, 128)
        copies.append(
            pltpu.make_async_copy(
                block.at[:, pl.ds(k * 128, 128)], out_back.at[:, pl.ds(at, 128)], sems.at[k]
            )
        )
        copies[-1].start()
    out_other[...] = lax.dot_general(cot[1][...], weight, dims, preferred_element_type=F32).astype(BF16)
    for k in range(2):
        keys = jnp.dot(rows[k], weight, preferred_element_type=F32)
        if not first:
            keys += acc[k][...]
        out_keys[k][...] = keys
    for copy in copies:
        copy.wait()


def use(place, hidden, cot, weights, spots, state, last=False):
    tokens, width = cot[0].shape
    count = len(spots)
    first = state is None
    flops = 8 * tokens * count * 128 * width
    cost = pl.CostEstimate(flops=flops, bytes_accessed=1 << 20, transcendentals=0)
    anywhere = pl.BlockSpec(memory_space=pl.ANY)
    in_specs = [packed(tokens, ORDER.index(s[1])) for s in spots] + [columns(tokens, s) for s in spots]
    in_specs += [whole(w.shape) for w in weights] + [whole((tokens, width))] * 2
    operands = [hidden[0][s[0]] for s in spots] + [hidden[1]] * count + list(weights) + list(cot)
    aliases = {}
    if not first:
        in_specs += [whole((tokens, width))] * 2 + [anywhere]
        operands += list(state)
        aliases = {len(operands): 2}
    return pl.pallas_call(
        functools.partial(use_kernel, spots, len(weights), first),
        out_shape=[
            jax.ShapeDtypeStruct((tokens, width), F32),
            jax.ShapeDtypeStruct((tokens, width), F32),
            jax.ShapeDtypeStruct(hidden[1].shape, BF16),
            jax.ShapeDtypeStruct((tokens, count * 128), BF16),
        ],
        grid_spec=pltpu.PrefetchScalarGridSpec(
            num_scalar_prefetch=1,
            grid=(1,),
            in_specs=in_specs,
            out_specs=[whole((tokens, width))] * 2 + [anywhere, whole((tokens, count * 128))],
            scratch_shapes=[
                pltpu.VMEM((tokens, count * 128), BF16),
                pltpu.SemaphoreType.DMA((count,)),
            ],
        ),
        input_output_aliases=aliases,
        compiler_params=params(40),
        cost_estimate=COST if last else cost,
        name="use",
    )(place, *operands)


def merge_kernel(groups, place, *refs):
    parts, out, sems = refs[: len(groups)], refs[len(groups) + 1], refs[len(groups) + 2]
    copies = []
    for part, spots in zip(parts, groups):
        for k, (dx, dz, _) in enumerate(spots):
            at = pl.multiple_of(block_at(place, dx, dz, 1) * 128, 128)
            copies.append(
                pltpu.make_async_copy(
                    part.at[:, pl.ds(k * 128, 128)], out.at[:, pl.ds(at, 128)], sems.at[len(copies)]
                )
            )
            copies[-1].start()
    for copy in copies:
        copy.wait()


def merge(place, parts, groups, back):
    anywhere = pl.BlockSpec(memory_space=pl.ANY)
    return pl.pallas_call(
        functools.partial(merge_kernel, groups),
        out_shape=jax.ShapeDtypeStruct(back.shape, back.dtype),
        grid_spec=pltpu.PrefetchScalarGridSpec(
            num_scalar_prefetch=1,
            grid=(1,),
            in_specs=[whole(p.shape) for p in parts] + [anywhere],
            out_specs=anywhere,
            scratch_shapes=[pltpu.SemaphoreType.DMA((sum(map(len, groups)),))],
        ),
        input_output_aliases={len(parts) + 1: 0},
        compiler_params=params(16),
        cost_estimate=COST,
        name="merge",
    )(place, *parts, back)


def outer_update(global_rows, momentum_rows, outer_grad):
    new_momentum = 0.9 * momentum_rows + outer_grad
    new_global = global_rows - 0.7 * (outer_grad + 0.9 * new_momentum)
    return (new_global, new_momentum)


def local(hidden, kv_weight, kv_cotangent, outer_global, outer_local, outer_momentum):
    rows = hidden[0]
    cot = kv_cotangent[0]
    shard = kv_weight[0]
    scale = (rows.shape[0] * lax.axis_size("fsdp")) ** (-0.5)
    me = lax.axis_index("fsdp")
    place = jnp.stack([me // 16, (me // 2) % ZS, me % 2]).astype(jnp.int32)
    step = Order(place)
    replica_count = lax.axis_size("replica")

    def send(value, pairs):
        return lax.ppermute(step.gate(value), "fsdp", pairs)

    def butterfly(value, bit):
        pairs = [(r, r ^ bit) for r in range(replica_count)]
        return lax.ppermute(step.gate(value), "replica", pairs)

    def both_ways(above, below):
        above, below = step.wait(above.astype(F16), below.astype(F16))
        return send(above, Z_UP), send(below, Z_DOWN)

    b0 = send(shard, X_SWAP)
    other = send(rows, CORE_SWAP), send(cot, CORE_SWAP)
    total = outer_global - outer_local[0]
    summed = butterfly(total, 2)
    own = pack(rows, step.place)
    b0, summed, *both = step.wait(b0, summed, *other, *own)
    total = total + summed
    hidden2, cot2 = (both[2:], both[0]), (cot, both[1])
    pair = jnp.concatenate([shard, b0], axis=0)
    up1, down1 = send(pair, Z_UP), send(pair, Z_DOWN)
    summed = butterfly(total, 4)

    sizes = (384, 256, 256, 128)
    far = grad(step.place, 1, hidden2, cot2, sizes, scale * UP)
    far = step.wait(*[f.astype(F16) for f in far])
    got_a, got_b = send(far[0], X_SWAP), send(far[1], X_SWAP)
    near = step.wait(*grad(step.place, 0, hidden2, cot2, sizes, scale * UP))

    up1, down1, summed = step.wait(up1, down1, summed)
    total = total + summed
    up2, down2 = send(up1, Z_UP), send(down1, Z_DOWN)
    spots = [(0, 0, 0), (1, 0, 0), (0, -1, 0), (1, -1, 0), (0, 1, 0), (1, 1, 0)]
    groups = [spots]
    *state, back1 = step.wait(*use(step.place, hidden2, cot2, [pair, up1, down1], spots, None))

    (got,) = step.wait(got_a)
    both = near[0] + got.astype(F32)
    above, below = send(both[:128].astype(F16), Z_UP), send(both[128:256].astype(F16), Z_DOWN)
    mine = both[256:]
    up2, down2 = step.wait(up2, down2)
    up3, down3 = send(up2, Z_UP), send(down2, Z_DOWN)

    above, below, got = step.wait(above, below, got_b)
    both = near[1] + got.astype(F32)
    above, below = both[:128] + above.astype(F32), both[128:] + below.astype(F32)
    above, below = send(above.astype(F16), Z_UP), send(below.astype(F16), Z_DOWN)
    got = send(far[2], X_SWAP)
    spots = [(0, -2, 0), (1, -2, 0), (0, 2, 0), (1, 2, 0)]
    groups.append(spots)
    *state, back2 = step.wait(*use(step.place, hidden2, cot2, [up2, down2], spots, state))

    up3, down3 = step.wait(up3, down3)
    up4, down4 = send(up3[:128], Z_UP), send(down3[128:], Z_DOWN)
    above, below, got = step.wait(above, below, got)
    both = near[2] + got.astype(F32)
    above, below = both[:128] + above.astype(F32), both[128:] + below.astype(F32)
    above, below = send(above.astype(F16), Z_UP), send(below.astype(F16), Z_DOWN)
    got = send(far[3], X_SWAP)
    spots = [(0, -3, 0), (1, -3, 0), (0, 3, 0), (1, 3, 0)]
    groups.append(spots)
    *state, back3 = step.wait(*use(step.place, hidden2, cot2, [up3, down3], spots, state, True))
    up4, down4 = step.wait(up4, down4)
    spots = [(0, 4, 0), (1, 4, 0)]
    groups.append(spots)
    keys, other_keys, back, back4 = step.wait(*use(step.place, hidden2, cot2, [up4, down4], spots, state, True))

    above, below, got = step.wait(above, below, got)
    both = near[3] + got.astype(F32)
    mine = mine + below.astype(F32)
    above = send((both + above.astype(F32)).astype(F16), Z_UP)
    summed = butterfly(total, 1)
    other_keys = send(other_keys, CORE_SWAP)
    back1 = send(jnp.concatenate([back1, back2], axis=1), CORE_SWAP)
    back3 = send(jnp.concatenate([back3, back4], axis=1), CORE_SWAP)
    other_keys, back1, back3 = step.wait(other_keys, back1, back3)
    back = merge(step.place, [back1, back3], [groups[0] + groups[1], groups[2] + groups[3]], back)
    keys = (keys + other_keys).astype(BF16)
    keys, back, summed = step.wait(keys, back, summed)
    new_global, new_momentum = outer_update(outer_global, outer_momentum, (total + summed) / replica_count)
    above, keys, back, new_global, new_momentum = step.wait(above, keys, back, new_global, new_momentum)
    grads = (mine + above.astype(F32)) * (1.0 / UP)
    return (keys[None], back[None], grads[None], new_global, new_momentum)


def solution(mesh):
    return jax.shard_map(
        local,
        mesh=mesh,
        in_specs=(
            P("replica", "fsdp", None),
            P("replica", "fsdp", None),
            P("replica", "fsdp", None),
            P("fsdp", None),
            P("replica", "fsdp", None),
            P("fsdp", None),
        ),
        out_specs=(
            P("replica", "fsdp", None),
            P("replica", "fsdp", None),
            P("replica", "fsdp", None),
            P("fsdp", None),
            P("fsdp", None),
        ),
        check_vma=False,
    )
```

time: 243 us -> 96.9 us (0.40); the launches traced: 240 us -> 96.7 us
  waiting for transfers between devices: 195 us -> 16.1 us
  starting transfers between devices: 0.12 us -> 43.9 us
  Pallas kernels: 0 us -> 27.4 us
  matrix products: 25.5 us -> 0 us
  between operations: 15.5 us -> 0.97 us
    reduce_scatter x1 -> x0, waiting for transfers between devices: 113 us -> none  [local(): lax.psum_scatter(lax.dot_general(rows, cotan, (((0,), (0,)), ((), ())), p...]
    psum x1 -> x0, waiting for transfers between devices: 81.2 us -> none  [local(): total = lax.psum(delta, 'replica')]
    ppermute x0 -> x28, starting transfers between devices: none -> 43.9 us  [the longest x25 37.7 us: send(): return lax.ppermute(step.gate(value), 'fsdp', pairs)]
    pallas_call x0 -> x8, Pallas kernels: none -> 27.4 us  [the longest x4 17.6 us: use(): pl.pallas_call(functools.partial(use_kernel, spots, len(weights), first),...]
    dot_general x3 -> x0, matrix products: 25.5 us -> none  [the longest x1 10.4 us: local(): lax.dot_general(rows, cotan, (((0,), (0,)), ((), ())), preferred_element_...]
    ppermute x0 -> x28, waiting for transfers between devices: none -> 16.1 us  [the longest x25 11 us: send(): return lax.ppermute(step.gate(value), 'fsdp', pairs)]
    sub x2 -> x1, other arithmetic: 3.67 us -> 1.06 us  [local(): total = outer_global - outer_local[0]]
  transfers between devices with their start and end apart: 3 -> 28, of which waited for: 2 -> 11; matrix products, arithmetic and copies ran while one was open for 11% -> 5% of each run, Pallas kernels for 0% -> 28%
where the time goes in v1:
time: 96.9 us; the launch traced here: 96.7 us
  starting transfers between devices  43.9 us (45%)
  Pallas kernels  27.4 us (28%)
  waiting for transfers between devices  16.1 us (17%)
  other arithmetic  6 us (6%)
  local copies, waits for them, and re-layouts  2.34 us (2%)
  between operations  0.97 us (1%)
    ppermute x25, starting transfers between devices, send(): return lax.ppermute(step.gate(value), 'fsdp', pairs)  37.7 us
    pallas_call x4, Pallas kernels, use(): pl.pallas_call(functools.partial(use_kernel, spots, len(weights), first),...  17.6 us
    ppermute x25, waiting for transfers between devices, send(): return lax.ppermute(step.gate(value), 'fsdp', pairs)  11 us
    ppermute x3, starting transfers between devices, butterfly(): return lax.ppermute(step.gate(value), 'replica', pairs)  6.17 us
    pallas_call x2, Pallas kernels, grad(): pl.pallas_call(functools.partial(grad_kernel, sizes, scale), out_shape=[j...  6.14 us
    ppermute x3, waiting for transfers between devices, butterfly(): return lax.ppermute(step.gate(value), 'replica', pairs)  5.08 us
    unnamed x12, local copies, waits for them, and re-layouts  2.21 us
    pallas_call x1, Pallas kernels, merge(): pl.pallas_call(functools.partial(merge_kernel, groups), out_shape=jax.Sha...  1.99 us
  transfers between devices with their start and end apart: 28, of which 11 were waited for; matrix products, arithmetic and copies ran while one was open for 5% of the time, Pallas kernels for 28%

profile of v1, /device:TPU:1, one launch (start us, length us, event | category | flops | bytes accessed | tf_op | source)
XLA Modules:
  0.0 96.7 jit_solution(16102427446088710884)
XLA Ops:
  0.7 3.3 %collective-permute-start.2 = (bf16[512,4096]{1,0:T(8,128)(2,1)}, bf16[512,4096]{1,0:T(8,128)(2,1)S(1)}, u32[]{:S(2)}, u32[]{:S(2)}) collective-permute-start(bf16[512,4096]{1,0:T(8,128)(2,1)} %bitcast.12), channel_id=1, source_target_pairs={{0,1},{1,0},{2,3},{3,2},{4,5},{5,4},{6,7},{7,6},{8,9},{9,8},{10,11... | collective-permute-start | bytes 12582920 | tf_op jit(solution)/shard_map/ppermute | solution.py:261
  4.1 1.1 %bitcast_subtract_fusion = f32[128,512]{1,0:T(8,128)S(1)} fusion(f32[128,512]{1,0:T(8,128)} %param.9, f32[1,128,512]{2,1,0:T(8,128)} %param.10), kind=kLoop, calls=%fused_computation.20 | loop fusion | flops 65536 | bytes 786432 | tf_op jit(solution)/shard_map/sub | solution.py:273
  5.3 0.8 collective-permute-start
  6.0 2.2 %copy-done.1 = bf16[1,512,4096]{2,1,0:T(8,128)(2,1)S(1)} copy-done((bf16[1,512,4096]{2,1,0:T(8,128)(2,1)S(1)}, bf16[1,512,4096]{2,1,0:T(8,128)(2,1)}, u32[]{:S(2)}) %copy-start.1) | copy-done | bytes 4194328
  8.2 1.6 %pack.1 = (bf16[512,1024]{1,0:T(8,128)(2,1)S(1)}, bf16[512,1024]{1,0:T(8,128)(2,1)S(1)}) custom-call(s32[3]{0:T(128)S(1)} %pad_add_fusion.place, bf16[512,4096]{1,0:T(8,128)(2,1)S(1)} %bitcast.13, bf16[512,4096]{1,0:T(8,128)(2,1)S(1)} %bitcast.14, bf16[512,4096]{1,0:T(8,128)(2,1)S(1)} %bitcast.15, bf16[512,4096]{1,0:T(8,128)(2,1)S(1)} %bitcast.16, ...), custom_call_target="tpu_custom_call" | custom-call | flops 1048576 | bytes 65536 | tf_op jit(solution)/shard_map/pack/pallas_call | solution.py:82
  9.9 2.9 %collective-permute-done.1 = f32[128,512]{1,0:T(8,128)S(1)} collective-permute-done((f32[128,512]{1,0:T(8,128)S(1)}, f32[128,512]{1,0:T(8,128)S(1)}, u32[]{:S(2)}, u32[]{:S(2)}) %collective-permute-start.1) | collective-permute-done | bytes 262176 | tf_op jit(solution)/shard_map/ppermute | solution.py:265
  12.7 0.3 collective-permute-done
  13.1 0.9 collective-permute-start.6
  14.0 4.0 %collective-permute-start.5 = (bf16[256,1024]{1,0:T(8,128)(2,1)S(1)}, bf16[256,1024]{1,0:T(8,128)(2,1)S(1)}, u32[]{:S(2)}, u32[]{:S(2)}) collective-permute-start(bf16[256,1024]{1,0:T(8,128)(2,1)S(1)} %pad_maximum_fusion.2.refs_12_), channel_id=1, source_target_pairs={{0,2},{1,15},{2,4},{3,1},{4,6},{5,3},{6,8},{7,5},{8,10},{9,7},{10,... | collective-permute-start | bytes 1572872 | tf_op jit(solution)/shard_map/ppermute | solution.py:261
  18.0 3.1 %grad.2 = (f32[384,1024]{1,0:T(8,128)S(1)}, f32[256,1024]{1,0:T(8,128)S(1)}, f32[256,1024]{1,0:T(8,128)S(1)}, f32[128,1024]{1,0:T(8,128)S(1)}) custom-call(s32[3]{0:T(128)S(1)} %pad_add_fusion.place, bf16[512,1024]{1,0:T(8,128)(2,1)S(1)} %get-tuple-element.141.refs_0_.refs_1_.refs_3_.refs_5_, ...), custom_call_target="tpu_custom_call" | custom-call | flops 1048576 | bytes 65536 | tf_op jit(solution)/shard_map/grad/pallas_call | solution.py:121
  21.4 1.3 %collective-permute-start.4 = (f16[384,1024]{1,0:T(8,128)(2,1)S(1)}, f16[384,1024]{1,0:T(8,128)(2,1)S(1)}, u32[]{:S(2)}, u32[]{:S(2)}) collective-permute-start(f16[384,1024]{1,0:T(8,128)(2,1)S(1)} %convert_element_type.65), channel_id=1, source_target_pairs={{0,16},{1,17},{2,18},{3,19},{4,20},{5,21},{6,22},{7,23},{8,24},{9,... | collective-permute-start | bytes 2359304 | tf_op jit(solution)/shard_map/ppermute | solution.py:261
  22.8 2.7 %collective-permute-start.7 = (f32[128,512]{1,0:T(8,128)S(1)}, f32[128,512]{1,0:T(8,128)S(1)}, u32[]{:S(2)}, u32[]{:S(2)}) collective-permute-start(f32[128,512]{1,0:T(8,128)S(1)} %add.62), channel_id=1, source_target_pairs={{0,128},{32,160},{64,192},{96,224},{128,0},{160,32},{192,64},{224,... | collective-permute-start | bytes 786440 | tf_op jit(solution)/shard_map/ppermute | solution.py:265
  25.5 0.3 collective-permute-start.10
  25.7 3.1 %grad.3 = (f32[384,1024]{1,0:T(8,128)S(1)}, f32[256,1024]{1,0:T(8,128)S(1)}, f32[256,1024]{1,0:T(8,128)S(1)}, f32[128,1024]{1,0:T(8,128)S(1)}) custom-call(s32[3]{0:T(128)S(1)} %pad_add_fusion.place, bf16[512,1024]{1,0:T(8,128)(2,1)S(1)} %get-tuple-element.149.refs_0_.refs_2_.refs_4_, ...), custom_call_target="tpu_custom_call" | custom-call | flops 1048576 | bytes 65536 | tf_op jit(solution)/shard_map/grad/pallas_call | solution.py:121
  28.8 1.3 %collective-permute-done.7 = f32[128,512]{1,0:T(8,128)S(1)} collective-permute-done((f32[128,512]{1,0:T(8,128)S(1)}, f32[128,512]{1,0:T(8,128)S(1)}, u32[]{:S(2)}, u32[]{:S(2)}) %collective-permute-start.7) | collective-permute-done | bytes 262176 | tf_op jit(solution)/shard_map/ppermute | solution.py:265
  30.1 2.7 %collective-permute-start.11 = (bf16[256,1024]{1,0:T(8,128)(2,1)S(1)}, bf16[256,1024]{1,0:T(8,128)(2,1)S(1)}, u32[]{:S(2)}, u32[]{:S(2)}) collective-permute-start(bf16[256,1024]{1,0:T(8,128)(2,1)S(1)} %collective-permute-done.5.refs_13_), channel_id=1, source_target_pairs={{0,2},{1,15},{2,4},{3,1},{4,6},{5,3},{6,8},{7,5},{8,10},{9,7},{10,... | collective-permute-start | bytes 1572872 | tf_op jit(solution)/shard_map/ppermute | solution.py:261
  32.8 5.4 %use.4 = (f32[512,1024]{1,0:T(8,128)S(1)}, f32[512,1024]{1,0:T(8,128)S(1)}, bf16[512,4096]{1,0:T(8,128)(2,1)}, bf16[512,768]{1,0:T(8,128)(2,1)S(1)}) custom-call(s32[3]{0:T(128)S(1)} %pad_add_fusion.place, bf16[512,1024]{1,0:T(8,128)(2,1)S(1)} %get-tuple-element.149.refs_0_.refs_2_.refs_4_, ...), custom_call_target="tpu_custom_call" | custom-call | flops 3221225472 | bytes 1048576 | tf_op jit(solution)/shard_map/use/pallas_call | solution.py:184
  38.2 0.5 collective-permute-done.4
  38.8 0.4 fusion.7
  39.3 1.5 %collective-permute-start.9 = (f16[128,1024]{1,0:T(8,128)(2,1)S(1)}, f16[128,1024]{1,0:T(8,128)(2,1)S(1)}, u32[]{:S(2)}, u32[]{:S(2)}) collective-permute-start(f16[128,1024]{1,0:T(8,128)(2,1)S(1)} %get-tuple-element.176), channel_id=1, source_target_pairs={{0,14},{1,3},{2,0},{3,5},{4,2},{5,7},{6,4},{7,9},{8,6},{9,11},{10,... | collective-permute-start | bytes 786440 | tf_op jit(solution)/shard_map/ppermute | solution.py:261
  40.8 0.3 collective-permute-done.11.refs_8_
  41.1 4.0 %collective-permute-start.17 = (bf16[256,1024]{1,0:T(8,128)(2,1)S(1)}, bf16[256,1024]{1,0:T(8,128)(2,1)S(1)}, u32[]{:S(2)}, u32[]{:S(2)}) collective-permute-start(bf16[256,1024]{1,0:T(8,128)(2,1)S(1)} %collective-permute-done.12.refs_9_), channel_id=1, source_target_pairs={{0,14},{1,3},{2,0},{3,5},{4,2},{5,7},{6,4},{7,9},{8,6},{9,11},{10,... | collective-permute-start | bytes 1572872 | tf_op jit(solution)/shard_map/ppermute | solution.py:261
  45.1 4.9 %collective-permute-done.10 = f16[256,1024]{1,0:T(8,128)(2,1)S(1)} collective-permute-done((f16[256,1024]{1,0:T(8,128)(2,1)S(1)}, f16[256,1024]{1,0:T(8,128)(2,1)S(1)}, u32[]{:S(2)}, u32[]{:S(2)}) %collective-permute-start.10) | collective-permute-done | bytes 524320 | tf_op jit(solution)/shard_map/ppermute | solution.py:261
  50.0 1.2 %collective-permute-start.15 = (f16[256,1024]{1,0:T(8,128)(2,1)S(1)}, f16[256,1024]{1,0:T(8,128)(2,1)S(1)}, u32[]{:S(2)}, u32[]{:S(2)}) collective-permute-start(f16[256,1024]{1,0:T(8,128)(2,1)S(1)} %convert_element_type.67), channel_id=1, source_target_pairs={{0,16},{1,17},{2,18},{3,19},{4,20},{5,21},{6,22},{7,23},{8,24},{9,... | collective-permute-start | bytes 1572872 | tf_op jit(solution)/shard_map/ppermute | solution.py:261
  51.2 0.2 convert_add_fusion.2
  51.7 1.5 %collective-permute-start.14 = (f16[128,1024]{1,0:T(8,128)(2,1)S(1)}, f16[128,1024]{1,0:T(8,128)(2,1)S(1)}, u32[]{:S(2)}, u32[]{:S(2)}) collective-permute-start(f16[128,1024]{1,0:T(8,128)(2,1)S(1)} %get-tuple-element.187), channel_id=1, source_target_pairs={{0,14},{1,3},{2,0},{3,5},{4,2},{5,7},{6,4},{7,9},{8,6},{9,11},{10,... | collective-permute-start | bytes 786440 | tf_op jit(solution)/shard_map/ppermute | solution.py:261
  53.1 4.4 %use.5 = (f32[512,1024]{1,0:T(8,128)S(1)}, f32[512,1024]{1,0:T(8,128)S(1)}, bf16[512,4096]{1,0:T(8,128)(2,1)}, bf16[512,512]{1,0:T(8,128)(2,1)S(1)}) custom-call(s32[3]{0:T(128)S(1)} %pad_add_fusion.place, bf16[512,1024]{1,0:T(8,128)(2,1)S(1)} %get-tuple-element.149.refs_0_.refs_2_.refs_4_, ...), custom_call_target="tpu_custom_call", output_to_operand_aliasing={{2}: (15, {})} | custom-call | flops 2147483648 | bytes 1048576 | tf_op jit(solution)/shard_map/use/pallas_call | solution.py:184
  57.6 0.4 collective-permute-done.17.refs_9_
  57.9 1.8 %collective-permute-done.16.refs_8_ = bf16[256,1024]{1,0:T(8,128)(2,1)S(1)} collective-permute-done((bf16[256,1024]{1,0:T(8,128)(2,1)S(1)}, bf16[256,1024]{1,0:T(8,128)(2,1)S(1)}, u32[]{:S(2)}, u32[]{:S(2)}) %collective-permute-start.16) | collective-permute-done | bytes 524320 | tf_op jit(solution)/shard_map/ppermute | solution.py:261
  59.8 1.4 %collective-permute-start.21 = (bf16[128,1024]{1,0:T(8,128)(2,1)S(1)}, bf16[128,1024]{1,0:T(8,128)(2,1)S(1)}, u32[]{:S(2)}, u32[]{:S(2)}) collective-permute-start(bf16[128,1024]{1,0:T(8,128)(2,1)S(1)} %slice.35), channel_id=1, source_target_pairs={{0,2},{1,15},{2,4},{3,1},{4,6},{5,3},{6,8},{7,5},{8,10},{9,7},{10,... | collective-permute-start | bytes 786440 | tf_op jit(solution)/shard_map/ppermute | solution.py:261
  61.1 2.2 %collective-permute-start.22 = (bf16[128,1024]{1,0:T(8,128)(2,1)S(1)}, bf16[128,1024]{1,0:T(8,128)(2,1)S(1)}, u32[]{:S(2)}, u32[]{:S(2)}) collective-permute-start(bf16[128,1024]{1,0:T(8,128)(2,1)S(1)} %slice.36), channel_id=1, source_target_pairs={{0,14},{1,3},{2,0},{3,5},{4,2},{5,7},{6,4},{7,9},{8,6},{9,11},{10,... | collective-permute-start | bytes 786440 | tf_op jit(solution)/shard_map/ppermute | solution.py:261
  63.3 2.1 %collective-permute-done.13 = f16[128,1024]{1,0:T(8,128)(2,1)S(1)} collective-permute-done((f16[128,1024]{1,0:T(8,128)(2,1)S(1)}, f16[128,1024]{1,0:T(8,128)(2,1)S(1)}, u32[]{:S(2)}, u32[]{:S(2)}) %collective-permute-start.13) | collective-permute-done | bytes 262176 | tf_op jit(solution)/shard_map/ppermute | solution.py:261
  65.3 0.2 convert_add_fusion.1
  65.7 0.9 collective-permute-start.20
  66.6 0.6 collective-permute-start.18
  67.2 2.4 %collective-permute-start.19 = (f16[128,1024]{1,0:T(8,128)(2,1)S(1)}, f16[128,1024]{1,0:T(8,128)(2,1)S(1)}, u32[]{:S(2)}, u32[]{:S(2)}) collective-permute-start(f16[128,1024]{1,0:T(8,128)(2,1)S(1)} %get-tuple-element.208), channel_id=1, source_target_pairs={{0,14},{1,3},{2,0},{3,5},{4,2},{5,7},{6,4},{7,9},{8,6},{9,11},{10,... | collective-permute-start | bytes 786440 | tf_op jit(solution)/shard_map/ppermute | solution.py:261
  69.6 4.4 %use.6 = (f32[512,1024]{1,0:T(8,128)S(1)}, f32[512,1024]{1,0:T(8,128)S(1)}, bf16[512,4096]{1,0:T(8,128)(2,1)}, bf16[512,512]{1,0:T(8,128)(2,1)S(1)}) custom-call(s32[3]{0:T(128)S(1)} %pad_add_fusion.place, bf16[512,1024]{1,0:T(8,128)(2,1)S(1)} %get-tuple-element.149.refs_0_.refs_2_.refs_4_, ...), custom_call_target="tpu_custom_call", output_to_operand_aliasing={{2}: (15, {})} | custom-call | flops 1048576 | bytes 65536 | tf_op jit(solution)/shard_map/use/pallas_call | solution.py:184
  74.0 3.3 %use.7 = (f32[512,1024]{1,0:T(8,128)S(1)}, f32[512,1024]{1,0:T(8,128)S(1)}, bf16[512,4096]{1,0:T(8,128)(2,1)}, bf16[512,256]{1,0:T(8,128)(2,1)S(1)}) custom-call(s32[3]{0:T(128)S(1)} %pad_add_fusion.place, bf16[512,1024]{1,0:T(8,128)(2,1)S(1)} %get-tuple-element.149.refs_0_.refs_2_.refs_4_, ...), custom_call_target="tpu_custom_call", output_to_operand_aliasing={{2}: (11, {})} | custom-call | flops 1048576 | bytes 65536 | tf_op jit(solution)/shard_map/use/pallas_call | solution.py:184
  77.4 6.4 %collective-permute-start.24 = (f32[512,1024]{1,0:T(8,128)S(1)}, f32[512,1024]{1,0:T(8,128)S(1)}, u32[]{:S(2)}, u32[]{:S(2)}) collective-permute-start(f32[512,1024]{1,0:T(8,128)S(1)} %get-tuple-element.240), channel_id=1, source_target_pairs={{0,1},{1,0},{2,3},{3,2},{4,5},{5,4},{6,7},{7,6},{8,9},{9,8},{10,11... | collective-permute-start | bytes 6291464 | tf_op jit(solution)/shard_map/ppermute | solution.py:261
  84.1 0.6 collective-permute-start.26
  84.8 3.4 %collective-permute-start.27 = (f32[128,512]{1,0:T(8,128)S(1)}, f32[128,512]{1,0:T(8,128)S(1)}, u32[]{:S(2)}, u32[]{:S(2)}) collective-permute-start(f32[128,512]{1,0:T(8,128)S(1)} %add.73), channel_id=1, source_target_pairs={{0,32},{32,0},{64,96},{96,64},{128,160},{160,128},{192,224},{224,1... | collective-permute-start | bytes 786440 | tf_op jit(solution)/shard_map/ppermute | solution.py:265
  88.2 1.7 %collective-permute-start.23 = (f16[128,1024]{1,0:T(8,128)(2,1)S(1)}, f16[128,1024]{1,0:T(8,128)(2,1)S(1)}, u32[]{:S(2)}, u32[]{:S(2)}) collective-permute-start(f16[128,1024]{1,0:T(8,128)(2,1)S(1)} %add_convert_fusion.1), channel_id=1, source_target_pairs={{0,2},{1,15},{2,4},{3,1},{4,6},{5,3},{6,8},{7,5},{8,10},{9,7},{10,... | collective-permute-start | bytes 786440 | tf_op jit(solution)/shard_map/ppermute | solution.py:261
  89.9 0.7 collective-permute-done.26.refs_1_
  90.6 2.0 %merge.1 = bf16[512,4096]{1,0:T(8,128)(2,1)} custom-call(s32[3]{0:T(128)S(1)} %pad_add_fusion.place, bf16[512,1280]{1,0:T(8,128)(2,1)S(1)} %collective-permute-done.25.refs_0_, bf16[512,768]{1,0:T(8,128)(2,1)S(1)} %collective-permute-done.26.refs_1_, bf16[512,4096]{1,0:T(8,128)(2,1)} %get-tuple-element.251.refs_2_), custom_call_target="tpu_custom_call", output_to_operand_aliasing={{}: (3, {})} | custom-call | flops 1048576 | bytes 65536 | tf_op jit(solution)/shard_map/merge/pallas_call | solution.py:227
  92.6 1.3 %add_convert_fusion = bf16[512,1024]{1,0:T(8,128)(2,1)} fusion(f32[512,1024]{1,0:T(8,128)S(1)} %get-tuple-element.238, f32[512,1024]{1,0:T(8,128)S(1)} %collective-permute-done.24), kind=kLoop, calls=%fused_computation | loop fusion | flops 1048576 | bytes 5242880 | tf_op jit(solution)/shard_map/convert_element_type | solution.py:337
  94.0 0.9 collective-permute-done.27
  94.9 0.9 multiply_add_fusion
  95.8 0.9 fusion.2
  (51 shorter events, 1.8 us)
Async XLA Ops:
  0.7 12.3 %collective-permute-start.2 = (bf16[512,4096]{1,0:T(8,128)(2,1)}, bf16[512,4096]{1,0:T(8,128)(2,1)S(1)}, u32[]{:S(2)}, u32[]{:S(2)}) collective-permute-start(bf16[512,4096]{1,0:T(8,128)(2,1)} %bitcast.12), channel_id=1, source_target_pairs={{0,1},{1,0},{2,3},{3,2},{4,5},{5,4},{6,7},{7,6},{8,9},{9,8},{10,11... | collective-permute-start | bytes 12582920 | tf_op jit(solution)/shard_map/ppermute | solution.py:261
  4.0 9.0 %collective-permute-start.3 = (bf16[512,1024]{1,0:T(8,128)(2,1)}, bf16[512,1024]{1,0:T(8,128)(2,1)S(1)}, u32[]{:S(2)}, u32[]{:S(2)}) collective-permute-start(bf16[512,1024]{1,0:T(8,128)(2,1)} %bitcast.29), channel_id=1, source_target_pairs={{0,1},{1,0},{2,3},{3,2},{4,5},{5,4},{6,7},{7,6},{8,9},{9,8},{10,11... | collective-permute-start | bytes 3145736 | tf_op jit(solution)/shard_map/ppermute | solution.py:261
  5.2 7.6 %collective-permute-start.1 = (f32[128,512]{1,0:T(8,128)S(1)}, f32[128,512]{1,0:T(8,128)S(1)}, u32[]{:S(2)}, u32[]{:S(2)}) collective-permute-start(f32[128,512]{1,0:T(8,128)S(1)} %bitcast_subtract_fusion), channel_id=1, source_target_pairs={{0,64},{32,96},{64,0},{96,32},{128,192},{160,224},{192,128},{224,1... | collective-permute-start | bytes 786440 | tf_op jit(solution)/shard_map/ppermute | solution.py:265
  5.3 7.8 %collective-permute-start = (bf16[128,1024]{1,0:T(8,128)(2,1)}, bf16[128,1024]{1,0:T(8,128)(2,1)S(1)}, u32[]{:S(2)}, u32[]{:S(2)}) collective-permute-start(bf16[128,1024]{1,0:T(8,128)(2,1)} %bitcast.38), channel_id=1, source_target_pairs={{0,16},{1,17},{2,18},{3,19},{4,20},{5,21},{6,22},{7,23},{8,24},{9,... | collective-permute-start | bytes 786440 | tf_op jit(solution)/shard_map/ppermute | solution.py:261
  6.0 2.2 %copy-start.1 = (bf16[1,512,4096]{2,1,0:T(8,128)(2,1)S(1)}, bf16[1,512,4096]{2,1,0:T(8,128)(2,1)}, u32[]{:S(2)}) copy-start(bf16[1,512,4096]{2,1,0:T(8,128)(2,1)} %param.6) | copy-start | bytes 12582916
  8.2 4.8 %copy-start.4 = (bf16[1,128,1024]{2,1,0:T(8,128)(2,1)S(1)}, bf16[1,128,1024]{2,1,0:T(8,128)(2,1)}, u32[]{:S(2)}) copy-start(bf16[1,128,1024]{2,1,0:T(8,128)(2,1)} %param.7) | copy-start | bytes 786436
  8.2 9.8 %copy-start.2 = (bf16[1,512,1024]{2,1,0:T(8,128)(2,1)S(1)}, bf16[1,512,1024]{2,1,0:T(8,128)(2,1)}, u32[]{:S(2)}) copy-start(bf16[1,512,1024]{2,1,0:T(8,128)(2,1)} %param.8) | copy-start | bytes 3145732
  13.1 12.6 %copy-start = (bf16[512,4096]{1,0:T(8,128)(2,1)}, bf16[512,4096]{1,0:T(8,128)(2,1)S(1)}, u32[]{:S(2)}) copy-start(bf16[512,4096]{1,0:T(8,128)(2,1)S(1)} %collective-permute-done.2.refs_1_.refs_2_.refs_3_.refs_4_.refs_5_.refs_6_.refs_7_.refs_8_.refs_9_.refs_10_.refs_11_) | copy-start | bytes 12582916
  13.1 17.0 %collective-permute-start.6 = (bf16[256,1024]{1,0:T(8,128)(2,1)S(1)}, bf16[256,1024]{1,0:T(8,128)(2,1)S(1)}, u32[]{:S(2)}, u32[]{:S(2)}) collective-permute-start(bf16[256,1024]{1,0:T(8,128)(2,1)S(1)} %pad_maximum_fusion.2.refs_12_), channel_id=1, source_target_pairs={{0,14},{1,3},{2,0},{3,5},{4,2},{5,7},{6,4},{7,9},{8,6},{9,11},{10,... | collective-permute-start | bytes 1572872 | tf_op jit(solution)/shard_map/ppermute | solution.py:261
  14.0 16.1 %collective-permute-start.5 = (bf16[256,1024]{1,0:T(8,128)(2,1)S(1)}, bf16[256,1024]{1,0:T(8,128)(2,1)S(1)}, u32[]{:S(2)}, u32[]{:S(2)}) collective-permute-start(bf16[256,1024]{1,0:T(8,128)(2,1)S(1)} %pad_maximum_fusion.2.refs_12_), channel_id=1, source_target_pairs={{0,2},{1,15},{2,4},{3,1},{4,6},{5,3},{6,8},{7,5},{8,10},{9,7},{10,... | collective-permute-start | bytes 1572872 | tf_op jit(solution)/shard_map/ppermute | solution.py:261
  21.4 17.4 %collective-permute-start.4 = (f16[384,1024]{1,0:T(8,128)(2,1)S(1)}, f16[384,1024]{1,0:T(8,128)(2,1)S(1)}, u32[]{:S(2)}, u32[]{:S(2)}) collective-permute-start(f16[384,1024]{1,0:T(8,128)(2,1)S(1)} %convert_element_type.65), channel_id=1, source_target_pairs={{0,16},{1,17},{2,18},{3,19},{4,20},{5,21},{6,22},{7,23},{8,24},{9,... | collective-permute-start | bytes 2359304 | tf_op jit(solution)/shard_map/ppermute | solution.py:261
  22.8 7.4 %collective-permute-start.7 = (f32[128,512]{1,0:T(8,128)S(1)}, f32[128,512]{1,0:T(8,128)S(1)}, u32[]{:S(2)}, u32[]{:S(2)}) collective-permute-start(f32[128,512]{1,0:T(8,128)S(1)} %add.62), channel_id=1, source_target_pairs={{0,128},{32,160},{64,192},{96,224},{128,0},{160,32},{192,64},{224,... | collective-permute-start | bytes 786440 | tf_op jit(solution)/shard_map/ppermute | solution.py:265
  25.5 24.6 %collective-permute-start.10 = (f16[256,1024]{1,0:T(8,128)(2,1)S(1)}, f16[256,1024]{1,0:T(8,128)(2,1)S(1)}, u32[]{:S(2)}, u32[]{:S(2)}) collective-permute-start(f16[256,1024]{1,0:T(8,128)(2,1)S(1)} %convert_element_type.66), channel_id=1, source_target_pairs={{0,16},{1,17},{2,18},{3,19},{4,20},{5,21},{6,22},{7,23},{8,24},{9,... | collective-permute-start | bytes 1572872 | tf_op jit(solution)/shard_map/ppermute | solution.py:261
  30.1 10.7 %collective-permute-start.12 = (bf16[256,1024]{1,0:T(8,128)(2,1)S(1)}, bf16[256,1024]{1,0:T(8,128)(2,1)S(1)}, u32[]{:S(2)}, u32[]{:S(2)}) collective-permute-start(bf16[256,1024]{1,0:T(8,128)(2,1)S(1)} %collective-permute-done.6.refs_14_), channel_id=1, source_target_pairs={{0,14},{1,3},{2,0},{3,5},{4,2},{5,7},{6,4},{7,9},{8,6},{9,11},{10,... | collective-permute-start | bytes 1572872 | tf_op jit(solution)/shard_map/ppermute | solution.py:261
  30.1 11.0 %collective-permute-start.11 = (bf16[256,1024]{1,0:T(8,128)(2,1)S(1)}, bf16[256,1024]{1,0:T(8,128)(2,1)S(1)}, u32[]{:S(2)}, u32[]{:S(2)}) collective-permute-start(bf16[256,1024]{1,0:T(8,128)(2,1)S(1)} %collective-permute-done.5.refs_13_), channel_id=1, source_target_pairs={{0,2},{1,15},{2,4},{3,1},{4,6},{5,3},{6,8},{7,5},{8,10},{9,7},{10,... | collective-permute-start | bytes 1572872 | tf_op jit(solution)/shard_map/ppermute | solution.py:261
  39.2 10.8 %collective-permute-start.8 = (f16[128,1024]{1,0:T(8,128)(2,1)S(1)}, f16[128,1024]{1,0:T(8,128)(2,1)S(1)}, u32[]{:S(2)}, u32[]{:S(2)}) collective-permute-start(f16[128,1024]{1,0:T(8,128)(2,1)S(1)} %get-tuple-element.175), channel_id=1, source_target_pairs={{0,2},{1,15},{2,4},{3,1},{4,6},{5,3},{6,8},{7,5},{8,10},{9,7},{10,... | collective-permute-start | bytes 786440 | tf_op jit(solution)/shard_map/ppermute | solution.py:261
  39.3 10.7 %collective-permute-start.9 = (f16[128,1024]{1,0:T(8,128)(2,1)S(1)}, f16[128,1024]{1,0:T(8,128)(2,1)S(1)}, u32[]{:S(2)}, u32[]{:S(2)}) collective-permute-start(f16[128,1024]{1,0:T(8,128)(2,1)S(1)} %get-tuple-element.176), channel_id=1, source_target_pairs={{0,14},{1,3},{2,0},{3,5},{4,2},{5,7},{6,4},{7,9},{8,6},{9,11},{10,... | collective-permute-start | bytes 786440 | tf_op jit(solution)/shard_map/ppermute | solution.py:261
  41.1 16.8 %collective-permute-start.17 = (bf16[256,1024]{1,0:T(8,128)(2,1)S(1)}, bf16[256,1024]{1,0:T(8,128)(2,1)S(1)}, u32[]{:S(2)}, u32[]{:S(2)}) collective-permute-start(bf16[256,1024]{1,0:T(8,128)(2,1)S(1)} %collective-permute-done.12.refs_9_), channel_id=1, source_target_pairs={{0,14},{1,3},{2,0},{3,5},{4,2},{5,7},{6,4},{7,9},{8,6},{9,11},{10,... | collective-permute-start | bytes 1572872 | tf_op jit(solution)/shard_map/ppermute | solution.py:261
  45.1 14.6 %collective-permute-start.16 = (bf16[256,1024]{1,0:T(8,128)(2,1)S(1)}, bf16[256,1024]{1,0:T(8,128)(2,1)S(1)}, u32[]{:S(2)}, u32[]{:S(2)}) collective-permute-start(bf16[256,1024]{1,0:T(8,128)(2,1)S(1)} %collective-permute-done.11.refs_8_), channel_id=1, source_target_pairs={{0,2},{1,15},{2,4},{3,1},{4,6},{5,3},{6,8},{7,5},{8,10},{9,7},{10,... | collective-permute-start | bytes 1572872 | tf_op jit(solution)/shard_map/ppermute | solution.py:261
  50.0 15.3 %collective-permute-start.15 = (f16[256,1024]{1,0:T(8,128)(2,1)S(1)}, f16[256,1024]{1,0:T(8,128)(2,1)S(1)}, u32[]{:S(2)}, u32[]{:S(2)}) collective-permute-start(f16[256,1024]{1,0:T(8,128)(2,1)S(1)} %convert_element_type.67), channel_id=1, source_target_pairs={{0,16},{1,17},{2,18},{3,19},{4,20},{5,21},{6,22},{7,23},{8,24},{9,... | collective-permute-start | bytes 1572872 | tf_op jit(solution)/shard_map/ppermute | solution.py:261
  51.6 13.7 %collective-permute-start.13 = (f16[128,1024]{1,0:T(8,128)(2,1)S(1)}, f16[128,1024]{1,0:T(8,128)(2,1)S(1)}, u32[]{:S(2)}, u32[]{:S(2)}) collective-permute-start(f16[128,1024]{1,0:T(8,128)(2,1)S(1)} %get-tuple-element.185), channel_id=1, source_target_pairs={{0,2},{1,15},{2,4},{3,1},{4,6},{5,3},{6,8},{7,5},{8,10},{9,7},{10,... | collective-permute-start | bytes 786440 | tf_op jit(solution)/shard_map/ppermute | solution.py:261
  51.7 13.6 %collective-permute-start.14 = (f16[128,1024]{1,0:T(8,128)(2,1)S(1)}, f16[128,1024]{1,0:T(8,128)(2,1)S(1)}, u32[]{:S(2)}, u32[]{:S(2)}) collective-permute-start(f16[128,1024]{1,0:T(8,128)(2,1)S(1)} %get-tuple-element.187), channel_id=1, source_target_pairs={{0,14},{1,3},{2,0},{3,5},{4,2},{5,7},{6,4},{7,9},{8,6},{9,11},{10,... | collective-permute-start | bytes 786440 | tf_op jit(solution)/shard_map/ppermute | solution.py:261
  59.8 14.3 %collective-permute-start.21 = (bf16[128,1024]{1,0:T(8,128)(2,1)S(1)}, bf16[128,1024]{1,0:T(8,128)(2,1)S(1)}, u32[]{:S(2)}, u32[]{:S(2)}) collective-permute-start(bf16[128,1024]{1,0:T(8,128)(2,1)S(1)} %slice.35), channel_id=1, source_target_pairs={{0,2},{1,15},{2,4},{3,1},{4,6},{5,3},{6,8},{7,5},{8,10},{9,7},{10,... | collective-permute-start | bytes 786440 | tf_op jit(solution)/shard_map/ppermute | solution.py:261
  61.1 12.9 %collective-permute-start.22 = (bf16[128,1024]{1,0:T(8,128)(2,1)S(1)}, bf16[128,1024]{1,0:T(8,128)(2,1)S(1)}, u32[]{:S(2)}, u32[]{:S(2)}) collective-permute-start(bf16[128,1024]{1,0:T(8,128)(2,1)S(1)} %slice.36), channel_id=1, source_target_pairs={{0,14},{1,3},{2,0},{3,5},{4,2},{5,7},{6,4},{7,9},{8,6},{9,11},{10,... | collective-permute-start | bytes 786440 | tf_op jit(solution)/shard_map/ppermute | solution.py:261
  65.7 11.7 %collective-permute-start.20 = (f16[128,1024]{1,0:T(8,128)(2,1)S(1)}, f16[128,1024]{1,0:T(8,128)(2,1)S(1)}, u32[]{:S(2)}, u32[]{:S(2)}) collective-permute-start(f16[128,1024]{1,0:T(8,128)(2,1)S(1)} %convert_element_type.68), channel_id=1, source_target_pairs={{0,16},{1,17},{2,18},{3,19},{4,20},{5,21},{6,22},{7,23},{8,24},{9,... | collective-permute-start | bytes 786440 | tf_op jit(solution)/shard_map/ppermute | solution.py:261
  66.6 10.8 %collective-permute-start.18 = (f16[128,1024]{1,0:T(8,128)(2,1)S(1)}, f16[128,1024]{1,0:T(8,128)(2,1)S(1)}, u32[]{:S(2)}, u32[]{:S(2)}) collective-permute-start(f16[128,1024]{1,0:T(8,128)(2,1)S(1)} %get-tuple-element.206), channel_id=1, source_target_pairs={{0,2},{1,15},{2,4},{3,1},{4,6},{5,3},{6,8},{7,5},{8,10},{9,7},{10,... | collective-permute-start | bytes 786440 | tf_op jit(solution)/shard_map/ppermute | solution.py:261
  67.2 10.2 %collective-permute-start.19 = (f16[128,1024]{1,0:T(8,128)(2,1)S(1)}, f16[128,1024]{1,0:T(8,128)(2,1)S(1)}, u32[]{:S(2)}, u32[]{:S(2)}) collective-permute-start(f16[128,1024]{1,0:T(8,128)(2,1)S(1)} %get-tuple-element.208), channel_id=1, source_target_pairs={{0,14},{1,3},{2,0},{3,5},{4,2},{5,7},{6,4},{7,9},{8,6},{9,11},{10,... | collective-permute-start | bytes 786440 | tf_op jit(solution)/shard_map/ppermute | solution.py:261
  77.4 13.2 %collective-permute-start.24 = (f32[512,1024]{1,0:T(8,128)S(1)}, f32[512,1024]{1,0:T(8,128)S(1)}, u32[]{:S(2)}, u32[]{:S(2)}) collective-permute-start(f32[512,1024]{1,0:T(8,128)S(1)} %get-tuple-element.240), channel_id=1, source_target_pairs={{0,1},{1,0},{2,3},{3,2},{4,5},{5,4},{6,7},{7,6},{8,9},{9,8},{10,11... | collective-permute-start | bytes 6291464 | tf_op jit(solution)/shard_map/ppermute | solution.py:261
  83.9 6.7 %collective-permute-start.25 = (bf16[512,1280]{1,0:T(8,128)(2,1)S(1)}, bf16[512,1280]{1,0:T(8,128)(2,1)S(1)}, u32[]{:S(2)}, u32[]{:S(2)}) collective-permute-start(bf16[512,1280]{1,0:T(8,128)(2,1)S(1)} %pad_maximum_fusion), channel_id=1, source_target_pairs={{0,1},{1,0},{2,3},{3,2},{4,5},{5,4},{6,7},{7,6},{8,9},{9,8},{10,11... | collective-permute-start | bytes 3932168 | tf_op jit(solution)/shard_map/ppermute | solution.py:261
  84.1 6.5 %collective-permute-start.26 = (bf16[512,768]{1,0:T(8,128)(2,1)S(1)}, bf16[512,768]{1,0:T(8,128)(2,1)S(1)}, u32[]{:S(2)}, u32[]{:S(2)}) collective-permute-start(bf16[512,768]{1,0:T(8,128)(2,1)S(1)} %pad_maximum_fusion.1), channel_id=1, source_target_pairs={{0,1},{1,0},{2,3},{3,2},{4,5},{5,4},{6,7},{7,6},{8,9},{9,8},{10,11... | collective-permute-start | bytes 2359304 | tf_op jit(solution)/shard_map/ppermute | solution.py:261
  84.8 10.0 %collective-permute-start.27 = (f32[128,512]{1,0:T(8,128)S(1)}, f32[128,512]{1,0:T(8,128)S(1)}, u32[]{:S(2)}, u32[]{:S(2)}) collective-permute-start(f32[128,512]{1,0:T(8,128)S(1)} %add.73), channel_id=1, source_target_pairs={{0,32},{32,0},{64,96},{96,64},{128,160},{160,128},{192,224},{224,1... | collective-permute-start | bytes 786440 | tf_op jit(solution)/shard_map/ppermute | solution.py:265
  88.2 7.6 %collective-permute-start.23 = (f16[128,1024]{1,0:T(8,128)(2,1)S(1)}, f16[128,1024]{1,0:T(8,128)(2,1)S(1)}, u32[]{:S(2)}, u32[]{:S(2)}) collective-permute-start(f16[128,1024]{1,0:T(8,128)(2,1)S(1)} %add_convert_fusion.1), channel_id=1, source_target_pairs={{0,2},{1,15},{2,4},{3,1},{4,6},{5,3},{6,8},{7,5},{8,10},{9,7},{10,... | collective-permute-start | bytes 786440 | tf_op jit(solution)/shard_map/ppermute | solution.py:261
  92.6 2.2 %copy-start.3 = (f32[128,512]{1,0:T(8,128)S(1)}, f32[128,512]{1,0:T(8,128)}, u32[]{:S(2)}) copy-start(f32[128,512]{1,0:T(8,128)} %param.9) | copy-start | bytes 786436
  92.6 2.2 %copy-start.5 = (f32[128,512]{1,0:T(8,128)S(1)}, f32[128,512]{1,0:T(8,128)}, u32[]{:S(2)}) copy-start(f32[128,512]{1,0:T(8,128)} %param.11) | copy-start | bytes 786436

commit v2 on v1

--- a/solution.py
+++ b/solution.py
@@ -207,7 +207,8 @@
 
 
 def merge_kernel(groups, place, *refs):
-    parts, out, sems = refs[: len(groups)], refs[len(groups) + 1], refs[len(groups) + 2]
+    parts, refs = refs[: len(groups)], refs[len(groups) :]
+    own, other, _, keys, out, sems = refs
     copies = []
     for part, spots in zip(parts, groups):
         for k, (dx, dz, _) in enumerate(spots):
@@ -218,27 +219,29 @@
                 )
             )
             copies[-1].start()
+    keys[...] = (own[...] + other[...]).astype(keys.dtype)
     for copy in copies:
         copy.wait()
 
 
-def merge(place, parts, groups, back):
+def merge(place, parts, groups, keys, back):
     anywhere = pl.BlockSpec(memory_space=pl.ANY)
+    shape = keys[0].shape
     return pl.pallas_call(
         functools.partial(merge_kernel, groups),
-        out_shape=jax.ShapeDtypeStruct(back.shape, back.dtype),
+        out_shape=[jax.ShapeDtypeStruct(shape, BF16), jax.ShapeDtypeStruct(back.shape, back.dtype)],
         grid_spec=pltpu.PrefetchScalarGridSpec(
             num_scalar_prefetch=1,
             grid=(1,),
-            in_specs=[whole(p.shape) for p in parts] + [anywhere],
-            out_specs=anywhere,
+            in_specs=[whole(p.shape) for p in parts] + [whole(shape)] * 2 + [anywhere],
+            out_specs=[whole(shape), anywhere],
             scratch_shapes=[pltpu.SemaphoreType.DMA((sum(map(len, groups)),))],
         ),
-        input_output_aliases={len(parts) + 1: 0},
-        compiler_params=params(16),
+        input_output_aliases={len(parts) + 3: 1},
+        compiler_params=params(24),
         cost_estimate=COST,
         name="merge",
-    )(place, *parts, back)
+    )(place, *parts, *keys, back)
 
 
 def outer_update(global_rows, momentum_rows, outer_grad):
@@ -293,29 +296,34 @@
     groups = [spots]
     *state, back1 = step.wait(*use(step.place, hidden2, cot2, [pair, up1, down1], spots, None))
 
-    (got,) = step.wait(got_a)
-    both = near[0] + got.astype(F32)
-    above, below = send(both[:128].astype(F16), Z_UP), send(both[128:256].astype(F16), Z_DOWN)
-    mine = both[256:]
+    def chip_sum(part, got, k):
+        rows = slice(k * 128, (k + 1) * 128)
+        return near[part][rows] + got[rows].astype(F32)
+
+    (got_a,) = step.wait(got_a)
+    above, below = chip_sum(0, got_a, 0), chip_sum(0, got_a, 1)
+    above, below = send(above.astype(F16), Z_UP), send(below.astype(F16), Z_DOWN)
     up2, down2 = step.wait(up2, down2)
     up3, down3 = send(up2, Z_UP), send(down2, Z_DOWN)
 
     above, below, got = step.wait(above, below, got_b)
-    both = near[1] + got.astype(F32)
-    above, below = both[:128] + above.astype(F32), both[128:] + below.astype(F32)
+    above = chip_sum(1, got, 0) + above.astype(F32)
+    below = chip_sum(1, got, 1) + below.astype(F32)
     above, below = send(above.astype(F16), Z_UP), send(below.astype(F16), Z_DOWN)
     got = send(far[2], X_SWAP)
     spots = [(0, -2, 0), (1, -2, 0), (0, 2, 0), (1, 2, 0)]
     groups.append(spots)
     *state, back2 = step.wait(*use(step.place, hidden2, cot2, [up2, down2], spots, state))
+    back1 = jnp.concatenate([back1, back2], axis=1)
+    (back1,) = step.wait(back1)
 
     up3, down3 = step.wait(up3, down3)
     up4, down4 = send(up3[:128], Z_UP), send(down3[128:], Z_DOWN)
     above, below, got = step.wait(above, below, got)
-    both = near[2] + got.astype(F32)
-    above, below = both[:128] + above.astype(F32), both[128:] + below.astype(F32)
-    above, below = send(above.astype(F16), Z_UP), send(below.astype(F16), Z_DOWN)
+    above = send((chip_sum(2, got, 0) + above.astype(F32)).astype(F16), Z_UP)
+    below = (chip_sum(2, got, 1) + below.astype(F32)).astype(F16)
     got = send(far[3], X_SWAP)
+    summed = butterfly(total, 1)
     spots = [(0, -3, 0), (1, -3, 0), (0, 3, 0), (1, 3, 0)]
     groups.append(spots)
     *state, back3 = step.wait(*use(step.place, hidden2, cot2, [up3, down3], spots, state, True))
@@ -324,21 +332,20 @@
     groups.append(spots)
     keys, other_keys, back, back4 = step.wait(*use(step.place, hidden2, cot2, [up4, down4], spots, state, True))
 
-    above, below, got = step.wait(above, below, got)
-    both = near[3] + got.astype(F32)
-    mine = mine + below.astype(F32)
-    above = send((both + above.astype(F32)).astype(F16), Z_UP)
-    summed = butterfly(total, 1)
-    other_keys = send(other_keys, CORE_SWAP)
-    back1 = send(jnp.concatenate([back1, back2], axis=1), CORE_SWAP)
+    above, got, summed = step.wait(above, got, summed)
+    above = (chip_sum(3, got, 0) + above.astype(F32)).astype(F16)
+    above, below = send(above, Z_UP), send(below, Z_DOWN)
+    other_keys, back1 = send(other_keys, CORE_SWAP), send(back1, CORE_SWAP)
     back3 = send(jnp.concatenate([back3, back4], axis=1), CORE_SWAP)
-    other_keys, back1, back3 = step.wait(other_keys, back1, back3)
-    back = merge(step.place, [back1, back3], [groups[0] + groups[1], groups[2] + groups[3]], back)
-    keys = (keys + other_keys).astype(BF16)
-    keys, back, summed = step.wait(keys, back, summed)
     new_global, new_momentum = outer_update(outer_global, outer_momentum, (total + summed) / replica_count)
-    above, keys, back, new_global, new_momentum = step.wait(above, keys, back, new_global, new_momentum)
-    grads = (mine + above.astype(F32)) * (1.0 / UP)
+    other_keys, back1, back3, new_global, new_momentum = step.wait(
+        other_keys, back1, back3, new_global, new_momentum
+    )
+    groups = [groups[0] + groups[1], groups[2] + groups[3]]
+    keys, back = merge(step.place, [back1, back3], groups, (keys, other_keys), back)
+    above, below, keys, back = step.wait(above, below, keys, back)
+    mine = near[0][256:] + got_a[256:].astype(F32)
+    grads = (mine + above.astype(F32) + below.astype(F32)) * (1.0 / UP)
     return (keys[None], back[None], grads[None], new_global, new_momentum)
 
 

time: 96.9 us -> 94.7 us (0.977)
  other arithmetic: 6 us -> 4.44 us
  waiting for transfers between devices: 16.1 us -> 15.1 us
    convert_element_type x2, other arithmetic: 1.45 us -> 0.4 us  [the longest x1 0.27 us: local(): below = (chip_sum(2, got, 1) + below.astype(F32)).astype(F16)]
  transfers between devices with their start and end apart: 28 -> 28, of which waited for: 11 -> 10; matrix products, arithmetic and copies ran while one was open for 5% -> 4% of each run, Pallas kernels for 28% -> 30%
where the time goes in v2:
time: 94.7 us; the launch traced here: 94.3 us
  starting transfers between devices  43.2 us (46%)
  Pallas kernels  28.3 us (30%)
  waiting for transfers between devices  15.1 us (16%)
  other arithmetic  4.44 us (5%)
  local copies, waits for them, and re-layouts  2.25 us (2%)
  between operations  0.97 us (1%)
    ppermute x25, starting transfers between devices, send(): return lax.ppermute(step.gate(value), 'fsdp', pairs)  37.6 us
    pallas_call x4, Pallas kernels, use(): pl.pallas_call(functools.partial(use_kernel, spots, len(weights), first),...  17.6 us
    ppermute x25, waiting for transfers between devices, send(): return lax.ppermute(step.gate(value), 'fsdp', pairs)  10.9 us
    pallas_call x2, Pallas kernels, grad(): pl.pallas_call(functools.partial(grad_kernel, sizes, scale), out_shape=[j...  6.13 us
    ppermute x3, starting transfers between devices, butterfly(): return lax.ppermute(step.gate(value), 'replica', pairs)  5.59 us
    ppermute x3, waiting for transfers between devices, butterfly(): return lax.ppermute(step.gate(value), 'replica', pairs)  4.18 us
    pallas_call x1, Pallas kernels, merge(): pl.pallas_call(functools.partial(merge_kernel, groups), out_shape=[jax.Sh...  2.96 us
    unnamed x12, local copies, waits for them, and re-layouts  2.21 us
  transfers between devices with their start and end apart: 28, of which 10 were waited for; matrix products, arithmetic and copies ran while one was open for 4% of the time, Pallas kernels for 30%

profile of v2, /device:TPU:1, one launch (start us, length us, event | category | flops | bytes accessed | tf_op | source)
XLA Modules:
  0.0 94.3 jit_solution(7856618867158137499)
XLA Ops:
  0.7 3.3 %collective-permute-start.2 = (bf16[512,4096]{1,0:T(8,128)(2,1)}, bf16[512,4096]{1,0:T(8,128)(2,1)S(1)}, u32[]{:S(2)}, u32[]{:S(2)}) collective-permute-start(bf16[512,4096]{1,0:T(8,128)(2,1)} %bitcast.12), channel_id=1, source_target_pairs={{0,1},{1,0},{2,3},{3,2},{4,5},{5,4},{6,7},{7,6},{8,9},{9,8},{10,11... | collective-permute-start | bytes 12582920 | tf_op jit(solution)/shard_map/ppermute | solution.py:264
  4.1 1.1 %bitcast_subtract_fusion = f32[128,512]{1,0:T(8,128)S(1)} fusion(f32[128,512]{1,0:T(8,128)} %param.9, f32[1,128,512]{2,1,0:T(8,128)} %param.10), kind=kLoop, calls=%fused_computation.11 | loop fusion | flops 65536 | bytes 786432 | tf_op jit(solution)/shard_map/sub | solution.py:276
  5.3 0.8 collective-permute-start
  6.0 2.2 %copy-done.1 = bf16[1,512,4096]{2,1,0:T(8,128)(2,1)S(1)} copy-done((bf16[1,512,4096]{2,1,0:T(8,128)(2,1)S(1)}, bf16[1,512,4096]{2,1,0:T(8,128)(2,1)}, u32[]{:S(2)}) %copy-start.1) | copy-done | bytes 4194328
  8.2 1.6 %pack.1 = (bf16[512,1024]{1,0:T(8,128)(2,1)S(1)}, bf16[512,1024]{1,0:T(8,128)(2,1)S(1)}) custom-call(s32[3]{0:T(128)S(1)} %pad_add_fusion.place, bf16[512,4096]{1,0:T(8,128)(2,1)S(1)} %bitcast.13, bf16[512,4096]{1,0:T(8,128)(2,1)S(1)} %bitcast.14, bf16[512,4096]{1,0:T(8,128)(2,1)S(1)} %bitcast.15, bf16[512,4096]{1,0:T(8,128)(2,1)S(1)} %bitcast.16, ...), custom_call_target="tpu_custom_call" | custom-call | flops 1048576 | bytes 65536 | tf_op jit(solution)/shard_map/pack/pallas_call | solution.py:82
  9.9 2.9 %collective-permute-done.1 = f32[128,512]{1,0:T(8,128)S(1)} collective-permute-done((f32[128,512]{1,0:T(8,128)S(1)}, f32[128,512]{1,0:T(8,128)S(1)}, u32[]{:S(2)}, u32[]{:S(2)}) %collective-permute-start.1) | collective-permute-done | bytes 262176 | tf_op jit(solution)/shard_map/ppermute | solution.py:268
  12.7 0.3 collective-permute-done
  13.1 0.9 collective-permute-start.6
  14.0 4.0 %collective-permute-start.5 = (bf16[256,1024]{1,0:T(8,128)(2,1)S(1)}, bf16[256,1024]{1,0:T(8,128)(2,1)S(1)}, u32[]{:S(2)}, u32[]{:S(2)}) collective-permute-start(bf16[256,1024]{1,0:T(8,128)(2,1)S(1)} %pad_maximum_fusion.2.refs_12_), channel_id=1, source_target_pairs={{0,2},{1,15},{2,4},{3,1},{4,6},{5,3},{6,8},{7,5},{8,10},{9,7},{10,... | collective-permute-start | bytes 1572872 | tf_op jit(solution)/shard_map/ppermute | solution.py:264
  18.0 3.1 %grad.2 = (f32[384,1024]{1,0:T(8,128)S(1)}, f32[256,1024]{1,0:T(8,128)S(1)}, f32[256,1024]{1,0:T(8,128)S(1)}, f32[128,1024]{1,0:T(8,128)S(1)}) custom-call(s32[3]{0:T(128)S(1)} %pad_add_fusion.place, bf16[512,1024]{1,0:T(8,128)(2,1)S(1)} %get-tuple-element.143.refs_0_.refs_1_.refs_3_.refs_5_, ...), custom_call_target="tpu_custom_call" | custom-call | flops 1048576 | bytes 65536 | tf_op jit(solution)/shard_map/grad/pallas_call | solution.py:121
  21.1 0.1 convert_element_type.78
  21.4 1.3 %collective-permute-start.4 = (f16[384,1024]{1,0:T(8,128)(2,1)S(1)}, f16[384,1024]{1,0:T(8,128)(2,1)S(1)}, u32[]{:S(2)}, u32[]{:S(2)}) collective-permute-start(f16[384,1024]{1,0:T(8,128)(2,1)S(1)} %convert_element_type.78), channel_id=1, source_target_pairs={{0,16},{1,17},{2,18},{3,19},{4,20},{5,21},{6,22},{7,23},{8,24},{9,... | collective-permute-start | bytes 2359304 | tf_op jit(solution)/shard_map/ppermute | solution.py:264
  22.8 2.7 %collective-permute-start.7 = (f32[128,512]{1,0:T(8,128)S(1)}, f32[128,512]{1,0:T(8,128)S(1)}, u32[]{:S(2)}, u32[]{:S(2)}) collective-permute-start(f32[128,512]{1,0:T(8,128)S(1)} %add.71), channel_id=1, source_target_pairs={{0,128},{32,160},{64,192},{96,224},{128,0},{160,32},{192,64},{224,... | collective-permute-start | bytes 786440 | tf_op jit(solution)/shard_map/ppermute | solution.py:268
  25.5 0.3 collective-permute-start.10
  25.7 3.1 %grad.3 = (f32[384,1024]{1,0:T(8,128)S(1)}, f32[256,1024]{1,0:T(8,128)S(1)}, f32[256,1024]{1,0:T(8,128)S(1)}, f32[128,1024]{1,0:T(8,128)S(1)}) custom-call(s32[3]{0:T(128)S(1)} %pad_add_fusion.place, bf16[512,1024]{1,0:T(8,128)(2,1)S(1)} %get-tuple-element.151.refs_0_.refs_2_.refs_4_, ...), custom_call_target="tpu_custom_call" | custom-call | flops 1048576 | bytes 65536 | tf_op jit(solution)/shard_map/grad/pallas_call | solution.py:121
  28.8 1.3 %collective-permute-done.7 = f32[128,512]{1,0:T(8,128)S(1)} collective-permute-done((f32[128,512]{1,0:T(8,128)S(1)}, f32[128,512]{1,0:T(8,128)S(1)}, u32[]{:S(2)}, u32[]{:S(2)}) %collective-permute-start.7) | collective-permute-done | bytes 262176 | tf_op jit(solution)/shard_map/ppermute | solution.py:268
  30.1 2.7 %collective-permute-start.11 = (bf16[256,1024]{1,0:T(8,128)(2,1)S(1)}, bf16[256,1024]{1,0:T(8,128)(2,1)S(1)}, u32[]{:S(2)}, u32[]{:S(2)}) collective-permute-start(bf16[256,1024]{1,0:T(8,128)(2,1)S(1)} %collective-permute-done.5.refs_13_), channel_id=1, source_target_pairs={{0,2},{1,15},{2,4},{3,1},{4,6},{5,3},{6,8},{7,5},{8,10},{9,7},{10,... | collective-permute-start | bytes 1572872 | tf_op jit(solution)/shard_map/ppermute | solution.py:264
  32.8 5.4 %use.4 = (f32[512,1024]{1,0:T(8,128)S(1)}, f32[512,1024]{1,0:T(8,128)S(1)}, bf16[512,4096]{1,0:T(8,128)(2,1)}, bf16[512,768]{1,0:T(8,128)(2,1)S(1)}) custom-call(s32[3]{0:T(128)S(1)} %pad_add_fusion.place, bf16[512,1024]{1,0:T(8,128)(2,1)S(1)} %get-tuple-element.151.refs_0_.refs_2_.refs_4_, ...), custom_call_target="tpu_custom_call" | custom-call | flops 3221225472 | bytes 1048576 | tf_op jit(solution)/shard_map/use/pallas_call | solution.py:184
  38.2 0.5 collective-permute-done.4
  38.8 0.2 add_convert_fusion.5
  39.1 1.5 %collective-permute-start.9 = (f16[128,1024]{1,0:T(8,128)(2,1)S(1)}, f16[128,1024]{1,0:T(8,128)(2,1)S(1)}, u32[]{:S(2)}, u32[]{:S(2)}) collective-permute-start(f16[128,1024]{1,0:T(8,128)(2,1)S(1)} %get-tuple-element.178), channel_id=1, source_target_pairs={{0,14},{1,3},{2,0},{3,5},{4,2},{5,7},{6,4},{7,9},{8,6},{9,11},{10,... | collective-permute-start | bytes 786440 | tf_op jit(solution)/shard_map/ppermute | solution.py:264
  40.6 0.5 collective-permute-done.11.refs_8_
  41.1 4.0 %collective-permute-start.17 = (bf16[256,1024]{1,0:T(8,128)(2,1)S(1)}, bf16[256,1024]{1,0:T(8,128)(2,1)S(1)}, u32[]{:S(2)}, u32[]{:S(2)}) collective-permute-start(bf16[256,1024]{1,0:T(8,128)(2,1)S(1)} %collective-permute-done.12.refs_9_), channel_id=1, source_target_pairs={{0,14},{1,3},{2,0},{3,5},{4,2},{5,7},{6,4},{7,9},{8,6},{9,11},{10,... | collective-permute-start | bytes 1572872 | tf_op jit(solution)/shard_map/ppermute | solution.py:264
  45.1 4.9 %collective-permute-done.10 = f16[256,1024]{1,0:T(8,128)(2,1)S(1)} collective-permute-done((f16[256,1024]{1,0:T(8,128)(2,1)S(1)}, f16[256,1024]{1,0:T(8,128)(2,1)S(1)}, u32[]{:S(2)}, u32[]{:S(2)}) %collective-permute-start.10) | collective-permute-done | bytes 524320 | tf_op jit(solution)/shard_map/ppermute | solution.py:264
  50.0 1.2 %collective-permute-start.15 = (f16[256,1024]{1,0:T(8,128)(2,1)S(1)}, f16[256,1024]{1,0:T(8,128)(2,1)S(1)}, u32[]{:S(2)}, u32[]{:S(2)}) collective-permute-start(f16[256,1024]{1,0:T(8,128)(2,1)S(1)} %convert_element_type.80), channel_id=1, source_target_pairs={{0,16},{1,17},{2,18},{3,19},{4,20},{5,21},{6,22},{7,23},{8,24},{9,... | collective-permute-start | bytes 1572872 | tf_op jit(solution)/shard_map/ppermute | solution.py:264
  51.2 0.3 add_convert_fusion.3
  51.6 1.5 %collective-permute-start.14 = (f16[128,1024]{1,0:T(8,128)(2,1)S(1)}, f16[128,1024]{1,0:T(8,128)(2,1)S(1)}, u32[]{:S(2)}, u32[]{:S(2)}) collective-permute-start(f16[128,1024]{1,0:T(8,128)(2,1)S(1)} %get-tuple-element.189), channel_id=1, source_target_pairs={{0,14},{1,3},{2,0},{3,5},{4,2},{5,7},{6,4},{7,9},{8,6},{9,11},{10,... | collective-permute-start | bytes 786440 | tf_op jit(solution)/shard_map/ppermute | solution.py:264
  53.1 4.4 %use.5 = (f32[512,1024]{1,0:T(8,128)S(1)}, f32[512,1024]{1,0:T(8,128)S(1)}, bf16[512,4096]{1,0:T(8,128)(2,1)}, bf16[512,512]{1,0:T(8,128)(2,1)S(1)}) custom-call(s32[3]{0:T(128)S(1)} %pad_add_fusion.place, bf16[512,1024]{1,0:T(8,128)(2,1)S(1)} %get-tuple-element.151.refs_0_.refs_2_.refs_4_, ...), custom_call_target="tpu_custom_call", output_to_operand_aliasing={{2}: (15, {})} | custom-call | flops 2147483648 | bytes 1048576 | tf_op jit(solution)/shard_map/use/pallas_call | solution.py:184
  57.6 0.3 collective-permute-done.17.refs_9_
  57.9 0.9 %collective-permute-done.16.refs_8_ = bf16[256,1024]{1,0:T(8,128)(2,1)S(1)} collective-permute-done((bf16[256,1024]{1,0:T(8,128)(2,1)S(1)}, bf16[256,1024]{1,0:T(8,128)(2,1)S(1)}, u32[]{:S(2)}, u32[]{:S(2)}) %collective-permute-start.16) | collective-permute-done | bytes 524320 | tf_op jit(solution)/shard_map/ppermute | solution.py:264
  58.9 2.5 %collective-permute-start.21 = (bf16[128,1024]{1,0:T(8,128)(2,1)S(1)}, bf16[128,1024]{1,0:T(8,128)(2,1)S(1)}, u32[]{:S(2)}, u32[]{:S(2)}) collective-permute-start(bf16[128,1024]{1,0:T(8,128)(2,1)S(1)} %slice.58), channel_id=1, source_target_pairs={{0,2},{1,15},{2,4},{3,1},{4,6},{5,3},{6,8},{7,5},{8,10},{9,7},{10,... | collective-permute-start | bytes 786440 | tf_op jit(solution)/shard_map/ppermute | solution.py:264
  61.4 1.8 %collective-permute-start.22 = (bf16[128,1024]{1,0:T(8,128)(2,1)S(1)}, bf16[128,1024]{1,0:T(8,128)(2,1)S(1)}, u32[]{:S(2)}, u32[]{:S(2)}) collective-permute-start(bf16[128,1024]{1,0:T(8,128)(2,1)S(1)} %slice.59), channel_id=1, source_target_pairs={{0,14},{1,3},{2,0},{3,5},{4,2},{5,7},{6,4},{7,9},{8,6},{9,11},{10,... | collective-permute-start | bytes 786440 | tf_op jit(solution)/shard_map/ppermute | solution.py:264
  63.2 1.3 %collective-permute-done.13 = f16[128,1024]{1,0:T(8,128)(2,1)S(1)} collective-permute-done((f16[128,1024]{1,0:T(8,128)(2,1)S(1)}, f16[128,1024]{1,0:T(8,128)(2,1)S(1)}, u32[]{:S(2)}, u32[]{:S(2)}) %collective-permute-start.13) | collective-permute-done | bytes 262176 | tf_op jit(solution)/shard_map/ppermute | solution.py:264
  64.5 0.3 add_convert_fusion
  64.8 1.7 %collective-permute-start.19 = (f16[128,1024]{1,0:T(8,128)(2,1)S(1)}, f16[128,1024]{1,0:T(8,128)(2,1)S(1)}, u32[]{:S(2)}, u32[]{:S(2)}) collective-permute-start(f16[128,1024]{1,0:T(8,128)(2,1)S(1)} %convert_element_type.81), channel_id=1, source_target_pairs={{0,16},{1,17},{2,18},{3,19},{4,20},{5,21},{6,22},{7,23},{8,24},{9,... | collective-permute-start | bytes 786440 | tf_op jit(solution)/shard_map/ppermute | solution.py:264
  66.5 2.8 %collective-permute-start.20 = (f32[128,512]{1,0:T(8,128)S(1)}, f32[128,512]{1,0:T(8,128)S(1)}, u32[]{:S(2)}, u32[]{:S(2)}) collective-permute-start(f32[128,512]{1,0:T(8,128)S(1)} %add.80), channel_id=1, source_target_pairs={{0,32},{32,0},{64,96},{96,64},{128,160},{160,128},{192,224},{224,1... | collective-permute-start | bytes 786440 | tf_op jit(solution)/shard_map/ppermute | solution.py:268
  69.3 0.2 collective-permute-start.18
  69.6 4.4 %use.6 = (f32[512,1024]{1,0:T(8,128)S(1)}, f32[512,1024]{1,0:T(8,128)S(1)}, bf16[512,4096]{1,0:T(8,128)(2,1)}, bf16[512,512]{1,0:T(8,128)(2,1)S(1)}) custom-call(s32[3]{0:T(128)S(1)} %pad_add_fusion.place, bf16[512,1024]{1,0:T(8,128)(2,1)S(1)} %get-tuple-element.151.refs_0_.refs_2_.refs_4_, ...), custom_call_target="tpu_custom_call", output_to_operand_aliasing={{2}: (15, {})} | custom-call | flops 1048576 | bytes 65536 | tf_op jit(solution)/shard_map/use/pallas_call | solution.py:184
  74.0 3.3 %use.7 = (f32[512,1024]{1,0:T(8,128)S(1)}, f32[512,1024]{1,0:T(8,128)S(1)}, bf16[512,4096]{1,0:T(8,128)(2,1)}, bf16[512,256]{1,0:T(8,128)(2,1)S(1)}) custom-call(s32[3]{0:T(128)S(1)} %pad_add_fusion.place, bf16[512,1024]{1,0:T(8,128)(2,1)S(1)} %get-tuple-element.151.refs_0_.refs_2_.refs_4_, ...), custom_call_target="tpu_custom_call", output_to_operand_aliasing={{2}: (11, {})} | custom-call | flops 1048576 | bytes 65536 | tf_op jit(solution)/shard_map/use/pallas_call | solution.py:184
  77.4 6.1 %collective-permute-start.25 = (f32[512,1024]{1,0:T(8,128)S(1)}, f32[512,1024]{1,0:T(8,128)S(1)}, u32[]{:S(2)}, u32[]{:S(2)}) collective-permute-start(f32[512,1024]{1,0:T(8,128)S(1)} %get-tuple-element.246), channel_id=1, source_target_pairs={{0,1},{1,0},{2,3},{3,2},{4,5},{5,4},{6,7},{7,6},{8,9},{9,8},{10,11... | collective-permute-start | bytes 6291464 | tf_op jit(solution)/shard_map/ppermute | solution.py:264
  83.7 0.5 collective-permute-start.27
  84.2 0.1 add_convert_fusion.1
  84.3 0.8 collective-permute-start.24
  85.1 2.3 %collective-permute-start.23 = (f16[128,1024]{1,0:T(8,128)(2,1)S(1)}, f16[128,1024]{1,0:T(8,128)(2,1)S(1)}, u32[]{:S(2)}, u32[]{:S(2)}) collective-permute-start(f16[128,1024]{1,0:T(8,128)(2,1)S(1)} %add_convert_fusion.1), channel_id=1, source_target_pairs={{0,2},{1,15},{2,4},{3,1},{4,6},{5,3},{6,8},{7,5},{8,10},{9,7},{10,... | collective-permute-start | bytes 786440 | tf_op jit(solution)/shard_map/ppermute | solution.py:264
  87.4 0.9 multiply_add_fusion
  88.3 2.0 %collective-permute-done.27.refs_1_ = bf16[512,768]{1,0:T(8,128)(2,1)S(1)} collective-permute-done((bf16[512,768]{1,0:T(8,128)(2,1)S(1)}, bf16[512,768]{1,0:T(8,128)(2,1)S(1)}, u32[]{:S(2)}, u32[]{:S(2)}) %collective-permute-start.27) | collective-permute-done | bytes 786464 | tf_op jit(solution)/shard_map/ppermute | solution.py:264
  90.3 3.0 %merge.1 = (bf16[512,1024]{1,0:T(8,128)(2,1)}, bf16[512,4096]{1,0:T(8,128)(2,1)}) custom-call(s32[3]{0:T(128)S(1)} %pad_add_fusion.place, bf16[512,1280]{1,0:T(8,128)(2,1)S(1)} %collective-permute-done.26.refs_0_, bf16[512,768]{1,0:T(8,128)(2,1)S(1)} %collective-permute-done.27.refs_1_, ...), custom_call_target="tpu_custom_call", output_to_operand_aliasing={{1}: (5, {})} | custom-call | flops 1048576 | bytes 65536 | tf_op jit(solution)/shard_map/merge/pallas_call | solution.py:230
  93.3 1.0 %multiply_bitcast_fusion = f32[1,128,1024]{2,1,0:T(8,128)} fusion(f16[128,1024]{1,0:T(8,128)(2,1)S(1)} %collective-permute-done.24, f16[128,1024]{1,0:T(8,128)(2,1)S(1)} %collective-permute-done.23, f32[384,1024]{1,0:T(8,128)S(1)} %get-tuple-element.159, f16[384,1024]{1,0:T(8,128)(2,1)S(1)} %collective-permute-done.4), kind=kLoop, calls=%fused_computation.3 | loop fusion | flops 917504 | bytes 1835008 | tf_op jit(solution)/shard_map/broadcast_in_dim | solution.py:349
  (47 shorter events, 1.1 us)
Async XLA Ops:
  0.7 12.3 %collective-permute-start.2 = (bf16[512,4096]{1,0:T(8,128)(2,1)}, bf16[512,4096]{1,0:T(8,128)(2,1)S(1)}, u32[]{:S(2)}, u32[]{:S(2)}) collective-permute-start(bf16[512,4096]{1,0:T(8,128)(2,1)} %bitcast.12), channel_id=1, source_target_pairs={{0,1},{1,0},{2,3},{3,2},{4,5},{5,4},{6,7},{7,6},{8,9},{9,8},{10,11... | collective-permute-start | bytes 12582920 | tf_op jit(solution)/shard_map/ppermute | solution.py:264
  4.0 9.0 %collective-permute-start.3 = (bf16[512,1024]{1,0:T(8,128)(2,1)}, bf16[512,1024]{1,0:T(8,128)(2,1)S(1)}, u32[]{:S(2)}, u32[]{:S(2)}) collective-permute-start(bf16[512,1024]{1,0:T(8,128)(2,1)} %bitcast.29), channel_id=1, source_target_pairs={{0,1},{1,0},{2,3},{3,2},{4,5},{5,4},{6,7},{7,6},{8,9},{9,8},{10,11... | collective-permute-start | bytes 3145736 | tf_op jit(solution)/shard_map/ppermute | solution.py:264
  5.2 7.6 %collective-permute-start.1 = (f32[128,512]{1,0:T(8,128)S(1)}, f32[128,512]{1,0:T(8,128)S(1)}, u32[]{:S(2)}, u32[]{:S(2)}) collective-permute-start(f32[128,512]{1,0:T(8,128)S(1)} %bitcast_subtract_fusion), channel_id=1, source_target_pairs={{0,64},{32,96},{64,0},{96,32},{128,192},{160,224},{192,128},{224,1... | collective-permute-start | bytes 786440 | tf_op jit(solution)/shard_map/ppermute | solution.py:268
  5.3 7.8 %collective-permute-start = (bf16[128,1024]{1,0:T(8,128)(2,1)}, bf16[128,1024]{1,0:T(8,128)(2,1)S(1)}, u32[]{:S(2)}, u32[]{:S(2)}) collective-permute-start(bf16[128,1024]{1,0:T(8,128)(2,1)} %bitcast.37), channel_id=1, source_target_pairs={{0,16},{1,17},{2,18},{3,19},{4,20},{5,21},{6,22},{7,23},{8,24},{9,... | collective-permute-start | bytes 786440 | tf_op jit(solution)/shard_map/ppermute | solution.py:264
  6.0 2.2 %copy-start.1 = (bf16[1,512,4096]{2,1,0:T(8,128)(2,1)S(1)}, bf16[1,512,4096]{2,1,0:T(8,128)(2,1)}, u32[]{:S(2)}) copy-start(bf16[1,512,4096]{2,1,0:T(8,128)(2,1)} %param.6) | copy-start | bytes 12582916
  8.2 4.8 %copy-start.4 = (bf16[1,128,1024]{2,1,0:T(8,128)(2,1)S(1)}, bf16[1,128,1024]{2,1,0:T(8,128)(2,1)}, u32[]{:S(2)}) copy-start(bf16[1,128,1024]{2,1,0:T(8,128)(2,1)} %param.7) | copy-start | bytes 786436
  8.2 9.8 %copy-start.2 = (bf16[1,512,1024]{2,1,0:T(8,128)(2,1)S(1)}, bf16[1,512,1024]{2,1,0:T(8,128)(2,1)}, u32[]{:S(2)}) copy-start(bf16[1,512,1024]{2,1,0:T(8,128)(2,1)} %param.8) | copy-start | bytes 3145732
  13.1 12.7 %copy-start = (bf16[512,4096]{1,0:T(8,128)(2,1)}, bf16[512,4096]{1,0:T(8,128)(2,1)S(1)}, u32[]{:S(2)}) copy-start(bf16[512,4096]{1,0:T(8,128)(2,1)S(1)} %collective-permute-done.2.refs_1_.refs_2_.refs_3_.refs_4_.refs_5_.refs_6_.refs_7_.refs_8_.refs_9_.refs_10_.refs_11_) | copy-start | bytes 12582916
  13.1 17.0 %collective-permute-start.6 = (bf16[256,1024]{1,0:T(8,128)(2,1)S(1)}, bf16[256,1024]{1,0:T(8,128)(2,1)S(1)}, u32[]{:S(2)}, u32[]{:S(2)}) collective-permute-start(bf16[256,1024]{1,0:T(8,128)(2,1)S(1)} %pad_maximum_fusion.2.refs_12_), channel_id=1, source_target_pairs={{0,14},{1,3},{2,0},{3,5},{4,2},{5,7},{6,4},{7,9},{8,6},{9,11},{10,... | collective-permute-start | bytes 1572872 | tf_op jit(solution)/shard_map/ppermute | solution.py:264
  14.0 16.1 %collective-permute-start.5 = (bf16[256,1024]{1,0:T(8,128)(2,1)S(1)}, bf16[256,1024]{1,0:T(8,128)(2,1)S(1)}, u32[]{:S(2)}, u32[]{:S(2)}) collective-permute-start(bf16[256,1024]{1,0:T(8,128)(2,1)S(1)} %pad_maximum_fusion.2.refs_12_), channel_id=1, source_target_pairs={{0,2},{1,15},{2,4},{3,1},{4,6},{5,3},{6,8},{7,5},{8,10},{9,7},{10,... | collective-permute-start | bytes 1572872 | tf_op jit(solution)/shard_map/ppermute | solution.py:264
  21.4 17.4 %collective-permute-start.4 = (f16[384,1024]{1,0:T(8,128)(2,1)S(1)}, f16[384,1024]{1,0:T(8,128)(2,1)S(1)}, u32[]{:S(2)}, u32[]{:S(2)}) collective-permute-start(f16[384,1024]{1,0:T(8,128)(2,1)S(1)} %convert_element_type.78), channel_id=1, source_target_pairs={{0,16},{1,17},{2,18},{3,19},{4,20},{5,21},{6,22},{7,23},{8,24},{9,... | collective-permute-start | bytes 2359304 | tf_op jit(solution)/shard_map/ppermute | solution.py:264
  22.8 7.4 %collective-permute-start.7 = (f32[128,512]{1,0:T(8,128)S(1)}, f32[128,512]{1,0:T(8,128)S(1)}, u32[]{:S(2)}, u32[]{:S(2)}) collective-permute-start(f32[128,512]{1,0:T(8,128)S(1)} %add.71), channel_id=1, source_target_pairs={{0,128},{32,160},{64,192},{96,224},{128,0},{160,32},{192,64},{224,... | collective-permute-start | bytes 786440 | tf_op jit(solution)/shard_map/ppermute | solution.py:268
  25.5 24.5 %collective-permute-start.10 = (f16[256,1024]{1,0:T(8,128)(2,1)S(1)}, f16[256,1024]{1,0:T(8,128)(2,1)S(1)}, u32[]{:S(2)}, u32[]{:S(2)}) collective-permute-start(f16[256,1024]{1,0:T(8,128)(2,1)S(1)} %convert_element_type.79), channel_id=1, source_target_pairs={{0,16},{1,17},{2,18},{3,19},{4,20},{5,21},{6,22},{7,23},{8,24},{9,... | collective-permute-start | bytes 1572872 | tf_op jit(solution)/shard_map/ppermute | solution.py:264
  30.1 10.4 %collective-permute-start.12 = (bf16[256,1024]{1,0:T(8,128)(2,1)S(1)}, bf16[256,1024]{1,0:T(8,128)(2,1)S(1)}, u32[]{:S(2)}, u32[]{:S(2)}) collective-permute-start(bf16[256,1024]{1,0:T(8,128)(2,1)S(1)} %collective-permute-done.6.refs_14_), channel_id=1, source_target_pairs={{0,14},{1,3},{2,0},{3,5},{4,2},{5,7},{6,4},{7,9},{8,6},{9,11},{10,... | collective-permute-start | bytes 1572872 | tf_op jit(solution)/shard_map/ppermute | solution.py:264
  30.1 11.0 %collective-permute-start.11 = (bf16[256,1024]{1,0:T(8,128)(2,1)S(1)}, bf16[256,1024]{1,0:T(8,128)(2,1)S(1)}, u32[]{:S(2)}, u32[]{:S(2)}) collective-permute-start(bf16[256,1024]{1,0:T(8,128)(2,1)S(1)} %collective-permute-done.5.refs_13_), channel_id=1, source_target_pairs={{0,2},{1,15},{2,4},{3,1},{4,6},{5,3},{6,8},{7,5},{8,10},{9,7},{10,... | collective-permute-start | bytes 1572872 | tf_op jit(solution)/shard_map/ppermute | solution.py:264
  39.0 11.0 %collective-permute-start.8 = (f16[128,1024]{1,0:T(8,128)(2,1)S(1)}, f16[128,1024]{1,0:T(8,128)(2,1)S(1)}, u32[]{:S(2)}, u32[]{:S(2)}) collective-permute-start(f16[128,1024]{1,0:T(8,128)(2,1)S(1)} %get-tuple-element.177), channel_id=1, source_target_pairs={{0,2},{1,15},{2,4},{3,1},{4,6},{5,3},{6,8},{7,5},{8,10},{9,7},{10,... | collective-permute-start | bytes 786440 | tf_op jit(solution)/shard_map/ppermute | solution.py:264
  39.1 11.0 %collective-permute-start.9 = (f16[128,1024]{1,0:T(8,128)(2,1)S(1)}, f16[128,1024]{1,0:T(8,128)(2,1)S(1)}, u32[]{:S(2)}, u32[]{:S(2)}) collective-permute-start(f16[128,1024]{1,0:T(8,128)(2,1)S(1)} %get-tuple-element.178), channel_id=1, source_target_pairs={{0,14},{1,3},{2,0},{3,5},{4,2},{5,7},{6,4},{7,9},{8,6},{9,11},{10,... | collective-permute-start | bytes 786440 | tf_op jit(solution)/shard_map/ppermute | solution.py:264
  41.1 16.8 %collective-permute-start.17 = (bf16[256,1024]{1,0:T(8,128)(2,1)S(1)}, bf16[256,1024]{1,0:T(8,128)(2,1)S(1)}, u32[]{:S(2)}, u32[]{:S(2)}) collective-permute-start(bf16[256,1024]{1,0:T(8,128)(2,1)S(1)} %collective-permute-done.12.refs_9_), channel_id=1, source_target_pairs={{0,14},{1,3},{2,0},{3,5},{4,2},{5,7},{6,4},{7,9},{8,6},{9,11},{10,... | collective-permute-start | bytes 1572872 | tf_op jit(solution)/shard_map/ppermute | solution.py:264
  45.1 13.8 %collective-permute-start.16 = (bf16[256,1024]{1,0:T(8,128)(2,1)S(1)}, bf16[256,1024]{1,0:T(8,128)(2,1)S(1)}, u32[]{:S(2)}, u32[]{:S(2)}) collective-permute-start(bf16[256,1024]{1,0:T(8,128)(2,1)S(1)} %collective-permute-done.11.refs_8_), channel_id=1, source_target_pairs={{0,2},{1,15},{2,4},{3,1},{4,6},{5,3},{6,8},{7,5},{8,10},{9,7},{10,... | collective-permute-start | bytes 1572872 | tf_op jit(solution)/shard_map/ppermute | solution.py:264
  50.0 14.5 %collective-permute-start.15 = (f16[256,1024]{1,0:T(8,128)(2,1)S(1)}, f16[256,1024]{1,0:T(8,128)(2,1)S(1)}, u32[]{:S(2)}, u32[]{:S(2)}) collective-permute-start(f16[256,1024]{1,0:T(8,128)(2,1)S(1)} %convert_element_type.80), channel_id=1, source_target_pairs={{0,16},{1,17},{2,18},{3,19},{4,20},{5,21},{6,22},{7,23},{8,24},{9,... | collective-permute-start | bytes 1572872 | tf_op jit(solution)/shard_map/ppermute | solution.py:264
  51.5 13.0 %collective-permute-start.13 = (f16[128,1024]{1,0:T(8,128)(2,1)S(1)}, f16[128,1024]{1,0:T(8,128)(2,1)S(1)}, u32[]{:S(2)}, u32[]{:S(2)}) collective-permute-start(f16[128,1024]{1,0:T(8,128)(2,1)S(1)} %get-tuple-element.187), channel_id=1, source_target_pairs={{0,2},{1,15},{2,4},{3,1},{4,6},{5,3},{6,8},{7,5},{8,10},{9,7},{10,... | collective-permute-start | bytes 786440 | tf_op jit(solution)/shard_map/ppermute | solution.py:264
  51.6 12.9 %collective-permute-start.14 = (f16[128,1024]{1,0:T(8,128)(2,1)S(1)}, f16[128,1024]{1,0:T(8,128)(2,1)S(1)}, u32[]{:S(2)}, u32[]{:S(2)}) collective-permute-start(f16[128,1024]{1,0:T(8,128)(2,1)S(1)} %get-tuple-element.189), channel_id=1, source_target_pairs={{0,14},{1,3},{2,0},{3,5},{4,2},{5,7},{6,4},{7,9},{8,6},{9,11},{10,... | collective-permute-start | bytes 786440 | tf_op jit(solution)/shard_map/ppermute | solution.py:264
  58.9 15.1 %collective-permute-start.21 = (bf16[128,1024]{1,0:T(8,128)(2,1)S(1)}, bf16[128,1024]{1,0:T(8,128)(2,1)S(1)}, u32[]{:S(2)}, u32[]{:S(2)}) collective-permute-start(bf16[128,1024]{1,0:T(8,128)(2,1)S(1)} %slice.58), channel_id=1, source_target_pairs={{0,2},{1,15},{2,4},{3,1},{4,6},{5,3},{6,8},{7,5},{8,10},{9,7},{10,... | collective-permute-start | bytes 786440 | tf_op jit(solution)/shard_map/ppermute | solution.py:264
  61.4 12.6 %collective-permute-start.22 = (bf16[128,1024]{1,0:T(8,128)(2,1)S(1)}, bf16[128,1024]{1,0:T(8,128)(2,1)S(1)}, u32[]{:S(2)}, u32[]{:S(2)}) collective-permute-start(bf16[128,1024]{1,0:T(8,128)(2,1)S(1)} %slice.59), channel_id=1, source_target_pairs={{0,14},{1,3},{2,0},{3,5},{4,2},{5,7},{6,4},{7,9},{8,6},{9,11},{10,... | collective-permute-start | bytes 786440 | tf_op jit(solution)/shard_map/ppermute | solution.py:264
  64.8 12.6 %collective-permute-start.19 = (f16[128,1024]{1,0:T(8,128)(2,1)S(1)}, f16[128,1024]{1,0:T(8,128)(2,1)S(1)}, u32[]{:S(2)}, u32[]{:S(2)}) collective-permute-start(f16[128,1024]{1,0:T(8,128)(2,1)S(1)} %convert_element_type.81), channel_id=1, source_target_pairs={{0,16},{1,17},{2,18},{3,19},{4,20},{5,21},{6,22},{7,23},{8,24},{9,... | collective-permute-start | bytes 786440 | tf_op jit(solution)/shard_map/ppermute | solution.py:264
  66.5 10.9 %collective-permute-start.20 = (f32[128,512]{1,0:T(8,128)S(1)}, f32[128,512]{1,0:T(8,128)S(1)}, u32[]{:S(2)}, u32[]{:S(2)}) collective-permute-start(f32[128,512]{1,0:T(8,128)S(1)} %add.80), channel_id=1, source_target_pairs={{0,32},{32,0},{64,96},{96,64},{128,160},{160,128},{192,224},{224,1... | collective-permute-start | bytes 786440 | tf_op jit(solution)/shard_map/ppermute | solution.py:268
  69.3 8.1 %collective-permute-start.18 = (f16[128,1024]{1,0:T(8,128)(2,1)S(1)}, f16[128,1024]{1,0:T(8,128)(2,1)S(1)}, u32[]{:S(2)}, u32[]{:S(2)}) collective-permute-start(f16[128,1024]{1,0:T(8,128)(2,1)S(1)} %get-tuple-element.211), channel_id=1, source_target_pairs={{0,2},{1,15},{2,4},{3,1},{4,6},{5,3},{6,8},{7,5},{8,10},{9,7},{10,... | collective-permute-start | bytes 786440 | tf_op jit(solution)/shard_map/ppermute | solution.py:264
  77.4 10.1 %copy-start.3 = (f32[128,512]{1,0:T(8,128)S(1)}, f32[128,512]{1,0:T(8,128)}, u32[]{:S(2)}) copy-start(f32[128,512]{1,0:T(8,128)} %param.9) | copy-start | bytes 786436
  77.4 10.1 %copy-start.5 = (f32[128,512]{1,0:T(8,128)S(1)}, f32[128,512]{1,0:T(8,128)}, u32[]{:S(2)}) copy-start(f32[128,512]{1,0:T(8,128)} %param.11) | copy-start | bytes 786436
  77.4 12.9 %collective-permute-start.25 = (f32[512,1024]{1,0:T(8,128)S(1)}, f32[512,1024]{1,0:T(8,128)S(1)}, u32[]{:S(2)}, u32[]{:S(2)}) collective-permute-start(f32[512,1024]{1,0:T(8,128)S(1)} %get-tuple-element.246), channel_id=1, source_target_pairs={{0,1},{1,0},{2,3},{3,2},{4,5},{5,4},{6,7},{7,6},{8,9},{9,8},{10,11... | collective-permute-start | bytes 6291464 | tf_op jit(solution)/shard_map/ppermute | solution.py:264
  83.5 6.8 %collective-permute-start.26 = (bf16[512,1280]{1,0:T(8,128)(2,1)S(1)}, bf16[512,1280]{1,0:T(8,128)(2,1)S(1)}, u32[]{:S(2)}, u32[]{:S(2)}) collective-permute-start(bf16[512,1280]{1,0:T(8,128)(2,1)S(1)} %pad_maximum_fusion), channel_id=1, source_target_pairs={{0,1},{1,0},{2,3},{3,2},{4,5},{5,4},{6,7},{7,6},{8,9},{9,8},{10,11... | collective-permute-start | bytes 3932168 | tf_op jit(solution)/shard_map/ppermute | solution.py:264
  83.7 6.6 %collective-permute-start.27 = (bf16[512,768]{1,0:T(8,128)(2,1)S(1)}, bf16[512,768]{1,0:T(8,128)(2,1)S(1)}, u32[]{:S(2)}, u32[]{:S(2)}) collective-permute-start(bf16[512,768]{1,0:T(8,128)(2,1)S(1)} %pad_maximum_fusion.1), channel_id=1, source_target_pairs={{0,1},{1,0},{2,3},{3,2},{4,5},{5,4},{6,7},{7,6},{8,9},{9,8},{10,11... | collective-permute-start | bytes 2359304 | tf_op jit(solution)/shard_map/ppermute | solution.py:264
  84.3 9.0 %collective-permute-start.24 = (f16[128,1024]{1,0:T(8,128)(2,1)S(1)}, f16[128,1024]{1,0:T(8,128)(2,1)S(1)}, u32[]{:S(2)}, u32[]{:S(2)}) collective-permute-start(f16[128,1024]{1,0:T(8,128)(2,1)S(1)} %get-tuple-element.244), channel_id=1, source_target_pairs={{0,14},{1,3},{2,0},{3,5},{4,2},{5,7},{6,4},{7,9},{8,6},{9,11},{10,... | collective-permute-start | bytes 786440 | tf_op jit(solution)/shard_map/ppermute | solution.py:264
  85.1 8.2 %collective-permute-start.23 = (f16[128,1024]{1,0:T(8,128)(2,1)S(1)}, f16[128,1024]{1,0:T(8,128)(2,1)S(1)}, u32[]{:S(2)}, u32[]{:S(2)}) collective-permute-start(f16[128,1024]{1,0:T(8,128)(2,1)S(1)} %add_convert_fusion.1), channel_id=1, source_target_pairs={{0,2},{1,15},{2,4},{3,1},{4,6},{5,3},{6,8},{7,5},{8,10},{9,7},{10,... | collective-permute-start | bytes 786440 | tf_op jit(solution)/shard_map/ppermute | solution.py:264

commit v3 on v2

--- a/solution.py
+++ b/solution.py
@@ -135,34 +135,34 @@
     )(place, hidden[0][dx], *([hidden[1]] * count), *cot)
 
 
-def use_kernel(spots, arrays, first, place, *refs):
+def use_kernel(spots, arrays, first, place, near, far, other, *refs):
     count = len(spots)
-    rows = [jnp.concatenate([r[...] for r in refs[k * count : (k + 1) * count]], axis=1) for k in range(2)]
-    refs = refs[2 * count :]
-    weight = jnp.concatenate([r[...] for r in refs[:arrays]], axis=0)
-    refs = refs[arrays:]
+    weights, refs = refs[:arrays], refs[arrays:]
     cot, refs = refs[:2], refs[2:]
     if not first:
         acc, refs = refs[:2], refs[3:]
-    out_keys, out_back, out_other, block, sems = refs[:2], refs[2], refs[3], refs[4], refs[5]
+    out_keys, out_back, out_other, block, rows, sems = refs[:2], *refs[2:]
+    places = [pl.ds(pl.multiple_of(block_at(place, *spot) * 128, 128), 128) for spot in spots]
+    parts = [pl.ds(k * 128, 128) for k in range(count)]
+    reads = [pltpu.make_async_copy(other.at[:, p], rows.at[:, q], sems.at[0, k]) for k, (p, q) in enumerate(zip(places, parts))]
+    writes = [pltpu.make_async_copy(block.at[:, q], out_back.at[:, p], sems.at[1, k]) for k, (p, q) in enumerate(zip(places, parts))]
+    for copy in reads:
+        copy.start()
+    weight = jnp.concatenate([r[...] for r in weights], axis=0)
     dims = (((1,), (1,)), ((), ()))
     block[...] = lax.dot_general(cot[0][...], weight, dims, preferred_element_type=F32).astype(BF16)
-    copies = []
-    for k, spot in enumerate(spots):
-        at = pl.multiple_of(block_at(place, *spot) * 128, 128)
-        copies.append(
-            pltpu.make_async_copy(
-                block.at[:, pl.ds(k * 128, 128)], out_back.at[:, pl.ds(at, 128)], sems.at[k]
-            )
-        )
-        copies[-1].start()
+    for copy in writes:
+        copy.start()
     out_other[...] = lax.dot_general(cot[1][...], weight, dims, preferred_element_type=F32).astype(BF16)
-    for k in range(2):
-        keys = jnp.dot(rows[k], weight, preferred_element_type=F32)
-        if not first:
-            keys += acc[k][...]
-        out_keys[k][...] = keys
-    for copy in copies:
+    sides = (near, far)
+    own = [sides[dx][:, ORDER.index(dz) * 128 : ORDER.index(dz) * 128 + 128] for dx, dz, _ in spots]
+    keys = jnp.dot(jnp.concatenate(own, axis=1), weight, preferred_element_type=F32)
+    out_keys[0][...] = keys if first else keys + acc[0][...]
+    for copy in reads:
+        copy.wait()
+    keys = jnp.dot(rows[...], weight, preferred_element_type=F32)
+    out_keys[1][...] = keys if first else keys + acc[1][...]
+    for copy in writes:
         copy.wait()
 
 
@@ -173,14 +173,14 @@
     flops = 8 * tokens * count * 128 * width
     cost = pl.CostEstimate(flops=flops, bytes_accessed=1 << 20, transcendentals=0)
     anywhere = pl.BlockSpec(memory_space=pl.ANY)
-    in_specs = [packed(tokens, ORDER.index(s[1])) for s in spots] + [columns(tokens, s) for s in spots]
-    in_specs += [whole(w.shape) for w in weights] + [whole((tokens, width))] * 2
-    operands = [hidden[0][s[0]] for s in spots] + [hidden[1]] * count + list(weights) + list(cot)
+    vmem = pl.BlockSpec(memory_space=pltpu.VMEM)
+    in_specs = [pl.BlockSpec(memory_space=pltpu.SMEM), vmem, vmem, anywhere] + [vmem] * (len(weights) + 2)
+    operands = [place, *hidden[0], hidden[1], *weights, *cot]
     aliases = {}
     if not first:
-        in_specs += [whole((tokens, width))] * 2 + [anywhere]
+        in_specs += [vmem, vmem, anywhere]
         operands += list(state)
-        aliases = {len(operands): 2}
+        aliases = {len(operands) - 1: 2, len(operands) - 2: 1, len(operands) - 3: 0}
     return pl.pallas_call(
         functools.partial(use_kernel, spots, len(weights), first),
         out_shape=[
@@ -189,21 +189,18 @@
             jax.ShapeDtypeStruct(hidden[1].shape, BF16),
             jax.ShapeDtypeStruct((tokens, count * 128), BF16),
         ],
-        grid_spec=pltpu.PrefetchScalarGridSpec(
-            num_scalar_prefetch=1,
-            grid=(1,),
-            in_specs=in_specs,
-            out_specs=[whole((tokens, width))] * 2 + [anywhere, whole((tokens, count * 128))],
-            scratch_shapes=[
-                pltpu.VMEM((tokens, count * 128), BF16),
-                pltpu.SemaphoreType.DMA((count,)),
-            ],
-        ),
+        in_specs=in_specs,
+        out_specs=[vmem, vmem, anywhere, vmem],
+        scratch_shapes=[
+            pltpu.VMEM((tokens, count * 128), BF16),
+            pltpu.VMEM((tokens, count * 128), BF16),
+            pltpu.SemaphoreType.DMA((2, count)),
+        ],
         input_output_aliases=aliases,
         compiler_params=params(40),
         cost_estimate=COST if last else cost,
         name="use",
-    )(place, *operands)
+    )(*operands)
 
 
 def merge_kernel(groups, place, *refs):

time: 94.7 us -> 94.1 us (level)
  Pallas kernels: 28.3 us -> 25.2 us
  waiting for transfers between devices: 15.1 us -> 17.1 us
    pallas_call x4, Pallas kernels: 17.6 us -> 14.5 us  [use(): pl.pallas_call(functools.partial(use_kernel, spots, len(weights), first),...]
    ppermute x25, waiting for transfers between devices: 10.9 us -> 12.4 us  [send(): return lax.ppermute(step.gate(value), 'fsdp', pairs)]
    unnamed x12 -> x14, local copies, waits for them, and re-layouts: 2.21 us -> 2.21 us
  transfers between devices with their start and end apart: 28 -> 28, of which waited for: 10 -> 11; matrix products, arithmetic and copies ran while one was open for 4% -> 4% of each run, Pallas kernels for 30% -> 27%
where the time goes in v3:
time: 94.1 us; the launch traced here: 93.9 us
  starting transfers between devices  43.1 us (46%)
  Pallas kernels  25.2 us (27%)
  waiting for transfers between devices  17.1 us (18%)
  other arithmetic  5.26 us (6%)
  local copies, waits for them, and re-layouts  2.25 us (2%)
    ppermute x25, starting transfers between devices, send(): return lax.ppermute(step.gate(value), 'fsdp', pairs)  37.6 us
    pallas_call x4, Pallas kernels, use(): pl.pallas_call(functools.partial(use_kernel, spots, len(weights), first),...  14.5 us
    ppermute x25, waiting for transfers between devices, send(): return lax.ppermute(step.gate(value), 'fsdp', pairs)  12.4 us
    pallas_call x2, Pallas kernels, grad(): pl.pallas_call(functools.partial(grad_kernel, sizes, scale), out_shape=[j...  6.13 us
    ppermute x3, starting transfers between devices, butterfly(): return lax.ppermute(step.gate(value), 'replica', pairs)  5.58 us
    ppermute x3, waiting for transfers between devices, butterfly(): return lax.ppermute(step.gate(value), 'replica', pairs)  4.73 us
    pallas_call x1, Pallas kernels, merge(): pl.pallas_call(functools.partial(merge_kernel, groups), out_shape=[jax.Sh...  2.96 us
    unnamed x14, local copies, waits for them, and re-layouts  2.21 us
  transfers between devices with their start and end apart: 28, of which 11 were waited for; matrix products, arithmetic and copies ran while one was open for 4% of the time, Pallas kernels for 27%

profile of v3, /device:TPU:1, one launch (start us, length us, event | category | flops | bytes accessed | tf_op | source)
XLA Modules:
  0.0 93.9 jit_solution(7311608874707225387)
XLA Ops:
  0.7 3.3 %collective-permute-start.2 = (bf16[512,4096]{1,0:T(8,128)(2,1)}, bf16[512,4096]{1,0:T(8,128)(2,1)S(1)}, u32[]{:S(2)}, u32[]{:S(2)}) collective-permute-start(bf16[512,4096]{1,0:T(8,128)(2,1)} %bitcast.12), channel_id=1, source_target_pairs={{0,1},{1,0},{2,3},{3,2},{4,5},{5,4},{6,7},{7,6},{8,9},{9,8},{10,11... | collective-permute-start | bytes 12582920 | tf_op jit(solution)/shard_map/ppermute | solution.py:261
  4.1 1.1 %bitcast_subtract_fusion = f32[128,512]{1,0:T(8,128)S(1)} fusion(f32[128,512]{1,0:T(8,128)} %param.9, f32[1,128,512]{2,1,0:T(8,128)} %param.10), kind=kLoop, calls=%fused_computation.11 | loop fusion | flops 65536 | bytes 786432 | tf_op jit(solution)/shard_map/sub | solution.py:273
  5.3 0.8 collective-permute-start
  6.0 2.2 %copy-done.2 = bf16[1,512,4096]{2,1,0:T(8,128)(2,1)S(1)} copy-done((bf16[1,512,4096]{2,1,0:T(8,128)(2,1)S(1)}, bf16[1,512,4096]{2,1,0:T(8,128)(2,1)}, u32[]{:S(2)}) %copy-start.2) | copy-done | bytes 4194328
  8.2 1.6 %pack.1 = (bf16[512,1024]{1,0:T(8,128)(2,1)S(1)}, bf16[512,1024]{1,0:T(8,128)(2,1)S(1)}) custom-call(s32[3]{0:T(128)S(1)} %pad_add_fusion.place, bf16[512,4096]{1,0:T(8,128)(2,1)S(1)} %bitcast.13, bf16[512,4096]{1,0:T(8,128)(2,1)S(1)} %bitcast.14, bf16[512,4096]{1,0:T(8,128)(2,1)S(1)} %bitcast.15, bf16[512,4096]{1,0:T(8,128)(2,1)S(1)} %bitcast.16, ...), custom_call_target="tpu_custom_call" | custom-call | flops 1048576 | bytes 65536 | tf_op jit(solution)/shard_map/pack/pallas_call | solution.py:82
  9.9 2.9 %collective-permute-done.1 = f32[128,512]{1,0:T(8,128)S(1)} collective-permute-done((f32[128,512]{1,0:T(8,128)S(1)}, f32[128,512]{1,0:T(8,128)S(1)}, u32[]{:S(2)}, u32[]{:S(2)}) %collective-permute-start.1) | collective-permute-done | bytes 262176 | tf_op jit(solution)/shard_map/ppermute | solution.py:265
  12.7 0.3 collective-permute-done
  13.1 0.9 collective-permute-start.6
  14.0 4.0 %collective-permute-start.5 = (bf16[256,1024]{1,0:T(8,128)(2,1)S(1)}, bf16[256,1024]{1,0:T(8,128)(2,1)S(1)}, u32[]{:S(2)}, u32[]{:S(2)}) collective-permute-start(bf16[256,1024]{1,0:T(8,128)(2,1)S(1)} %pad_maximum_fusion.2.refs_0_), channel_id=1, source_target_pairs={{0,2},{1,15},{2,4},{3,1},{4,6},{5,3},{6,8},{7,5},{8,10},{9,7},{10,... | collective-permute-start | bytes 1572872 | tf_op jit(solution)/shard_map/ppermute | solution.py:261
  18.0 3.1 %grad.2 = (f32[384,1024]{1,0:T(8,128)S(1)}, f32[256,1024]{1,0:T(8,128)S(1)}, f32[256,1024]{1,0:T(8,128)S(1)}, f32[128,1024]{1,0:T(8,128)S(1)}) custom-call(s32[3]{0:T(128)S(1)} %pad_add_fusion.place, bf16[512,1024]{1,0:T(8,128)(2,1)S(1)} %get-tuple-element.143.refs_0_.far, ...), custom_call_target="tpu_custom_call" | custom-call | flops 1048576 | bytes 65536 | tf_op jit(solution)/shard_map/grad/pallas_call | solution.py:121
  21.4 1.3 %collective-permute-start.4 = (f16[384,1024]{1,0:T(8,128)(2,1)S(1)}, f16[384,1024]{1,0:T(8,128)(2,1)S(1)}, u32[]{:S(2)}, u32[]{:S(2)}) collective-permute-start(f16[384,1024]{1,0:T(8,128)(2,1)S(1)} %convert_element_type.78), channel_id=1, source_target_pairs={{0,16},{1,17},{2,18},{3,19},{4,20},{5,21},{6,22},{7,23},{8,24},{9,... | collective-permute-start | bytes 2359304 | tf_op jit(solution)/shard_map/ppermute | solution.py:261
  22.7 2.7 %collective-permute-start.7 = (f32[128,512]{1,0:T(8,128)S(1)}, f32[128,512]{1,0:T(8,128)S(1)}, u32[]{:S(2)}, u32[]{:S(2)}) collective-permute-start(f32[128,512]{1,0:T(8,128)S(1)} %add.71), channel_id=1, source_target_pairs={{0,128},{32,160},{64,192},{96,224},{128,0},{160,32},{192,64},{224,... | collective-permute-start | bytes 786440 | tf_op jit(solution)/shard_map/ppermute | solution.py:265
  25.5 0.3 collective-permute-start.10
  25.7 3.1 %grad.3 = (f32[384,1024]{1,0:T(8,128)S(1)}, f32[256,1024]{1,0:T(8,128)S(1)}, f32[256,1024]{1,0:T(8,128)S(1)}, f32[128,1024]{1,0:T(8,128)S(1)}) custom-call(s32[3]{0:T(128)S(1)} %pad_add_fusion.place, bf16[512,1024]{1,0:T(8,128)(2,1)S(1)} %get-tuple-element.151.refs_0_.near, ...), custom_call_target="tpu_custom_call" | custom-call | flops 1048576 | bytes 65536 | tf_op jit(solution)/shard_map/grad/pallas_call | solution.py:121
  28.8 1.3 %collective-permute-done.7 = f32[128,512]{1,0:T(8,128)S(1)} collective-permute-done((f32[128,512]{1,0:T(8,128)S(1)}, f32[128,512]{1,0:T(8,128)S(1)}, u32[]{:S(2)}, u32[]{:S(2)}) %collective-permute-start.7) | collective-permute-done | bytes 262176 | tf_op jit(solution)/shard_map/ppermute | solution.py:265
  30.1 2.7 %collective-permute-start.11 = (bf16[256,1024]{1,0:T(8,128)(2,1)S(1)}, bf16[256,1024]{1,0:T(8,128)(2,1)S(1)}, u32[]{:S(2)}, u32[]{:S(2)}) collective-permute-start(bf16[256,1024]{1,0:T(8,128)(2,1)S(1)} %collective-permute-done.5.refs_1_), channel_id=1, source_target_pairs={{0,2},{1,15},{2,4},{3,1},{4,6},{5,3},{6,8},{7,5},{8,10},{9,7},{10,... | collective-permute-start | bytes 1572872 | tf_op jit(solution)/shard_map/ppermute | solution.py:261
  32.8 5.3 %use.4 = (f32[512,1024]{1,0:T(8,128)S(1)}, f32[512,1024]{1,0:T(8,128)S(1)}, bf16[512,4096]{1,0:T(8,128)(2,1)}, bf16[512,768]{1,0:T(8,128)(2,1)S(1)}) custom-call(s32[3]{0:T(128)S(1)} %pad_add_fusion.place, bf16[512,1024]{1,0:T(8,128)(2,1)S(1)} %get-tuple-element.151.refs_0_.near, bf16[512,1024]{1,0:T(8,128)(2,1)S(1)} %get-tuple-element.143.refs_0_.far, ...), custom_call_target="tpu_custom_call" | custom-call | flops 3221225472 | bytes 1048576 | tf_op jit(solution)/shard_map/use/pallas_call | solution.py:184
  38.1 0.7 collective-permute-done.4
  38.8 0.2 add_convert_fusion.5
  39.1 1.5 %collective-permute-start.9 = (f16[128,1024]{1,0:T(8,128)(2,1)S(1)}, f16[128,1024]{1,0:T(8,128)(2,1)S(1)}, u32[]{:S(2)}, u32[]{:S(2)}) collective-permute-start(f16[128,1024]{1,0:T(8,128)(2,1)S(1)} %get-tuple-element.178), channel_id=1, source_target_pairs={{0,14},{1,3},{2,0},{3,5},{4,2},{5,7},{6,4},{7,9},{8,6},{9,11},{10,... | collective-permute-start | bytes 786440 | tf_op jit(solution)/shard_map/ppermute | solution.py:261
  40.6 0.5 collective-permute-done.11.refs_0_
  41.1 4.0 %collective-permute-start.17 = (bf16[256,1024]{1,0:T(8,128)(2,1)S(1)}, bf16[256,1024]{1,0:T(8,128)(2,1)S(1)}, u32[]{:S(2)}, u32[]{:S(2)}) collective-permute-start(bf16[256,1024]{1,0:T(8,128)(2,1)S(1)} %collective-permute-done.12.refs_1_), channel_id=1, source_target_pairs={{0,14},{1,3},{2,0},{3,5},{4,2},{5,7},{6,4},{7,9},{8,6},{9,11},{10,... | collective-permute-start | bytes 1572872 | tf_op jit(solution)/shard_map/ppermute | solution.py:261
  45.1 4.9 %collective-permute-done.10 = f16[256,1024]{1,0:T(8,128)(2,1)S(1)} collective-permute-done((f16[256,1024]{1,0:T(8,128)(2,1)S(1)}, f16[256,1024]{1,0:T(8,128)(2,1)S(1)}, u32[]{:S(2)}, u32[]{:S(2)}) %collective-permute-start.10) | collective-permute-done | bytes 524320 | tf_op jit(solution)/shard_map/ppermute | solution.py:261
  50.0 1.2 %collective-permute-start.15 = (f16[256,1024]{1,0:T(8,128)(2,1)S(1)}, f16[256,1024]{1,0:T(8,128)(2,1)S(1)}, u32[]{:S(2)}, u32[]{:S(2)}) collective-permute-start(f16[256,1024]{1,0:T(8,128)(2,1)S(1)} %convert_element_type.80), channel_id=1, source_target_pairs={{0,16},{1,17},{2,18},{3,19},{4,20},{5,21},{6,22},{7,23},{8,24},{9,... | collective-permute-start | bytes 1572872 | tf_op jit(solution)/shard_map/ppermute | solution.py:261
  51.2 1.1 %add_convert_fusion.3 = (f16[128,1024]{1,0:T(8,128)(2,1)}, f16[128,1024]{1,0:T(8,128)(2,1)}) fusion(f16[128,1024]{1,0:T(8,128)(2,1)S(1)} %collective-permute-done.9, f32[256,1024]{1,0:T(8,128)S(1)} %get-tuple-element.158, f16[256,1024]{1,0:T(8,128)(2,1)S(1)} %collective-permute-done.10, f16[128,1024]{1,0:T(8,128)(2,1)S(1)} %collective-permute-done.8), kind=kLoop, calls=%fused_computation.7 | loop fusion | flops 1310720 | bytes 2621440 | tf_op jit(solution)/shard_map/convert_element_type | solution.py:309
  52.3 1.5 %collective-permute-start.14 = (f16[128,1024]{1,0:T(8,128)(2,1)}, f16[128,1024]{1,0:T(8,128)(2,1)S(1)}, u32[]{:S(2)}, u32[]{:S(2)}) collective-permute-start(f16[128,1024]{1,0:T(8,128)(2,1)} %get-tuple-element.189), channel_id=1, source_target_pairs={{0,14},{1,3},{2,0},{3,5},{4,2},{5,7},{6,4},{7,9},{8,6},{9,11},{10,... | collective-permute-start | bytes 786440 | tf_op jit(solution)/shard_map/ppermute | solution.py:261
  53.8 3.5 %use.5 = (f32[512,1024]{1,0:T(8,128)S(1)}, f32[512,1024]{1,0:T(8,128)S(1)}, bf16[512,4096]{1,0:T(8,128)(2,1)}, bf16[512,512]{1,0:T(8,128)(2,1)S(1)}) custom-call(s32[3]{0:T(128)S(1)} %pad_add_fusion.place, bf16[512,1024]{1,0:T(8,128)(2,1)S(1)} %get-tuple-element.151.refs_0_.near, ...), custom_call_target="tpu_custom_call", output_to_operand_aliasing={{2}: (10, {}), {1}: (9, {}), {0}: (8, {})} | custom-call | flops 2147483648 | bytes 1048576 | tf_op jit(solution)/shard_map/use/pallas_call | solution.py:184
  57.4 0.5 collective-permute-done.17.refs_1_
  57.9 1.0 %collective-permute-done.16.refs_0_ = bf16[256,1024]{1,0:T(8,128)(2,1)S(1)} collective-permute-done((bf16[256,1024]{1,0:T(8,128)(2,1)S(1)}, bf16[256,1024]{1,0:T(8,128)(2,1)S(1)}, u32[]{:S(2)}, u32[]{:S(2)}) %collective-permute-start.16) | collective-permute-done | bytes 524320 | tf_op jit(solution)/shard_map/ppermute | solution.py:261
  59.0 2.4 %collective-permute-start.21 = (bf16[128,1024]{1,0:T(8,128)(2,1)S(1)}, bf16[128,1024]{1,0:T(8,128)(2,1)S(1)}, u32[]{:S(2)}, u32[]{:S(2)}) collective-permute-start(bf16[128,1024]{1,0:T(8,128)(2,1)S(1)} %slice.58), channel_id=1, source_target_pairs={{0,2},{1,15},{2,4},{3,1},{4,6},{5,3},{6,8},{7,5},{8,10},{9,7},{10,... | collective-permute-start | bytes 786440 | tf_op jit(solution)/shard_map/ppermute | solution.py:261
  61.4 1.1 %collective-permute-start.22 = (bf16[128,1024]{1,0:T(8,128)(2,1)S(1)}, bf16[128,1024]{1,0:T(8,128)(2,1)S(1)}, u32[]{:S(2)}, u32[]{:S(2)}) collective-permute-start(bf16[128,1024]{1,0:T(8,128)(2,1)S(1)} %slice.59), channel_id=1, source_target_pairs={{0,14},{1,3},{2,0},{3,5},{4,2},{5,7},{6,4},{7,9},{8,6},{9,11},{10,... | collective-permute-start | bytes 786440 | tf_op jit(solution)/shard_map/ppermute | solution.py:261
  62.5 2.1 %collective-permute-done.13 = f16[128,1024]{1,0:T(8,128)(2,1)S(1)} collective-permute-done((f16[128,1024]{1,0:T(8,128)(2,1)}, f16[128,1024]{1,0:T(8,128)(2,1)S(1)}, u32[]{:S(2)}, u32[]{:S(2)}) %collective-permute-start.13) | collective-permute-done | bytes 262176 | tf_op jit(solution)/shard_map/ppermute | solution.py:261
  64.5 0.3 add_convert_fusion
  64.8 1.7 %collective-permute-start.19 = (f16[128,1024]{1,0:T(8,128)(2,1)S(1)}, f16[128,1024]{1,0:T(8,128)(2,1)S(1)}, u32[]{:S(2)}, u32[]{:S(2)}) collective-permute-start(f16[128,1024]{1,0:T(8,128)(2,1)S(1)} %convert_element_type.81), channel_id=1, source_target_pairs={{0,16},{1,17},{2,18},{3,19},{4,20},{5,21},{6,22},{7,23},{8,24},{9,... | collective-permute-start | bytes 786440 | tf_op jit(solution)/shard_map/ppermute | solution.py:261
  66.5 2.8 %collective-permute-start.20 = (f32[128,512]{1,0:T(8,128)S(1)}, f32[128,512]{1,0:T(8,128)S(1)}, u32[]{:S(2)}, u32[]{:S(2)}) collective-permute-start(f32[128,512]{1,0:T(8,128)S(1)} %add.80), channel_id=1, source_target_pairs={{0,32},{32,0},{64,96},{96,64},{128,160},{160,128},{192,224},{224,1... | collective-permute-start | bytes 786440 | tf_op jit(solution)/shard_map/ppermute | solution.py:265
  69.3 0.2 collective-permute-start.18
  69.6 3.5 %use.6 = (f32[512,1024]{1,0:T(8,128)S(1)}, f32[512,1024]{1,0:T(8,128)S(1)}, bf16[512,4096]{1,0:T(8,128)(2,1)}, bf16[512,512]{1,0:T(8,128)(2,1)S(1)}) custom-call(s32[3]{0:T(128)S(1)} %pad_add_fusion.place, bf16[512,1024]{1,0:T(8,128)(2,1)S(1)} %get-tuple-element.151.refs_0_.near, ...), custom_call_target="tpu_custom_call", output_to_operand_aliasing={{2}: (10, {}), {1}: (9, {}), {0}: (8, {})} | custom-call | flops 1048576 | bytes 65536 | tf_op jit(solution)/shard_map/use/pallas_call | solution.py:184
  73.1 2.2 %use.7 = (f32[512,1024]{1,0:T(8,128)S(1)}, f32[512,1024]{1,0:T(8,128)S(1)}, bf16[512,4096]{1,0:T(8,128)(2,1)}, bf16[512,256]{1,0:T(8,128)(2,1)S(1)}) custom-call(s32[3]{0:T(128)S(1)} %pad_add_fusion.place, bf16[512,1024]{1,0:T(8,128)(2,1)S(1)} %get-tuple-element.151.refs_0_.near, ...), custom_call_target="tpu_custom_call", output_to_operand_aliasing={{2}: (10, {}), {1}: (9, {}), {0}: (8, {})} | custom-call | flops 1048576 | bytes 65536 | tf_op jit(solution)/shard_map/use/pallas_call | solution.py:184
  75.3 0.6 collective-permute-done.20
  75.9 7.3 %collective-permute-start.25 = (f32[512,1024]{1,0:T(8,128)S(1)}, f32[512,1024]{1,0:T(8,128)S(1)}, u32[]{:S(2)}, u32[]{:S(2)}) collective-permute-start(f32[512,1024]{1,0:T(8,128)S(1)} %get-tuple-element.246), channel_id=1, source_target_pairs={{0,1},{1,0},{2,3},{3,2},{4,5},{5,4},{6,7},{7,6},{8,9},{9,8},{10,11... | collective-permute-start | bytes 6291464 | tf_op jit(solution)/shard_map/ppermute | solution.py:261
  83.2 0.6 collective-permute-start.27
  83.8 0.1 add_convert_fusion.1
  84.0 1.4 %collective-permute-start.24 = (f16[128,1024]{1,0:T(8,128)(2,1)S(1)}, f16[128,1024]{1,0:T(8,128)(2,1)S(1)}, u32[]{:S(2)}, u32[]{:S(2)}) collective-permute-start(f16[128,1024]{1,0:T(8,128)(2,1)S(1)} %get-tuple-element.244), channel_id=1, source_target_pairs={{0,14},{1,3},{2,0},{3,5},{4,2},{5,7},{6,4},{7,9},{8,6},{9,11},{10,... | collective-permute-start | bytes 786440 | tf_op jit(solution)/shard_map/ppermute | solution.py:261
  85.4 1.4 %collective-permute-start.23 = (f16[128,1024]{1,0:T(8,128)(2,1)S(1)}, f16[128,1024]{1,0:T(8,128)(2,1)S(1)}, u32[]{:S(2)}, u32[]{:S(2)}) collective-permute-start(f16[128,1024]{1,0:T(8,128)(2,1)S(1)} %add_convert_fusion.1), channel_id=1, source_target_pairs={{0,2},{1,15},{2,4},{3,1},{4,6},{5,3},{6,8},{7,5},{8,10},{9,7},{10,... | collective-permute-start | bytes 786440 | tf_op jit(solution)/shard_map/ppermute | solution.py:261
  86.7 0.9 multiply_add_fusion
  87.6 2.3 %collective-permute-done.27.refs_1_ = bf16[512,768]{1,0:T(8,128)(2,1)S(1)} collective-permute-done((bf16[512,768]{1,0:T(8,128)(2,1)S(1)}, bf16[512,768]{1,0:T(8,128)(2,1)S(1)}, u32[]{:S(2)}, u32[]{:S(2)}) %collective-permute-start.27) | collective-permute-done | bytes 786464 | tf_op jit(solution)/shard_map/ppermute | solution.py:261
  90.0 3.0 %merge.1 = (bf16[512,1024]{1,0:T(8,128)(2,1)}, bf16[512,4096]{1,0:T(8,128)(2,1)}) custom-call(s32[3]{0:T(128)S(1)} %pad_add_fusion.place, bf16[512,1280]{1,0:T(8,128)(2,1)S(1)} %collective-permute-done.26.refs_0_, bf16[512,768]{1,0:T(8,128)(2,1)S(1)} %collective-permute-done.27.refs_1_, ...), custom_call_target="tpu_custom_call", output_to_operand_aliasing={{1}: (5, {})} | custom-call | flops 1048576 | bytes 65536 | tf_op jit(solution)/shard_map/merge/pallas_call | solution.py:227
  93.0 1.0 %multiply_bitcast_fusion = f32[1,128,1024]{2,1,0:T(8,128)} fusion(f16[128,1024]{1,0:T(8,128)(2,1)S(1)} %collective-permute-done.24, f16[128,1024]{1,0:T(8,128)(2,1)S(1)} %collective-permute-done.23, f32[384,1024]{1,0:T(8,128)S(1)} %get-tuple-element.159, f16[384,1024]{1,0:T(8,128)(2,1)S(1)} %collective-permute-done.4), kind=kLoop, calls=%fused_computation.3 | loop fusion | flops 917504 | bytes 1835008 | tf_op jit(solution)/shard_map/broadcast_in_dim | solution.py:346
  (49 shorter events, 1.0 us)
Async XLA Ops:
  0.7 12.3 %collective-permute-start.2 = (bf16[512,4096]{1,0:T(8,128)(2,1)}, bf16[512,4096]{1,0:T(8,128)(2,1)S(1)}, u32[]{:S(2)}, u32[]{:S(2)}) collective-permute-start(bf16[512,4096]{1,0:T(8,128)(2,1)} %bitcast.12), channel_id=1, source_target_pairs={{0,1},{1,0},{2,3},{3,2},{4,5},{5,4},{6,7},{7,6},{8,9},{9,8},{10,11... | collective-permute-start | bytes 12582920 | tf_op jit(solution)/shard_map/ppermute | solution.py:261
  4.0 9.0 %collective-permute-start.3 = (bf16[512,1024]{1,0:T(8,128)(2,1)}, bf16[512,1024]{1,0:T(8,128)(2,1)S(1)}, u32[]{:S(2)}, u32[]{:S(2)}) collective-permute-start(bf16[512,1024]{1,0:T(8,128)(2,1)} %bitcast.29), channel_id=1, source_target_pairs={{0,1},{1,0},{2,3},{3,2},{4,5},{5,4},{6,7},{7,6},{8,9},{9,8},{10,11... | collective-permute-start | bytes 3145736 | tf_op jit(solution)/shard_map/ppermute | solution.py:261
  5.2 7.6 %collective-permute-start.1 = (f32[128,512]{1,0:T(8,128)S(1)}, f32[128,512]{1,0:T(8,128)S(1)}, u32[]{:S(2)}, u32[]{:S(2)}) collective-permute-start(f32[128,512]{1,0:T(8,128)S(1)} %bitcast_subtract_fusion), channel_id=1, source_target_pairs={{0,64},{32,96},{64,0},{96,32},{128,192},{160,224},{192,128},{224,1... | collective-permute-start | bytes 786440 | tf_op jit(solution)/shard_map/ppermute | solution.py:265
  5.3 7.8 %collective-permute-start = (bf16[128,1024]{1,0:T(8,128)(2,1)}, bf16[128,1024]{1,0:T(8,128)(2,1)S(1)}, u32[]{:S(2)}, u32[]{:S(2)}) collective-permute-start(bf16[128,1024]{1,0:T(8,128)(2,1)} %bitcast.37), channel_id=1, source_target_pairs={{0,16},{1,17},{2,18},{3,19},{4,20},{5,21},{6,22},{7,23},{8,24},{9,... | collective-permute-start | bytes 786440 | tf_op jit(solution)/shard_map/ppermute | solution.py:261
  6.0 2.2 %copy-start.2 = (bf16[1,512,4096]{2,1,0:T(8,128)(2,1)S(1)}, bf16[1,512,4096]{2,1,0:T(8,128)(2,1)}, u32[]{:S(2)}) copy-start(bf16[1,512,4096]{2,1,0:T(8,128)(2,1)} %param.6) | copy-start | bytes 12582916
  8.2 4.8 %copy-start.5 = (bf16[1,128,1024]{2,1,0:T(8,128)(2,1)S(1)}, bf16[1,128,1024]{2,1,0:T(8,128)(2,1)}, u32[]{:S(2)}) copy-start(bf16[1,128,1024]{2,1,0:T(8,128)(2,1)} %param.7) | copy-start | bytes 786436
  8.2 9.8 %copy-start.3 = (bf16[1,512,1024]{2,1,0:T(8,128)(2,1)S(1)}, bf16[1,512,1024]{2,1,0:T(8,128)(2,1)}, u32[]{:S(2)}) copy-start(bf16[1,512,1024]{2,1,0:T(8,128)(2,1)} %param.8) | copy-start | bytes 3145732
  13.1 12.6 %copy-start = (bf16[512,4096]{1,0:T(8,128)(2,1)}, bf16[512,4096]{1,0:T(8,128)(2,1)S(1)}, u32[]{:S(2)}) copy-start(bf16[512,4096]{1,0:T(8,128)(2,1)S(1)} %collective-permute-done.2.refs_1_.refs_2_.refs_3_.refs_4_.refs_5_.refs_6_.refs_7_.refs_8_.other) | copy-start | bytes 12582916
  13.1 17.0 %collective-permute-start.6 = (bf16[256,1024]{1,0:T(8,128)(2,1)S(1)}, bf16[256,1024]{1,0:T(8,128)(2,1)S(1)}, u32[]{:S(2)}, u32[]{:S(2)}) collective-permute-start(bf16[256,1024]{1,0:T(8,128)(2,1)S(1)} %pad_maximum_fusion.2.refs_0_), channel_id=1, source_target_pairs={{0,14},{1,3},{2,0},{3,5},{4,2},{5,7},{6,4},{7,9},{8,6},{9,11},{10,... | collective-permute-start | bytes 1572872 | tf_op jit(solution)/shard_map/ppermute | solution.py:261
  14.0 16.1 %collective-permute-start.5 = (bf16[256,1024]{1,0:T(8,128)(2,1)S(1)}, bf16[256,1024]{1,0:T(8,128)(2,1)S(1)}, u32[]{:S(2)}, u32[]{:S(2)}) collective-permute-start(bf16[256,1024]{1,0:T(8,128)(2,1)S(1)} %pad_maximum_fusion.2.refs_0_), channel_id=1, source_target_pairs={{0,2},{1,15},{2,4},{3,1},{4,6},{5,3},{6,8},{7,5},{8,10},{9,7},{10,... | collective-permute-start | bytes 1572872 | tf_op jit(solution)/shard_map/ppermute | solution.py:261
  21.4 17.4 %collective-permute-start.4 = (f16[384,1024]{1,0:T(8,128)(2,1)S(1)}, f16[384,1024]{1,0:T(8,128)(2,1)S(1)}, u32[]{:S(2)}, u32[]{:S(2)}) collective-permute-start(f16[384,1024]{1,0:T(8,128)(2,1)S(1)} %convert_element_type.78), channel_id=1, source_target_pairs={{0,16},{1,17},{2,18},{3,19},{4,20},{5,21},{6,22},{7,23},{8,24},{9,... | collective-permute-start | bytes 2359304 | tf_op jit(solution)/shard_map/ppermute | solution.py:261
  22.7 7.3 %collective-permute-start.7 = (f32[128,512]{1,0:T(8,128)S(1)}, f32[128,512]{1,0:T(8,128)S(1)}, u32[]{:S(2)}, u32[]{:S(2)}) collective-permute-start(f32[128,512]{1,0:T(8,128)S(1)} %add.71), channel_id=1, source_target_pairs={{0,128},{32,160},{64,192},{96,224},{128,0},{160,32},{192,64},{224,... | collective-permute-start | bytes 786440 | tf_op jit(solution)/shard_map/ppermute | solution.py:265
  25.5 24.6 %collective-permute-start.10 = (f16[256,1024]{1,0:T(8,128)(2,1)S(1)}, f16[256,1024]{1,0:T(8,128)(2,1)S(1)}, u32[]{:S(2)}, u32[]{:S(2)}) collective-permute-start(f16[256,1024]{1,0:T(8,128)(2,1)S(1)} %convert_element_type.79), channel_id=1, source_target_pairs={{0,16},{1,17},{2,18},{3,19},{4,20},{5,21},{6,22},{7,23},{8,24},{9,... | collective-permute-start | bytes 1572872 | tf_op jit(solution)/shard_map/ppermute | solution.py:261
  30.1 10.5 %collective-permute-start.12 = (bf16[256,1024]{1,0:T(8,128)(2,1)S(1)}, bf16[256,1024]{1,0:T(8,128)(2,1)S(1)}, u32[]{:S(2)}, u32[]{:S(2)}) collective-permute-start(bf16[256,1024]{1,0:T(8,128)(2,1)S(1)} %collective-permute-done.6.refs_2_), channel_id=1, source_target_pairs={{0,14},{1,3},{2,0},{3,5},{4,2},{5,7},{6,4},{7,9},{8,6},{9,11},{10,... | collective-permute-start | bytes 1572872 | tf_op jit(solution)/shard_map/ppermute | solution.py:261
  30.1 11.0 %collective-permute-start.11 = (bf16[256,1024]{1,0:T(8,128)(2,1)S(1)}, bf16[256,1024]{1,0:T(8,128)(2,1)S(1)}, u32[]{:S(2)}, u32[]{:S(2)}) collective-permute-start(bf16[256,1024]{1,0:T(8,128)(2,1)S(1)} %collective-permute-done.5.refs_1_), channel_id=1, source_target_pairs={{0,2},{1,15},{2,4},{3,1},{4,6},{5,3},{6,8},{7,5},{8,10},{9,7},{10,... | collective-permute-start | bytes 1572872 | tf_op jit(solution)/shard_map/ppermute | solution.py:261
  38.8 15.0 %copy-start.1 = (bf16[512,4096]{1,0:T(8,128)(2,1)S(1)}, bf16[512,4096]{1,0:T(8,128)(2,1)}, u32[]{:S(2)}) copy-start(bf16[512,4096]{1,0:T(8,128)(2,1)} %copy-done) | copy-start | bytes 12582916
  39.0 11.0 %collective-permute-start.8 = (f16[128,1024]{1,0:T(8,128)(2,1)S(1)}, f16[128,1024]{1,0:T(8,128)(2,1)S(1)}, u32[]{:S(2)}, u32[]{:S(2)}) collective-permute-start(f16[128,1024]{1,0:T(8,128)(2,1)S(1)} %get-tuple-element.177), channel_id=1, source_target_pairs={{0,2},{1,15},{2,4},{3,1},{4,6},{5,3},{6,8},{7,5},{8,10},{9,7},{10,... | collective-permute-start | bytes 786440 | tf_op jit(solution)/shard_map/ppermute | solution.py:261
  39.1 10.9 %collective-permute-start.9 = (f16[128,1024]{1,0:T(8,128)(2,1)S(1)}, f16[128,1024]{1,0:T(8,128)(2,1)S(1)}, u32[]{:S(2)}, u32[]{:S(2)}) collective-permute-start(f16[128,1024]{1,0:T(8,128)(2,1)S(1)} %get-tuple-element.178), channel_id=1, source_target_pairs={{0,14},{1,3},{2,0},{3,5},{4,2},{5,7},{6,4},{7,9},{8,6},{9,11},{10,... | collective-permute-start | bytes 786440 | tf_op jit(solution)/shard_map/ppermute | solution.py:261
  41.1 16.8 %collective-permute-start.17 = (bf16[256,1024]{1,0:T(8,128)(2,1)S(1)}, bf16[256,1024]{1,0:T(8,128)(2,1)S(1)}, u32[]{:S(2)}, u32[]{:S(2)}) collective-permute-start(bf16[256,1024]{1,0:T(8,128)(2,1)S(1)} %collective-permute-done.12.refs_1_), channel_id=1, source_target_pairs={{0,14},{1,3},{2,0},{3,5},{4,2},{5,7},{6,4},{7,9},{8,6},{9,11},{10,... | collective-permute-start | bytes 1572872 | tf_op jit(solution)/shard_map/ppermute | solution.py:261
  45.1 13.8 %collective-permute-start.16 = (bf16[256,1024]{1,0:T(8,128)(2,1)S(1)}, bf16[256,1024]{1,0:T(8,128)(2,1)S(1)}, u32[]{:S(2)}, u32[]{:S(2)}) collective-permute-start(bf16[256,1024]{1,0:T(8,128)(2,1)S(1)} %collective-permute-done.11.refs_0_), channel_id=1, source_target_pairs={{0,2},{1,15},{2,4},{3,1},{4,6},{5,3},{6,8},{7,5},{8,10},{9,7},{10,... | collective-permute-start | bytes 1572872 | tf_op jit(solution)/shard_map/ppermute | solution.py:261
  50.0 14.5 %collective-permute-start.15 = (f16[256,1024]{1,0:T(8,128)(2,1)S(1)}, f16[256,1024]{1,0:T(8,128)(2,1)S(1)}, u32[]{:S(2)}, u32[]{:S(2)}) collective-permute-start(f16[256,1024]{1,0:T(8,128)(2,1)S(1)} %convert_element_type.80), channel_id=1, source_target_pairs={{0,16},{1,17},{2,18},{3,19},{4,20},{5,21},{6,22},{7,23},{8,24},{9,... | collective-permute-start | bytes 1572872 | tf_op jit(solution)/shard_map/ppermute | solution.py:261
  52.3 12.2 %collective-permute-start.13 = (f16[128,1024]{1,0:T(8,128)(2,1)}, f16[128,1024]{1,0:T(8,128)(2,1)S(1)}, u32[]{:S(2)}, u32[]{:S(2)}) collective-permute-start(f16[128,1024]{1,0:T(8,128)(2,1)} %get-tuple-element.187), channel_id=1, source_target_pairs={{0,2},{1,15},{2,4},{3,1},{4,6},{5,3},{6,8},{7,5},{8,10},{9,7},{10,... | collective-permute-start | bytes 786440 | tf_op jit(solution)/shard_map/ppermute | solution.py:261
  52.3 12.2 %collective-permute-start.14 = (f16[128,1024]{1,0:T(8,128)(2,1)}, f16[128,1024]{1,0:T(8,128)(2,1)S(1)}, u32[]{:S(2)}, u32[]{:S(2)}) collective-permute-start(f16[128,1024]{1,0:T(8,128)(2,1)} %get-tuple-element.189), channel_id=1, source_target_pairs={{0,14},{1,3},{2,0},{3,5},{4,2},{5,7},{6,4},{7,9},{8,6},{9,11},{10,... | collective-permute-start | bytes 786440 | tf_op jit(solution)/shard_map/ppermute | solution.py:261
  59.0 14.1 %collective-permute-start.21 = (bf16[128,1024]{1,0:T(8,128)(2,1)S(1)}, bf16[128,1024]{1,0:T(8,128)(2,1)S(1)}, u32[]{:S(2)}, u32[]{:S(2)}) collective-permute-start(bf16[128,1024]{1,0:T(8,128)(2,1)S(1)} %slice.58), channel_id=1, source_target_pairs={{0,2},{1,15},{2,4},{3,1},{4,6},{5,3},{6,8},{7,5},{8,10},{9,7},{10,... | collective-permute-start | bytes 786440 | tf_op jit(solution)/shard_map/ppermute | solution.py:261
  61.4 11.7 %collective-permute-start.22 = (bf16[128,1024]{1,0:T(8,128)(2,1)S(1)}, bf16[128,1024]{1,0:T(8,128)(2,1)S(1)}, u32[]{:S(2)}, u32[]{:S(2)}) collective-permute-start(bf16[128,1024]{1,0:T(8,128)(2,1)S(1)} %slice.59), channel_id=1, source_target_pairs={{0,14},{1,3},{2,0},{3,5},{4,2},{5,7},{6,4},{7,9},{8,6},{9,11},{10,... | collective-permute-start | bytes 786440 | tf_op jit(solution)/shard_map/ppermute | solution.py:261
  64.8 10.5 %collective-permute-start.19 = (f16[128,1024]{1,0:T(8,128)(2,1)S(1)}, f16[128,1024]{1,0:T(8,128)(2,1)S(1)}, u32[]{:S(2)}, u32[]{:S(2)}) collective-permute-start(f16[128,1024]{1,0:T(8,128)(2,1)S(1)} %convert_element_type.81), channel_id=1, source_target_pairs={{0,16},{1,17},{2,18},{3,19},{4,20},{5,21},{6,22},{7,23},{8,24},{9,... | collective-permute-start | bytes 786440 | tf_op jit(solution)/shard_map/ppermute | solution.py:261
  66.5 9.3 %collective-permute-start.20 = (f32[128,512]{1,0:T(8,128)S(1)}, f32[128,512]{1,0:T(8,128)S(1)}, u32[]{:S(2)}, u32[]{:S(2)}) collective-permute-start(f32[128,512]{1,0:T(8,128)S(1)} %add.80), channel_id=1, source_target_pairs={{0,32},{32,0},{64,96},{96,64},{128,160},{160,128},{192,224},{224,1... | collective-permute-start | bytes 786440 | tf_op jit(solution)/shard_map/ppermute | solution.py:265
  69.3 6.6 %collective-permute-start.18 = (f16[128,1024]{1,0:T(8,128)(2,1)S(1)}, f16[128,1024]{1,0:T(8,128)(2,1)S(1)}, u32[]{:S(2)}, u32[]{:S(2)}) collective-permute-start(f16[128,1024]{1,0:T(8,128)(2,1)S(1)} %get-tuple-element.211), channel_id=1, source_target_pairs={{0,2},{1,15},{2,4},{3,1},{4,6},{5,3},{6,8},{7,5},{8,10},{9,7},{10,... | collective-permute-start | bytes 786440 | tf_op jit(solution)/shard_map/ppermute | solution.py:261
  75.3 11.4 %copy-start.4 = (f32[128,512]{1,0:T(8,128)S(1)}, f32[128,512]{1,0:T(8,128)}, u32[]{:S(2)}) copy-start(f32[128,512]{1,0:T(8,128)} %param.9) | copy-start | bytes 786436
  75.3 11.4 %copy-start.6 = (f32[128,512]{1,0:T(8,128)S(1)}, f32[128,512]{1,0:T(8,128)}, u32[]{:S(2)}) copy-start(f32[128,512]{1,0:T(8,128)} %param.11) | copy-start | bytes 786436
  75.9 14.1 %collective-permute-start.25 = (f32[512,1024]{1,0:T(8,128)S(1)}, f32[512,1024]{1,0:T(8,128)S(1)}, u32[]{:S(2)}, u32[]{:S(2)}) collective-permute-start(f32[512,1024]{1,0:T(8,128)S(1)} %get-tuple-element.246), channel_id=1, source_target_pairs={{0,1},{1,0},{2,3},{3,2},{4,5},{5,4},{6,7},{7,6},{8,9},{9,8},{10,11... | collective-permute-start | bytes 6291464 | tf_op jit(solution)/shard_map/ppermute | solution.py:261
  83.2 6.8 %collective-permute-start.26 = (bf16[512,1280]{1,0:T(8,128)(2,1)S(1)}, bf16[512,1280]{1,0:T(8,128)(2,1)S(1)}, u32[]{:S(2)}, u32[]{:S(2)}) collective-permute-start(bf16[512,1280]{1,0:T(8,128)(2,1)S(1)} %pad_maximum_fusion), channel_id=1, source_target_pairs={{0,1},{1,0},{2,3},{3,2},{4,5},{5,4},{6,7},{7,6},{8,9},{9,8},{10,11... | collective-permute-start | bytes 3932168 | tf_op jit(solution)/shard_map/ppermute | solution.py:261
  83.2 6.7 %collective-permute-start.27 = (bf16[512,768]{1,0:T(8,128)(2,1)S(1)}, bf16[512,768]{1,0:T(8,128)(2,1)S(1)}, u32[]{:S(2)}, u32[]{:S(2)}) collective-permute-start(bf16[512,768]{1,0:T(8,128)(2,1)S(1)} %pad_maximum_fusion.1), channel_id=1, source_target_pairs={{0,1},{1,0},{2,3},{3,2},{4,5},{5,4},{6,7},{7,6},{8,9},{9,8},{10,11... | collective-permute-start | bytes 2359304 | tf_op jit(solution)/shard_map/ppermute | solution.py:261
  84.0 9.0 %collective-permute-start.24 = (f16[128,1024]{1,0:T(8,128)(2,1)S(1)}, f16[128,1024]{1,0:T(8,128)(2,1)S(1)}, u32[]{:S(2)}, u32[]{:S(2)}) collective-permute-start(f16[128,1024]{1,0:T(8,128)(2,1)S(1)} %get-tuple-element.244), channel_id=1, source_target_pairs={{0,14},{1,3},{2,0},{3,5},{4,2},{5,7},{6,4},{7,9},{8,6},{9,11},{10,... | collective-permute-start | bytes 786440 | tf_op jit(solution)/shard_map/ppermute | solution.py:261
  85.4 7.6 %collective-permute-start.23 = (f16[128,1024]{1,0:T(8,128)(2,1)S(1)}, f16[128,1024]{1,0:T(8,128)(2,1)S(1)}, u32[]{:S(2)}, u32[]{:S(2)}) collective-permute-start(f16[128,1024]{1,0:T(8,128)(2,1)S(1)} %add_convert_fusion.1), channel_id=1, source_target_pairs={{0,2},{1,15},{2,4},{3,1},{4,6},{5,3},{6,8},{7,5},{8,10},{9,7},{10,... | collective-permute-start | bytes 786440 | tf_op jit(solution)/shard_map/ppermute | solution.py:261

commit v4 on v3

--- a/solution.py
+++ b/solution.py
@@ -135,8 +135,10 @@
     )(place, hidden[0][dx], *([hidden[1]] * count), *cot)
 
 
-def use_kernel(spots, arrays, first, place, near, far, other, *refs):
+def use_kernel(spots, arrays, first, before, place, near, far, other, *refs):
     count = len(spots)
+    if before:
+        earlier, refs = refs[0], refs[1:]
     weights, refs = refs[:arrays], refs[arrays:]
     cot, refs = refs[:2], refs[2:]
     if not first:
@@ -153,7 +155,11 @@
     block[...] = lax.dot_general(cot[0][...], weight, dims, preferred_element_type=F32).astype(BF16)
     for copy in writes:
         copy.start()
-    out_other[...] = lax.dot_general(cot[1][...], weight, dims, preferred_element_type=F32).astype(BF16)
+    if before:
+        out_other[:, :before] = earlier[...]
+    out_other[:, before:] = lax.dot_general(
+        cot[1][...], weight, dims, preferred_element_type=F32
+    ).astype(BF16)
     sides = (near, far)
     own = [sides[dx][:, ORDER.index(dz) * 128 : ORDER.index(dz) * 128 + 128] for dx, dz, _ in spots]
     keys = jnp.dot(jnp.concatenate(own, axis=1), weight, preferred_element_type=F32)
@@ -166,7 +172,7 @@
         copy.wait()
 
 
-def use(place, hidden, cot, weights, spots, state, last=False):
+def use(place, hidden, cot, weights, spots, state, last=False, earlier=None):
     tokens, width = cot[0].shape
     count = len(spots)
     first = state is None
@@ -174,20 +180,23 @@
     cost = pl.CostEstimate(flops=flops, bytes_accessed=1 << 20, transcendentals=0)
     anywhere = pl.BlockSpec(memory_space=pl.ANY)
     vmem = pl.BlockSpec(memory_space=pltpu.VMEM)
-    in_specs = [pl.BlockSpec(memory_space=pltpu.SMEM), vmem, vmem, anywhere] + [vmem] * (len(weights) + 2)
-    operands = [place, *hidden[0], hidden[1], *weights, *cot]
+    extra = [] if earlier is None else [earlier]
+    before = sum(e.shape[1] for e in extra)
+    in_specs = [pl.BlockSpec(memory_space=pltpu.SMEM), vmem, vmem, anywhere]
+    in_specs += [vmem] * (len(extra) + len(weights) + 2)
+    operands = [place, *hidden[0], hidden[1], *extra, *weights, *cot]
     aliases = {}
     if not first:
         in_specs += [vmem, vmem, anywhere]
         operands += list(state)
         aliases = {len(operands) - 1: 2, len(operands) - 2: 1, len(operands) - 3: 0}
     return pl.pallas_call(
-        functools.partial(use_kernel, spots, len(weights), first),
+        functools.partial(use_kernel, spots, len(weights), first, before),
         out_shape=[
             jax.ShapeDtypeStruct((tokens, width), F32),
             jax.ShapeDtypeStruct((tokens, width), F32),
             jax.ShapeDtypeStruct(hidden[1].shape, BF16),
-            jax.ShapeDtypeStruct((tokens, count * 128), BF16),
+            jax.ShapeDtypeStruct((tokens, before + count * 128), BF16),
         ],
         in_specs=in_specs,
         out_specs=[vmem, vmem, anywhere, vmem],
@@ -327,13 +336,15 @@
     up4, down4 = step.wait(up4, down4)
     spots = [(0, 4, 0), (1, 4, 0)]
     groups.append(spots)
-    keys, other_keys, back, back4 = step.wait(*use(step.place, hidden2, cot2, [up4, down4], spots, state, True))
+    keys, other_keys, back, back3 = step.wait(
+        *use(step.place, hidden2, cot2, [up4, down4], spots, state, True, back3)
+    )
 
     above, got, summed = step.wait(above, got, summed)
     above = (chip_sum(3, got, 0) + above.astype(F32)).astype(F16)
     above, below = send(above, Z_UP), send(below, Z_DOWN)
     other_keys, back1 = send(other_keys, CORE_SWAP), send(back1, CORE_SWAP)
-    back3 = send(jnp.concatenate([back3, back4], axis=1), CORE_SWAP)
+    back3 = send(back3, CORE_SWAP)
     new_global, new_momentum = outer_update(outer_global, outer_momentum, (total + summed) / replica_count)
     other_keys, back1, back3, new_global, new_momentum = step.wait(
         other_keys, back1, back3, new_global, new_momentum

time: 94.1 us -> 94.1 us (level)
  no operation moved by 1% of the time
where the time goes in v4:
time: 94.1 us; the launch traced here: 94 us
  starting transfers between devices  43.4 us (46%)
  Pallas kernels  25.3 us (27%)
  waiting for transfers between devices  17.1 us (18%)
  other arithmetic  5.04 us (5%)
  local copies, waits for them, and re-layouts  2.25 us (2%)
  between operations  0.95 us (1%)
    ppermute x25, starting transfers between devices, send(): return lax.ppermute(step.gate(value), 'fsdp', pairs)  37.8 us
    pallas_call x4, Pallas kernels, use(): pl.pallas_call(functools.partial(use_kernel, spots, len(weights), first,...  14.5 us
    ppermute x25, waiting for transfers between devices, send(): return lax.ppermute(step.gate(value), 'fsdp', pairs)  12.4 us
    pallas_call x2, Pallas kernels, grad(): pl.pallas_call(functools.partial(grad_kernel, sizes, scale), out_shape=[j...  6.13 us
    ppermute x3, starting transfers between devices, butterfly(): return lax.ppermute(step.gate(value), 'replica', pairs)  5.58 us
    ppermute x3, waiting for transfers between devices, butterfly(): return lax.ppermute(step.gate(value), 'replica', pairs)  4.67 us
    pallas_call x1, Pallas kernels, merge(): pl.pallas_call(functools.partial(merge_kernel, groups), out_shape=[jax.Sh...  2.96 us
    unnamed x14, local copies, waits for them, and re-layouts  2.21 us
  transfers between devices with their start and end apart: 28, of which 11 were waited for; matrix products, arithmetic and copies ran while one was open for 4% of the time, Pallas kernels for 27%

profile of v4, /device:TPU:1, one launch (start us, length us, event | category | flops | bytes accessed | tf_op | source)
XLA Modules:
  0.0 94.0 jit_solution(10693623790529177609)
XLA Ops:
  0.7 3.3 %collective-permute-start.2 = (bf16[512,4096]{1,0:T(8,128)(2,1)}, bf16[512,4096]{1,0:T(8,128)(2,1)S(1)}, u32[]{:S(2)}, u32[]{:S(2)}) collective-permute-start(bf16[512,4096]{1,0:T(8,128)(2,1)} %bitcast.12), channel_id=1, source_target_pairs={{0,1},{1,0},{2,3},{3,2},{4,5},{5,4},{6,7},{7,6},{8,9},{9,8},{10,11... | collective-permute-start | bytes 12582920 | tf_op jit(solution)/shard_map/ppermute | solution.py:270
  4.1 1.1 %bitcast_subtract_fusion = f32[128,512]{1,0:T(8,128)S(1)} fusion(f32[128,512]{1,0:T(8,128)} %param.9, f32[1,128,512]{2,1,0:T(8,128)} %param.10), kind=kLoop, calls=%fused_computation.10 | loop fusion | flops 65536 | bytes 786432 | tf_op jit(solution)/shard_map/sub | solution.py:282
  5.3 0.8 collective-permute-start
  6.0 2.2 %copy-done.2 = bf16[1,512,4096]{2,1,0:T(8,128)(2,1)S(1)} copy-done((bf16[1,512,4096]{2,1,0:T(8,128)(2,1)S(1)}, bf16[1,512,4096]{2,1,0:T(8,128)(2,1)}, u32[]{:S(2)}) %copy-start.2) | copy-done | bytes 4194328
  8.2 1.6 %pack.1 = (bf16[512,1024]{1,0:T(8,128)(2,1)S(1)}, bf16[512,1024]{1,0:T(8,128)(2,1)S(1)}) custom-call(s32[3]{0:T(128)S(1)} %pad_add_fusion.place, bf16[512,4096]{1,0:T(8,128)(2,1)S(1)} %bitcast.13, bf16[512,4096]{1,0:T(8,128)(2,1)S(1)} %bitcast.14, bf16[512,4096]{1,0:T(8,128)(2,1)S(1)} %bitcast.15, bf16[512,4096]{1,0:T(8,128)(2,1)S(1)} %bitcast.16, ...), custom_call_target="tpu_custom_call" | custom-call | flops 1048576 | bytes 65536 | tf_op jit(solution)/shard_map/pack/pallas_call | solution.py:82
  9.9 2.9 %collective-permute-done.1 = f32[128,512]{1,0:T(8,128)S(1)} collective-permute-done((f32[128,512]{1,0:T(8,128)S(1)}, f32[128,512]{1,0:T(8,128)S(1)}, u32[]{:S(2)}, u32[]{:S(2)}) %collective-permute-start.1) | collective-permute-done | bytes 262176 | tf_op jit(solution)/shard_map/ppermute | solution.py:274
  12.7 0.3 collective-permute-done
  13.1 0.9 collective-permute-start.6
  14.0 4.0 %collective-permute-start.5 = (bf16[256,1024]{1,0:T(8,128)(2,1)S(1)}, bf16[256,1024]{1,0:T(8,128)(2,1)S(1)}, u32[]{:S(2)}, u32[]{:S(2)}) collective-permute-start(bf16[256,1024]{1,0:T(8,128)(2,1)S(1)} %pad_maximum_fusion.1.refs_0_), channel_id=1, source_target_pairs={{0,2},{1,15},{2,4},{3,1},{4,6},{5,3},{6,8},{7,5},{8,10},{9,7},{10,... | collective-permute-start | bytes 1572872 | tf_op jit(solution)/shard_map/ppermute | solution.py:270
  18.0 3.1 %grad.2 = (f32[384,1024]{1,0:T(8,128)S(1)}, f32[256,1024]{1,0:T(8,128)S(1)}, f32[256,1024]{1,0:T(8,128)S(1)}, f32[128,1024]{1,0:T(8,128)S(1)}) custom-call(s32[3]{0:T(128)S(1)} %pad_add_fusion.place, bf16[512,1024]{1,0:T(8,128)(2,1)S(1)} %get-tuple-element.143.refs_0_.far, ...), custom_call_target="tpu_custom_call" | custom-call | flops 1048576 | bytes 65536 | tf_op jit(solution)/shard_map/grad/pallas_call | solution.py:121
  21.1 0.1 convert_element_type.78
  21.4 1.3 %collective-permute-start.4 = (f16[384,1024]{1,0:T(8,128)(2,1)S(1)}, f16[384,1024]{1,0:T(8,128)(2,1)S(1)}, u32[]{:S(2)}, u32[]{:S(2)}) collective-permute-start(f16[384,1024]{1,0:T(8,128)(2,1)S(1)} %convert_element_type.78), channel_id=1, source_target_pairs={{0,16},{1,17},{2,18},{3,19},{4,20},{5,21},{6,22},{7,23},{8,24},{9,... | collective-permute-start | bytes 2359304 | tf_op jit(solution)/shard_map/ppermute | solution.py:270
  22.7 2.7 %collective-permute-start.7 = (f32[128,512]{1,0:T(8,128)S(1)}, f32[128,512]{1,0:T(8,128)S(1)}, u32[]{:S(2)}, u32[]{:S(2)}) collective-permute-start(f32[128,512]{1,0:T(8,128)S(1)} %add.71), channel_id=1, source_target_pairs={{0,128},{32,160},{64,192},{96,224},{128,0},{160,32},{192,64},{224,... | collective-permute-start | bytes 786440 | tf_op jit(solution)/shard_map/ppermute | solution.py:274
  25.5 0.3 collective-permute-start.10
  25.7 3.1 %grad.3 = (f32[384,1024]{1,0:T(8,128)S(1)}, f32[256,1024]{1,0:T(8,128)S(1)}, f32[256,1024]{1,0:T(8,128)S(1)}, f32[128,1024]{1,0:T(8,128)S(1)}) custom-call(s32[3]{0:T(128)S(1)} %pad_add_fusion.place, bf16[512,1024]{1,0:T(8,128)(2,1)S(1)} %get-tuple-element.151.refs_0_.near, ...), custom_call_target="tpu_custom_call" | custom-call | flops 1048576 | bytes 65536 | tf_op jit(solution)/shard_map/grad/pallas_call | solution.py:121
  28.8 1.3 %collective-permute-done.7 = f32[128,512]{1,0:T(8,128)S(1)} collective-permute-done((f32[128,512]{1,0:T(8,128)S(1)}, f32[128,512]{1,0:T(8,128)S(1)}, u32[]{:S(2)}, u32[]{:S(2)}) %collective-permute-start.7) | collective-permute-done | bytes 262176 | tf_op jit(solution)/shard_map/ppermute | solution.py:274
  30.1 2.7 %collective-permute-start.11 = (bf16[256,1024]{1,0:T(8,128)(2,1)S(1)}, bf16[256,1024]{1,0:T(8,128)(2,1)S(1)}, u32[]{:S(2)}, u32[]{:S(2)}) collective-permute-start(bf16[256,1024]{1,0:T(8,128)(2,1)S(1)} %collective-permute-done.5.refs_1_), channel_id=1, source_target_pairs={{0,2},{1,15},{2,4},{3,1},{4,6},{5,3},{6,8},{7,5},{8,10},{9,7},{10,... | collective-permute-start | bytes 1572872 | tf_op jit(solution)/shard_map/ppermute | solution.py:270
  32.8 5.3 %use.4 = (f32[512,1024]{1,0:T(8,128)S(1)}, f32[512,1024]{1,0:T(8,128)S(1)}, bf16[512,4096]{1,0:T(8,128)(2,1)}, bf16[512,768]{1,0:T(8,128)(2,1)S(1)}) custom-call(s32[3]{0:T(128)S(1)} %pad_add_fusion.place, bf16[512,1024]{1,0:T(8,128)(2,1)S(1)} %get-tuple-element.151.refs_0_.near, bf16[512,1024]{1,0:T(8,128)(2,1)S(1)} %get-tuple-element.143.refs_0_.far, ...), custom_call_target="tpu_custom_call" | custom-call | flops 3221225472 | bytes 1048576 | tf_op jit(solution)/shard_map/use/pallas_call | solution.py:193
  38.1 0.7 collective-permute-done.4
  38.8 0.2 add_convert_fusion.5
  39.0 1.5 %collective-permute-start.9 = (f16[128,1024]{1,0:T(8,128)(2,1)S(1)}, f16[128,1024]{1,0:T(8,128)(2,1)S(1)}, u32[]{:S(2)}, u32[]{:S(2)}) collective-permute-start(f16[128,1024]{1,0:T(8,128)(2,1)S(1)} %get-tuple-element.178), channel_id=1, source_target_pairs={{0,14},{1,3},{2,0},{3,5},{4,2},{5,7},{6,4},{7,9},{8,6},{9,11},{10,... | collective-permute-start | bytes 786440 | tf_op jit(solution)/shard_map/ppermute | solution.py:270
  40.5 0.6 collective-permute-done.11.refs_0_
  41.1 4.0 %collective-permute-start.17 = (bf16[256,1024]{1,0:T(8,128)(2,1)S(1)}, bf16[256,1024]{1,0:T(8,128)(2,1)S(1)}, u32[]{:S(2)}, u32[]{:S(2)}) collective-permute-start(bf16[256,1024]{1,0:T(8,128)(2,1)S(1)} %collective-permute-done.12.refs_1_), channel_id=1, source_target_pairs={{0,14},{1,3},{2,0},{3,5},{4,2},{5,7},{6,4},{7,9},{8,6},{9,11},{10,... | collective-permute-start | bytes 1572872 | tf_op jit(solution)/shard_map/ppermute | solution.py:270
  45.1 4.9 %collective-permute-done.10 = f16[256,1024]{1,0:T(8,128)(2,1)S(1)} collective-permute-done((f16[256,1024]{1,0:T(8,128)(2,1)S(1)}, f16[256,1024]{1,0:T(8,128)(2,1)S(1)}, u32[]{:S(2)}, u32[]{:S(2)}) %collective-permute-start.10) | collective-permute-done | bytes 524320 | tf_op jit(solution)/shard_map/ppermute | solution.py:270
  50.0 1.2 %collective-permute-start.15 = (f16[256,1024]{1,0:T(8,128)(2,1)S(1)}, f16[256,1024]{1,0:T(8,128)(2,1)S(1)}, u32[]{:S(2)}, u32[]{:S(2)}) collective-permute-start(f16[256,1024]{1,0:T(8,128)(2,1)S(1)} %convert_element_type.80), channel_id=1, source_target_pairs={{0,16},{1,17},{2,18},{3,19},{4,20},{5,21},{6,22},{7,23},{8,24},{9,... | collective-permute-start | bytes 1572872 | tf_op jit(solution)/shard_map/ppermute | solution.py:270
  51.2 1.0 %add_convert_fusion.3 = (f16[128,1024]{1,0:T(8,128)(2,1)S(1)}, f16[128,1024]{1,0:T(8,128)(2,1)}) fusion(f16[128,1024]{1,0:T(8,128)(2,1)S(1)} %collective-permute-done.9, f32[256,1024]{1,0:T(8,128)S(1)} %get-tuple-element.158, f16[256,1024]{1,0:T(8,128)(2,1)S(1)} %collective-permute-done.10, f16[128,1024]{1,0:T(8,128)(2,1)S(1)} %collective-permute-done.8), kind=kLoop, calls=%fused_computation.6 | loop fusion | flops 1310720 | bytes 2621440 | tf_op jit(solution)/shard_map/convert_element_type | solution.py:318
  52.2 1.5 %collective-permute-start.14 = (f16[128,1024]{1,0:T(8,128)(2,1)S(1)}, f16[128,1024]{1,0:T(8,128)(2,1)S(1)}, u32[]{:S(2)}, u32[]{:S(2)}) collective-permute-start(f16[128,1024]{1,0:T(8,128)(2,1)S(1)} %get-tuple-element.189), channel_id=1, source_target_pairs={{0,14},{1,3},{2,0},{3,5},{4,2},{5,7},{6,4},{7,9},{8,6},{9,11},{10,... | collective-permute-start | bytes 786440 | tf_op jit(solution)/shard_map/ppermute | solution.py:270
  53.7 3.5 %use.5 = (f32[512,1024]{1,0:T(8,128)S(1)}, f32[512,1024]{1,0:T(8,128)S(1)}, bf16[512,4096]{1,0:T(8,128)(2,1)}, bf16[512,512]{1,0:T(8,128)(2,1)S(1)}) custom-call(s32[3]{0:T(128)S(1)} %pad_add_fusion.place, bf16[512,1024]{1,0:T(8,128)(2,1)S(1)} %get-tuple-element.151.refs_0_.near, ...), custom_call_target="tpu_custom_call", output_to_operand_aliasing={{2}: (10, {}), {1}: (9, {}), {0}: (8, {})} | custom-call | flops 2147483648 | bytes 1048576 | tf_op jit(solution)/shard_map/use/pallas_call | solution.py:193
  57.3 0.7 collective-permute-done.17.refs_1_
  57.9 0.9 collective-permute-done.16.refs_0_
  58.9 2.5 %collective-permute-start.21 = (bf16[128,1024]{1,0:T(8,128)(2,1)S(1)}, bf16[128,1024]{1,0:T(8,128)(2,1)S(1)}, u32[]{:S(2)}, u32[]{:S(2)}) collective-permute-start(bf16[128,1024]{1,0:T(8,128)(2,1)S(1)} %slice.58), channel_id=1, source_target_pairs={{0,2},{1,15},{2,4},{3,1},{4,6},{5,3},{6,8},{7,5},{8,10},{9,7},{10,... | collective-permute-start | bytes 786440 | tf_op jit(solution)/shard_map/ppermute | solution.py:270
  61.4 1.2 %collective-permute-start.22 = (bf16[128,1024]{1,0:T(8,128)(2,1)S(1)}, bf16[128,1024]{1,0:T(8,128)(2,1)S(1)}, u32[]{:S(2)}, u32[]{:S(2)}) collective-permute-start(bf16[128,1024]{1,0:T(8,128)(2,1)S(1)} %slice.59), channel_id=1, source_target_pairs={{0,14},{1,3},{2,0},{3,5},{4,2},{5,7},{6,4},{7,9},{8,6},{9,11},{10,... | collective-permute-start | bytes 786440 | tf_op jit(solution)/shard_map/ppermute | solution.py:270
  62.6 1.8 %collective-permute-done.13 = f16[128,1024]{1,0:T(8,128)(2,1)S(1)} collective-permute-done((f16[128,1024]{1,0:T(8,128)(2,1)}, f16[128,1024]{1,0:T(8,128)(2,1)S(1)}, u32[]{:S(2)}, u32[]{:S(2)}) %collective-permute-start.13) | collective-permute-done | bytes 262176 | tf_op jit(solution)/shard_map/ppermute | solution.py:270
  64.5 0.3 add_convert_fusion
  64.8 1.8 %collective-permute-start.19 = (f16[128,1024]{1,0:T(8,128)(2,1)S(1)}, f16[128,1024]{1,0:T(8,128)(2,1)S(1)}, u32[]{:S(2)}, u32[]{:S(2)}) collective-permute-start(f16[128,1024]{1,0:T(8,128)(2,1)S(1)} %convert_element_type.81), channel_id=1, source_target_pairs={{0,16},{1,17},{2,18},{3,19},{4,20},{5,21},{6,22},{7,23},{8,24},{9,... | collective-permute-start | bytes 786440 | tf_op jit(solution)/shard_map/ppermute | solution.py:270
  66.6 2.8 %collective-permute-start.20 = (f32[128,512]{1,0:T(8,128)S(1)}, f32[128,512]{1,0:T(8,128)S(1)}, u32[]{:S(2)}, u32[]{:S(2)}) collective-permute-start(f32[128,512]{1,0:T(8,128)S(1)} %add.80), channel_id=1, source_target_pairs={{0,32},{32,0},{64,96},{96,64},{128,160},{160,128},{192,224},{224,1... | collective-permute-start | bytes 786440 | tf_op jit(solution)/shard_map/ppermute | solution.py:274
  69.3 0.3 collective-permute-start.18
  69.6 3.5 %use.6 = (f32[512,1024]{1,0:T(8,128)S(1)}, f32[512,1024]{1,0:T(8,128)S(1)}, bf16[512,4096]{1,0:T(8,128)(2,1)}, bf16[512,512]{1,0:T(8,128)(2,1)S(1)}) custom-call(s32[3]{0:T(128)S(1)} %pad_add_fusion.place, bf16[512,1024]{1,0:T(8,128)(2,1)S(1)} %get-tuple-element.151.refs_0_.near, ...), custom_call_target="tpu_custom_call", output_to_operand_aliasing={{2}: (10, {}), {1}: (9, {}), {0}: (8, {})} | custom-call | flops 1048576 | bytes 65536 | tf_op jit(solution)/shard_map/use/pallas_call | solution.py:193
  73.2 2.2 %use.7 = (f32[512,1024]{1,0:T(8,128)S(1)}, f32[512,1024]{1,0:T(8,128)S(1)}, bf16[512,4096]{1,0:T(8,128)(2,1)}, bf16[512,768]{1,0:T(8,128)(2,1)S(1)}) custom-call(s32[3]{0:T(128)S(1)} %pad_add_fusion.place, bf16[512,1024]{1,0:T(8,128)(2,1)S(1)} %get-tuple-element.151.refs_0_.near, ...), custom_call_target="tpu_custom_call", output_to_operand_aliasing={{2}: (11, {}), {1}: (10, {}), {0}: (9, {})} | custom-call | flops 1048576 | bytes 65536 | tf_op jit(solution)/shard_map/use/pallas_call | solution.py:193
  75.4 0.5 collective-permute-done.20
  75.9 7.3 %collective-permute-start.25 = (f32[512,1024]{1,0:T(8,128)S(1)}, f32[512,1024]{1,0:T(8,128)S(1)}, u32[]{:S(2)}, u32[]{:S(2)}) collective-permute-start(f32[512,1024]{1,0:T(8,128)S(1)} %get-tuple-element.247), channel_id=1, source_target_pairs={{0,1},{1,0},{2,3},{3,2},{4,5},{5,4},{6,7},{7,6},{8,9},{9,8},{10,11... | collective-permute-start | bytes 6291464 | tf_op jit(solution)/shard_map/ppermute | solution.py:270
  83.2 0.5 collective-permute-start.27
  83.8 1.4 %collective-permute-start.24 = (f16[128,1024]{1,0:T(8,128)(2,1)S(1)}, f16[128,1024]{1,0:T(8,128)(2,1)S(1)}, u32[]{:S(2)}, u32[]{:S(2)}) collective-permute-start(f16[128,1024]{1,0:T(8,128)(2,1)S(1)} %get-tuple-element.245), channel_id=1, source_target_pairs={{0,14},{1,3},{2,0},{3,5},{4,2},{5,7},{6,4},{7,9},{8,6},{9,11},{10,... | collective-permute-start | bytes 786440 | tf_op jit(solution)/shard_map/ppermute | solution.py:270
  85.3 1.3 %collective-permute-start.23 = (f16[128,1024]{1,0:T(8,128)(2,1)S(1)}, f16[128,1024]{1,0:T(8,128)(2,1)S(1)}, u32[]{:S(2)}, u32[]{:S(2)}) collective-permute-start(f16[128,1024]{1,0:T(8,128)(2,1)S(1)} %add_convert_fusion.1), channel_id=1, source_target_pairs={{0,2},{1,15},{2,4},{3,1},{4,6},{5,3},{6,8},{7,5},{8,10},{9,7},{10,... | collective-permute-start | bytes 786440 | tf_op jit(solution)/shard_map/ppermute | solution.py:270
  86.6 0.9 multiply_add_fusion
  87.5 2.5 %collective-permute-done.27.refs_1_ = bf16[512,768]{1,0:T(8,128)(2,1)S(1)} collective-permute-done((bf16[512,768]{1,0:T(8,128)(2,1)S(1)}, bf16[512,768]{1,0:T(8,128)(2,1)S(1)}, u32[]{:S(2)}, u32[]{:S(2)}) %collective-permute-start.27) | collective-permute-done | bytes 786464 | tf_op jit(solution)/shard_map/ppermute | solution.py:270
  90.0 3.0 %merge.1 = (bf16[512,1024]{1,0:T(8,128)(2,1)}, bf16[512,4096]{1,0:T(8,128)(2,1)}) custom-call(s32[3]{0:T(128)S(1)} %pad_add_fusion.place, bf16[512,1280]{1,0:T(8,128)(2,1)S(1)} %collective-permute-done.26.refs_0_, bf16[512,768]{1,0:T(8,128)(2,1)S(1)} %collective-permute-done.27.refs_1_, ...), custom_call_target="tpu_custom_call", output_to_operand_aliasing={{1}: (5, {})} | custom-call | flops 1048576 | bytes 65536 | tf_op jit(solution)/shard_map/merge/pallas_call | solution.py:236
  93.0 1.0 %multiply_bitcast_fusion = f32[1,128,1024]{2,1,0:T(8,128)} fusion(f16[128,1024]{1,0:T(8,128)(2,1)S(1)} %collective-permute-done.24, f16[128,1024]{1,0:T(8,128)(2,1)S(1)} %collective-permute-done.23, f32[384,1024]{1,0:T(8,128)S(1)} %get-tuple-element.159, f16[384,1024]{1,0:T(8,128)(2,1)S(1)} %collective-permute-done.4), kind=kLoop, calls=%fused_computation.2 | loop fusion | flops 917504 | bytes 1835008 | tf_op jit(solution)/shard_map/broadcast_in_dim | solution.py:357
  (48 shorter events, 1.0 us)
Async XLA Ops:
  0.7 12.3 %collective-permute-start.2 = (bf16[512,4096]{1,0:T(8,128)(2,1)}, bf16[512,4096]{1,0:T(8,128)(2,1)S(1)}, u32[]{:S(2)}, u32[]{:S(2)}) collective-permute-start(bf16[512,4096]{1,0:T(8,128)(2,1)} %bitcast.12), channel_id=1, source_target_pairs={{0,1},{1,0},{2,3},{3,2},{4,5},{5,4},{6,7},{7,6},{8,9},{9,8},{10,11... | collective-permute-start | bytes 12582920 | tf_op jit(solution)/shard_map/ppermute | solution.py:270
  4.0 9.0 %collective-permute-start.3 = (bf16[512,1024]{1,0:T(8,128)(2,1)}, bf16[512,1024]{1,0:T(8,128)(2,1)S(1)}, u32[]{:S(2)}, u32[]{:S(2)}) collective-permute-start(bf16[512,1024]{1,0:T(8,128)(2,1)} %bitcast.29), channel_id=1, source_target_pairs={{0,1},{1,0},{2,3},{3,2},{4,5},{5,4},{6,7},{7,6},{8,9},{9,8},{10,11... | collective-permute-start | bytes 3145736 | tf_op jit(solution)/shard_map/ppermute | solution.py:270
  5.2 7.6 %collective-permute-start.1 = (f32[128,512]{1,0:T(8,128)S(1)}, f32[128,512]{1,0:T(8,128)S(1)}, u32[]{:S(2)}, u32[]{:S(2)}) collective-permute-start(f32[128,512]{1,0:T(8,128)S(1)} %bitcast_subtract_fusion), channel_id=1, source_target_pairs={{0,64},{32,96},{64,0},{96,32},{128,192},{160,224},{192,128},{224,1... | collective-permute-start | bytes 786440 | tf_op jit(solution)/shard_map/ppermute | solution.py:274
  5.3 7.8 %collective-permute-start = (bf16[128,1024]{1,0:T(8,128)(2,1)}, bf16[128,1024]{1,0:T(8,128)(2,1)S(1)}, u32[]{:S(2)}, u32[]{:S(2)}) collective-permute-start(bf16[128,1024]{1,0:T(8,128)(2,1)} %bitcast.37), channel_id=1, source_target_pairs={{0,16},{1,17},{2,18},{3,19},{4,20},{5,21},{6,22},{7,23},{8,24},{9,... | collective-permute-start | bytes 786440 | tf_op jit(solution)/shard_map/ppermute | solution.py:270
  6.0 2.2 %copy-start.2 = (bf16[1,512,4096]{2,1,0:T(8,128)(2,1)S(1)}, bf16[1,512,4096]{2,1,0:T(8,128)(2,1)}, u32[]{:S(2)}) copy-start(bf16[1,512,4096]{2,1,0:T(8,128)(2,1)} %param.6) | copy-start | bytes 12582916
  8.2 4.8 %copy-start.5 = (bf16[1,128,1024]{2,1,0:T(8,128)(2,1)S(1)}, bf16[1,128,1024]{2,1,0:T(8,128)(2,1)}, u32[]{:S(2)}) copy-start(bf16[1,128,1024]{2,1,0:T(8,128)(2,1)} %param.7) | copy-start | bytes 786436
  8.2 9.8 %copy-start.3 = (bf16[1,512,1024]{2,1,0:T(8,128)(2,1)S(1)}, bf16[1,512,1024]{2,1,0:T(8,128)(2,1)}, u32[]{:S(2)}) copy-start(bf16[1,512,1024]{2,1,0:T(8,128)(2,1)} %param.8) | copy-start | bytes 3145732
  13.1 12.6 %copy-start = (bf16[512,4096]{1,0:T(8,128)(2,1)}, bf16[512,4096]{1,0:T(8,128)(2,1)S(1)}, u32[]{:S(2)}) copy-start(bf16[512,4096]{1,0:T(8,128)(2,1)S(1)} %collective-permute-done.2.refs_1_.refs_2_.refs_3_.refs_4_.refs_5_.refs_6_.refs_7_.refs_8_.other) | copy-start | bytes 12582916
  13.1 17.0 %collective-permute-start.6 = (bf16[256,1024]{1,0:T(8,128)(2,1)S(1)}, bf16[256,1024]{1,0:T(8,128)(2,1)S(1)}, u32[]{:S(2)}, u32[]{:S(2)}) collective-permute-start(bf16[256,1024]{1,0:T(8,128)(2,1)S(1)} %pad_maximum_fusion.1.refs_0_), channel_id=1, source_target_pairs={{0,14},{1,3},{2,0},{3,5},{4,2},{5,7},{6,4},{7,9},{8,6},{9,11},{10,... | collective-permute-start | bytes 1572872 | tf_op jit(solution)/shard_map/ppermute | solution.py:270
  14.0 16.1 %collective-permute-start.5 = (bf16[256,1024]{1,0:T(8,128)(2,1)S(1)}, bf16[256,1024]{1,0:T(8,128)(2,1)S(1)}, u32[]{:S(2)}, u32[]{:S(2)}) collective-permute-start(bf16[256,1024]{1,0:T(8,128)(2,1)S(1)} %pad_maximum_fusion.1.refs_0_), channel_id=1, source_target_pairs={{0,2},{1,15},{2,4},{3,1},{4,6},{5,3},{6,8},{7,5},{8,10},{9,7},{10,... | collective-permute-start | bytes 1572872 | tf_op jit(solution)/shard_map/ppermute | solution.py:270
  21.4 17.4 %collective-permute-start.4 = (f16[384,1024]{1,0:T(8,128)(2,1)S(1)}, f16[384,1024]{1,0:T(8,128)(2,1)S(1)}, u32[]{:S(2)}, u32[]{:S(2)}) collective-permute-start(f16[384,1024]{1,0:T(8,128)(2,1)S(1)} %convert_element_type.78), channel_id=1, source_target_pairs={{0,16},{1,17},{2,18},{3,19},{4,20},{5,21},{6,22},{7,23},{8,24},{9,... | collective-permute-start | bytes 2359304 | tf_op jit(solution)/shard_map/ppermute | solution.py:270
  22.7 7.4 %collective-permute-start.7 = (f32[128,512]{1,0:T(8,128)S(1)}, f32[128,512]{1,0:T(8,128)S(1)}, u32[]{:S(2)}, u32[]{:S(2)}) collective-permute-start(f32[128,512]{1,0:T(8,128)S(1)} %add.71), channel_id=1, source_target_pairs={{0,128},{32,160},{64,192},{96,224},{128,0},{160,32},{192,64},{224,... | collective-permute-start | bytes 786440 | tf_op jit(solution)/shard_map/ppermute | solution.py:274
  25.5 24.6 %collective-permute-start.10 = (f16[256,1024]{1,0:T(8,128)(2,1)S(1)}, f16[256,1024]{1,0:T(8,128)(2,1)S(1)}, u32[]{:S(2)}, u32[]{:S(2)}) collective-permute-start(f16[256,1024]{1,0:T(8,128)(2,1)S(1)} %convert_element_type.79), channel_id=1, source_target_pairs={{0,16},{1,17},{2,18},{3,19},{4,20},{5,21},{6,22},{7,23},{8,24},{9,... | collective-permute-start | bytes 1572872 | tf_op jit(solution)/shard_map/ppermute | solution.py:270
  30.1 10.4 %collective-permute-start.12 = (bf16[256,1024]{1,0:T(8,128)(2,1)S(1)}, bf16[256,1024]{1,0:T(8,128)(2,1)S(1)}, u32[]{:S(2)}, u32[]{:S(2)}) collective-permute-start(bf16[256,1024]{1,0:T(8,128)(2,1)S(1)} %collective-permute-done.6.refs_2_), channel_id=1, source_target_pairs={{0,14},{1,3},{2,0},{3,5},{4,2},{5,7},{6,4},{7,9},{8,6},{9,11},{10,... | collective-permute-start | bytes 1572872 | tf_op jit(solution)/shard_map/ppermute | solution.py:270
  30.1 11.0 %collective-permute-start.11 = (bf16[256,1024]{1,0:T(8,128)(2,1)S(1)}, bf16[256,1024]{1,0:T(8,128)(2,1)S(1)}, u32[]{:S(2)}, u32[]{:S(2)}) collective-permute-start(bf16[256,1024]{1,0:T(8,128)(2,1)S(1)} %collective-permute-done.5.refs_1_), channel_id=1, source_target_pairs={{0,2},{1,15},{2,4},{3,1},{4,6},{5,3},{6,8},{7,5},{8,10},{9,7},{10,... | collective-permute-start | bytes 1572872 | tf_op jit(solution)/shard_map/ppermute | solution.py:270
  38.8 14.9 %copy-start.1 = (bf16[512,4096]{1,0:T(8,128)(2,1)S(1)}, bf16[512,4096]{1,0:T(8,128)(2,1)}, u32[]{:S(2)}) copy-start(bf16[512,4096]{1,0:T(8,128)(2,1)} %copy-done) | copy-start | bytes 12582916
  38.9 11.1 %collective-permute-start.8 = (f16[128,1024]{1,0:T(8,128)(2,1)S(1)}, f16[128,1024]{1,0:T(8,128)(2,1)S(1)}, u32[]{:S(2)}, u32[]{:S(2)}) collective-permute-start(f16[128,1024]{1,0:T(8,128)(2,1)S(1)} %get-tuple-element.177), channel_id=1, source_target_pairs={{0,2},{1,15},{2,4},{3,1},{4,6},{5,3},{6,8},{7,5},{8,10},{9,7},{10,... | collective-permute-start | bytes 786440 | tf_op jit(solution)/shard_map/ppermute | solution.py:270
  39.0 11.0 %collective-permute-start.9 = (f16[128,1024]{1,0:T(8,128)(2,1)S(1)}, f16[128,1024]{1,0:T(8,128)(2,1)S(1)}, u32[]{:S(2)}, u32[]{:S(2)}) collective-permute-start(f16[128,1024]{1,0:T(8,128)(2,1)S(1)} %get-tuple-element.178), channel_id=1, source_target_pairs={{0,14},{1,3},{2,0},{3,5},{4,2},{5,7},{6,4},{7,9},{8,6},{9,11},{10,... | collective-permute-start | bytes 786440 | tf_op jit(solution)/shard_map/ppermute | solution.py:270
  41.1 16.8 %collective-permute-start.17 = (bf16[256,1024]{1,0:T(8,128)(2,1)S(1)}, bf16[256,1024]{1,0:T(8,128)(2,1)S(1)}, u32[]{:S(2)}, u32[]{:S(2)}) collective-permute-start(bf16[256,1024]{1,0:T(8,128)(2,1)S(1)} %collective-permute-done.12.refs_1_), channel_id=1, source_target_pairs={{0,14},{1,3},{2,0},{3,5},{4,2},{5,7},{6,4},{7,9},{8,6},{9,11},{10,... | collective-permute-start | bytes 1572872 | tf_op jit(solution)/shard_map/ppermute | solution.py:270
  45.1 13.7 %collective-permute-start.16 = (bf16[256,1024]{1,0:T(8,128)(2,1)S(1)}, bf16[256,1024]{1,0:T(8,128)(2,1)S(1)}, u32[]{:S(2)}, u32[]{:S(2)}) collective-permute-start(bf16[256,1024]{1,0:T(8,128)(2,1)S(1)} %collective-permute-done.11.refs_0_), channel_id=1, source_target_pairs={{0,2},{1,15},{2,4},{3,1},{4,6},{5,3},{6,8},{7,5},{8,10},{9,7},{10,... | collective-permute-start | bytes 1572872 | tf_op jit(solution)/shard_map/ppermute | solution.py:270
  50.0 14.4 %collective-permute-start.15 = (f16[256,1024]{1,0:T(8,128)(2,1)S(1)}, f16[256,1024]{1,0:T(8,128)(2,1)S(1)}, u32[]{:S(2)}, u32[]{:S(2)}) collective-permute-start(f16[256,1024]{1,0:T(8,128)(2,1)S(1)} %convert_element_type.80), channel_id=1, source_target_pairs={{0,16},{1,17},{2,18},{3,19},{4,20},{5,21},{6,22},{7,23},{8,24},{9,... | collective-permute-start | bytes 1572872 | tf_op jit(solution)/shard_map/ppermute | solution.py:270
  52.2 12.2 %collective-permute-start.13 = (f16[128,1024]{1,0:T(8,128)(2,1)}, f16[128,1024]{1,0:T(8,128)(2,1)S(1)}, u32[]{:S(2)}, u32[]{:S(2)}) collective-permute-start(f16[128,1024]{1,0:T(8,128)(2,1)} %get-tuple-element.187), channel_id=1, source_target_pairs={{0,2},{1,15},{2,4},{3,1},{4,6},{5,3},{6,8},{7,5},{8,10},{9,7},{10,... | collective-permute-start | bytes 786440 | tf_op jit(solution)/shard_map/ppermute | solution.py:270
  52.2 12.2 %collective-permute-start.14 = (f16[128,1024]{1,0:T(8,128)(2,1)S(1)}, f16[128,1024]{1,0:T(8,128)(2,1)S(1)}, u32[]{:S(2)}, u32[]{:S(2)}) collective-permute-start(f16[128,1024]{1,0:T(8,128)(2,1)S(1)} %get-tuple-element.189), channel_id=1, source_target_pairs={{0,14},{1,3},{2,0},{3,5},{4,2},{5,7},{6,4},{7,9},{8,6},{9,11},{10,... | collective-permute-start | bytes 786440 | tf_op jit(solution)/shard_map/ppermute | solution.py:270
  58.9 14.3 %collective-permute-start.21 = (bf16[128,1024]{1,0:T(8,128)(2,1)S(1)}, bf16[128,1024]{1,0:T(8,128)(2,1)S(1)}, u32[]{:S(2)}, u32[]{:S(2)}) collective-permute-start(bf16[128,1024]{1,0:T(8,128)(2,1)S(1)} %slice.58), channel_id=1, source_target_pairs={{0,2},{1,15},{2,4},{3,1},{4,6},{5,3},{6,8},{7,5},{8,10},{9,7},{10,... | collective-permute-start | bytes 786440 | tf_op jit(solution)/shard_map/ppermute | solution.py:270
  61.4 11.8 %collective-permute-start.22 = (bf16[128,1024]{1,0:T(8,128)(2,1)S(1)}, bf16[128,1024]{1,0:T(8,128)(2,1)S(1)}, u32[]{:S(2)}, u32[]{:S(2)}) collective-permute-start(bf16[128,1024]{1,0:T(8,128)(2,1)S(1)} %slice.59), channel_id=1, source_target_pairs={{0,14},{1,3},{2,0},{3,5},{4,2},{5,7},{6,4},{7,9},{8,6},{9,11},{10,... | collective-permute-start | bytes 786440 | tf_op jit(solution)/shard_map/ppermute | solution.py:270
  64.8 10.6 %collective-permute-start.19 = (f16[128,1024]{1,0:T(8,128)(2,1)S(1)}, f16[128,1024]{1,0:T(8,128)(2,1)S(1)}, u32[]{:S(2)}, u32[]{:S(2)}) collective-permute-start(f16[128,1024]{1,0:T(8,128)(2,1)S(1)} %convert_element_type.81), channel_id=1, source_target_pairs={{0,16},{1,17},{2,18},{3,19},{4,20},{5,21},{6,22},{7,23},{8,24},{9,... | collective-permute-start | bytes 786440 | tf_op jit(solution)/shard_map/ppermute | solution.py:270
  66.6 9.3 %collective-permute-start.20 = (f32[128,512]{1,0:T(8,128)S(1)}, f32[128,512]{1,0:T(8,128)S(1)}, u32[]{:S(2)}, u32[]{:S(2)}) collective-permute-start(f32[128,512]{1,0:T(8,128)S(1)} %add.80), channel_id=1, source_target_pairs={{0,32},{32,0},{64,96},{96,64},{128,160},{160,128},{192,224},{224,1... | collective-permute-start | bytes 786440 | tf_op jit(solution)/shard_map/ppermute | solution.py:274
  69.3 6.6 %collective-permute-start.18 = (f16[128,1024]{1,0:T(8,128)(2,1)S(1)}, f16[128,1024]{1,0:T(8,128)(2,1)S(1)}, u32[]{:S(2)}, u32[]{:S(2)}) collective-permute-start(f16[128,1024]{1,0:T(8,128)(2,1)S(1)} %get-tuple-element.211), channel_id=1, source_target_pairs={{0,2},{1,15},{2,4},{3,1},{4,6},{5,3},{6,8},{7,5},{8,10},{9,7},{10,... | collective-permute-start | bytes 786440 | tf_op jit(solution)/shard_map/ppermute | solution.py:270
  73.1 13.5 %copy-start.4 = (f32[128,512]{1,0:T(8,128)S(1)}, f32[128,512]{1,0:T(8,128)}, u32[]{:S(2)}) copy-start(f32[128,512]{1,0:T(8,128)} %param.9) | copy-start | bytes 786436
  73.2 13.4 %copy-start.6 = (f32[128,512]{1,0:T(8,128)S(1)}, f32[128,512]{1,0:T(8,128)}, u32[]{:S(2)}) copy-start(f32[128,512]{1,0:T(8,128)} %param.11) | copy-start | bytes 786436
  75.9 14.1 %collective-permute-start.25 = (f32[512,1024]{1,0:T(8,128)S(1)}, f32[512,1024]{1,0:T(8,128)S(1)}, u32[]{:S(2)}, u32[]{:S(2)}) collective-permute-start(f32[512,1024]{1,0:T(8,128)S(1)} %get-tuple-element.247), channel_id=1, source_target_pairs={{0,1},{1,0},{2,3},{3,2},{4,5},{5,4},{6,7},{7,6},{8,9},{9,8},{10,11... | collective-permute-start | bytes 6291464 | tf_op jit(solution)/shard_map/ppermute | solution.py:270
  83.2 6.8 %collective-permute-start.26 = (bf16[512,1280]{1,0:T(8,128)(2,1)S(1)}, bf16[512,1280]{1,0:T(8,128)(2,1)S(1)}, u32[]{:S(2)}, u32[]{:S(2)}) collective-permute-start(bf16[512,1280]{1,0:T(8,128)(2,1)S(1)} %pad_maximum_fusion), channel_id=1, source_target_pairs={{0,1},{1,0},{2,3},{3,2},{4,5},{5,4},{6,7},{7,6},{8,9},{9,8},{10,11... | collective-permute-start | bytes 3932168 | tf_op jit(solution)/shard_map/ppermute | solution.py:270
  83.2 6.8 %collective-permute-start.27 = (bf16[512,768]{1,0:T(8,128)(2,1)S(1)}, bf16[512,768]{1,0:T(8,128)(2,1)S(1)}, u32[]{:S(2)}, u32[]{:S(2)}) collective-permute-start(bf16[512,768]{1,0:T(8,128)(2,1)S(1)} %get-tuple-element.251), channel_id=1, source_target_pairs={{0,1},{1,0},{2,3},{3,2},{4,5},{5,4},{6,7},{7,6},{8,9},{9,8},{10,11... | collective-permute-start | bytes 2359304 | tf_op jit(solution)/shard_map/ppermute | solution.py:270
  83.8 9.1 %collective-permute-start.24 = (f16[128,1024]{1,0:T(8,128)(2,1)S(1)}, f16[128,1024]{1,0:T(8,128)(2,1)S(1)}, u32[]{:S(2)}, u32[]{:S(2)}) collective-permute-start(f16[128,1024]{1,0:T(8,128)(2,1)S(1)} %get-tuple-element.245), channel_id=1, source_target_pairs={{0,14},{1,3},{2,0},{3,5},{4,2},{5,7},{6,4},{7,9},{8,6},{9,11},{10,... | collective-permute-start | bytes 786440 | tf_op jit(solution)/shard_map/ppermute | solution.py:270
  85.3 7.7 %collective-permute-start.23 = (f16[128,1024]{1,0:T(8,128)(2,1)S(1)}, f16[128,1024]{1,0:T(8,128)(2,1)S(1)}, u32[]{:S(2)}, u32[]{:S(2)}) collective-permute-start(f16[128,1024]{1,0:T(8,128)(2,1)S(1)} %add_convert_fusion.1), channel_id=1, source_target_pairs={{0,2},{1,15},{2,4},{3,1},{4,6},{5,3},{6,8},{7,5},{8,10},{9,7},{10,... | collective-permute-start | bytes 786440 | tf_op jit(solution)/shard_map/ppermute | solution.py:270
